TPU v7x, 256 devices: a whole 4x4x8 slice. The times are simulated.
256 devices in a mesh: dp: 32 (over x, z_hi, core), tensor: 8 (over y, z_lo).
Axes of the slice: x: 4, y: 4, z: 8 (z_hi: 4, z_lo: 2; z = z_hi * 2 + z_lo), core: 2. Of those that a mesh axis runs over, the one named last changes fastest.
Arguments:
- hidden: bfloat16 [16384, 8192], P(('dp', 'tensor')), may hold values from -6 to 6
- norm_gain: float32 [8192], replicated, may hold values from 0.1 to 1.9
- w_query: bfloat16 [8192, 8192], P('dp', 'tensor'), may hold values from -0.0625 to 0.0625
- w_key: bfloat16 [8192, 1024], P('dp', 'tensor'), may hold values from -0.0625 to 0.0625
- w_value: bfloat16 [8192, 1024], P('dp', 'tensor'), may hold values from -0.0625 to 0.0625
- d_query: bfloat16 [16384, 8192], P('dp', 'tensor'), may hold values from -12 to 12
- d_key: bfloat16 [16384, 1024], P('dp', 'tensor'), may hold values from -12 to 12
- d_value: bfloat16 [16384, 1024], P('dp', 'tensor'), may hold values from -12 to 12
- lengths: int32 [64], P('dp'), may hold values from 64 to 256, as said below
- proj_in: bfloat16 [8192, 64], replicated, may hold values from -0.0625 to 0.0625
- proj_query: bfloat16 [8192, 64], P('tensor'), may hold values from -0.0625 to 0.0625
- proj_key: bfloat16 [1024, 64], P('tensor'), may hold values from -0.1875 to 0.1875
- proj_value: bfloat16 [1024, 64], P('tensor'), may hold values from -0.1875 to 0.1875
- queries: bfloat16 [32768, 12288], P(('dp', 'tensor')), may hold values from -0.0034179688 to 0.0034179688
Outputs:
- scores: float32 [64, 32768], P(None, ('dp', 'tensor'))
- grad_hidden: bfloat16 [16384, 8192], P(('dp', 'tensor'))
Inputs may be any that keep to these rules, and one draw needn't show every extreme that they name: lengths[e] counts the live leading tokens of sequence e among its 256 positions; the rest is padding.
All inputs are finite; a program needn't handle non-finite values.
Results may differ from a plain program's by a relative error of at most 0.02.
Values may be sent and summed in bfloat16 or wider, within the bound.
No kernel may reach another device: no remote copies, remote signals or barrier semaphores. Data moves between devices by JAX's collectives and lax.ppermute only.
A program may use at most 128 MiB of HBM per device.

v0:
```python
import jax
import jax.numpy as jnp
from jax import lax
from jax.sharding import PartitionSpec as P

EPSILON = 1e-05


def local(
    hidden,
    norm_gain,
    w_query,
    w_key,
    w_value,
    d_query,
    d_key,
    d_value,
    lengths,
    proj_in,
    proj_query,
    proj_key,
    proj_value,
    queries,
):
    tok_rows = d_query.shape[0]
    seqs_here = lengths.shape[0]
    rank = proj_in.shape[1]
    contract = (((1,), (1,)), ((), ()))
    w_local = jnp.concatenate([w_query, w_key, w_value], axis=1)
    cot_local = jnp.concatenate([d_query, d_key, d_value], axis=1)
    partial_sum = lax.dot_general(
        cot_local,
        lax.all_gather(w_local, "dp", axis=0, tiled=True),
        contract,
        preferred_element_type=jnp.float32,
    )
    input_grad = lax.psum_scatter(
        partial_sum.astype(jnp.bfloat16), "tensor", scatter_dimension=0, tiled=True
    ).astype(jnp.float32)
    rows32 = hidden.astype(jnp.float32)
    inv_rms = lax.rsqrt(jnp.mean(rows32 * rows32, axis=1, keepdims=True) + EPSILON)
    unit = rows32 * inv_rms
    normed = (unit * norm_gain).astype(jnp.bfloat16)
    gained = input_grad * norm_gain
    grad_hidden = (
        inv_rms * (gained - unit * jnp.mean(gained * unit, axis=1, keepdims=True))
    ).astype(jnp.bfloat16)
    local_sketch = jnp.dot(normed, proj_in, preferred_element_type=jnp.float32).astype(jnp.bfloat16)
    token_sketch = lax.all_gather(local_sketch.reshape(-1), "tensor", axis=0, tiled=True).reshape(
        tok_rows, rank
    )
    head_terms = jnp.stack(
        [
            jnp.dot(d_query, proj_query, preferred_element_type=jnp.float32),
            jnp.dot(d_key, proj_key, preferred_element_type=jnp.float32),
            jnp.dot(d_value, proj_value, preferred_element_type=jnp.float32),
        ],
        axis=1,
    )
    head_sketch = lax.psum(head_terms.reshape(-1).astype(jnp.bfloat16), "tensor").astype(
        jnp.float32
    )
    seq_length = tok_rows // seqs_here
    head_sketch = head_sketch.reshape(seqs_here, seq_length, 3, rank)
    live = (lax.broadcasted_iota(jnp.int32, (seqs_here, seq_length), 1) < lengths[:, None]).astype(
        jnp.float32
    )
    masked = head_sketch * live[:, :, None, None]
    inputs32 = token_sketch.astype(jnp.float32).reshape(seqs_here, seq_length, rank)
    example_grad = jnp.einsum("sli,slmj->smij", inputs32, masked, precision=lax.Precision.HIGHEST)
    example_grad = example_grad.reshape(seqs_here, 3 * rank * rank).astype(jnp.bfloat16)
    every_grad = lax.all_gather(example_grad, "dp", axis=0, tiled=True)
    scores = lax.dot_general(every_grad, queries, contract, preferred_element_type=jnp.float32)
    return (scores, grad_hidden)


def solution(mesh):
    placed = (
        P(("dp", "tensor"), None),
        P(),
        P("dp", "tensor"),
        P("dp", "tensor"),
        P("dp", "tensor"),
        P("dp", "tensor"),
        P("dp", "tensor"),
        P("dp", "tensor"),
        P("dp"),
        P(),
        P("tensor", None),
        P("tensor", None),
        P("tensor", None),
        P(("dp", "tensor"), None),
    )
    return jax.shard_map(
        local,
        mesh=mesh,
        in_specs=placed,
        out_specs=(P(None, ("dp", "tensor")), P(("dp", "tensor"), None)),
        check_vma=False,
    )
```

profile of v0, /device:TPU:14, one launch (start us, length us, event | category | flops | bytes accessed | tf_op | source)
XLA Modules:
  0.0 383.6 jit_solution(1181721048877394232)
XLA Ops:
  8.0 0.0 copy-start
  8.0 0.0 copy-start.6
  8.0 0.0 copy-start.5
  8.0 0.0 all-reduce.2.cloned.1.call-start
  8.1 1.2 fusion.15
  9.3 1.1 fusion.16
  10.4 1.7 fusion.17
  12.1 0.0 copy-start.3
  12.1 0.7 copy.28
  12.8 0.0 all-reduce.2.cloned.1.call-update
  12.8 0.0 all-gather.4.cloned.1.call-start
  12.9 0.0 copy-done.6
  12.9 0.0 copy-done.5
  12.9 1.9 pad_maximum_fusion
  14.8 0.0 all-gather.4.cloned.1.call-update
  14.8 0.0 copy-start.7
  14.9 0.0 all-gather.6.cloned.1.call-start
  14.9 1.5 fusion.8
  16.4 0.0 copy-start.4
  16.5 0.0 copy-done.3
  16.5 2.1 convolution_convert_fusion.5
  18.6 0.1 reshape.57
  18.6 27.4 %all_gather.9 = bf16[32768]{0:T(1024)(128)(2,1)S(1)} all-gather(bf16[4096]{0:T(1024)(128)(2,1)S(1)} %reshape.57), channel_id=1, replica_groups=mesh['dp'=32,'tensor'=8] {'tensor'}, dimensions={0}, use_global_device_ids=true | all-gather | bytes 73728 | tf_op jit(solution)/shard_map/all_gather | solution.py:49
  46.1 0.1 reshape.58
  46.2 0.0 copy-done.7
  46.2 0.1 compare_convert_fusion
  46.3 123.2 %all-reduce.2.cloned.1.call-done = bf16[2,256,3,64]{1,3,2,0:T(8,128)(2,1)} async-done(((bf16[2,256,3,64]{1,3,2,0:T(8,128)(2,1)}), bf16[2,256,3,64]{1,3,2,0:T(8,128)(2,1)}) %all-reduce.2.cloned.1.call-update) | async-done | bytes 196624 | tf_op jit(solution)/shard_map/psum | solution.py:60
  169.4 1.3 fusion.14
  170.7 0.1 copy.22
  170.8 0.8 reshape.60
  171.6 0.0 all-gather.6.cloned.1.call-update
  171.6 0.0 reduce-scatter.2.cloned.1.call-start
  171.7 0.0 all-gather.4.cloned.1.call-done
  171.7 0.0 copy-done.4
  171.7 17.6 %convolution_convert_fusion = bf16[512,8192]{1,0:T(8,128)(2,1)} fusion(bf16[8192,1280]{1,0:T(8,128)(2,1)} %all-gather.4.cloned.1.call-done, bf16[512,128]{1,0:T(8,128)(2,1)S(1)} %copy-done.4, bf16[512,128]{1,0:T(8,128)(2,1)} %param.20, bf16[512,1024]{1,0:T(8,128)(2,1)} %param.19), kind=kOutput, calls=%fused_computation | convolution fusion | flops 10745544704 | bytes 30670848 | tf_op jit(solution)/shard_map/dot_general | solution.py:31
  189.3 0.0 reduce-scatter.2.cloned.1.call-update
  189.3 96.2 %all-gather.6.cloned.1.call-done = bf16[32,2,12288]{2,1,0:T(2,128)(2,1)} async-done(((bf16[1,2,12288]{2,1,0:T(2,128)(2,1)}), bf16[32,2,12288]{2,1,0:T(2,128)(2,1)}) %all-gather.6.cloned.1.call-update) | async-done | bytes 1572880 | tf_op jit(solution)/shard_map/all_gather | solution.py:72
  285.5 4.5 %reshape.61 = bf16[64,12288]{1,0:T(8,128)(2,1)} reshape(bf16[32,2,12288]{2,1,0:T(2,128)(2,1)} %all-gather.6.cloned.1.call-done) | data formatting | bytes 3145728
  290.0 0.0 copy-done
  290.1 3.2 fusion.26
  293.3 79.1 %reduce-scatter.2.cloned.1.call-done = bf16[64,8192]{1,0:T(8,128)(2,1)} async-done(((bf16[512,8192]{1,0:T(8,128)(2,1)}), bf16[64,8192]{1,0:T(8,128)(2,1)}) %reduce-scatter.2.cloned.1.call-update) | async-done | bytes 1048592 | tf_op jit(solution)/shard_map/reduce_scatter | solution.py:37
  372.4 0.0 copy-start.1
  372.4 0.0 copy-start.2
  372.4 2.2 fusion.4
  374.6 0.0 copy-done.1
  374.6 0.0 copy-done.2
  374.7 1.5 fusion.7
  (3 shorter events, 0.0 us)
Async XLA Ops:
  8.0 282.1 %copy-start = (bf16[128,12288]{1,0:T(8,128)(2,1)S(1)}, bf16[128,12288]{1,0:T(8,128)(2,1)}, u32[]{:S(2)}) copy-start(bf16[128,12288]{1,0:T(8,128)(2,1)} %param.27) | copy-start | bytes 9437188
  8.0 4.9 %copy-start.6 = (bf16[256,128]{1,0:T(8,128)(2,1)S(1)}, bf16[256,128]{1,0:T(8,128)(2,1)}, u32[]{:S(2)}) copy-start(bf16[256,128]{1,0:T(8,128)(2,1)} %param.17) | copy-start | bytes 196612
  8.0 4.9 %copy-start.5 = (bf16[256,128]{1,0:T(8,128)(2,1)S(1)}, bf16[256,128]{1,0:T(8,128)(2,1)}, u32[]{:S(2)}) copy-start(bf16[256,128]{1,0:T(8,128)(2,1)} %param.18) | copy-start | bytes 196612
  8.0 161.4 %all-reduce.2.cloned.1.call-start = ((), (), s32[]{:S(2)}) async-start(), calls=%async_computation.1 | async-start | bytes 393216 | tf_op jit(solution)/shard_map/psum | solution.py:60
  12.1 4.4 %copy-start.3 = (f32[8192]{0:T(1024)S(1)}, f32[8192]{0:T(1024)}, u32[]{:S(2)}) copy-start(f32[8192]{0:T(1024)} %param.15) | copy-start | bytes 98308
  12.8 158.9 %all-gather.4.cloned.1.call-start = ((), (), s32[]{:S(2)}) async-start(), calls=%async_computation.2 | async-start | bytes 21626880 | tf_op jit(solution)/shard_map/all_gather | solution.py:33
  14.8 31.4 %copy-start.7 = (s32[2]{0:T(128)S(1)}, s32[2]{0:T(128)}, u32[]{:S(2)}) copy-start(s32[2]{0:T(128)} %param.22) | copy-start | bytes 28
  14.9 270.7 %all-gather.6.cloned.1.call-start = ((), (), s32[]{:S(2)}) async-start(), calls=%async_computation.4 | async-start | bytes 1622016 | tf_op jit(solution)/shard_map/all_gather | solution.py:72
  16.4 155.3 %copy-start.4 = (bf16[512,128]{1,0:T(8,128)(2,1)S(1)}, bf16[512,128]{1,0:T(8,128)(2,1)}, u32[]{:S(2)}) copy-start(bf16[512,128]{1,0:T(8,128)(2,1)} %param.21) | copy-start | bytes 393220
  171.6 200.8 %reduce-scatter.2.cloned.1.call-start = ((), (), s32[]{:S(2)}) async-start(), calls=%async_computation.3 | async-start | bytes 9437184 | tf_op jit(solution)/shard_map/reduce_scatter | solution.py:37
  372.4 2.2 copy-start.1
  372.4 2.2 copy-start.2
Sparse Core Ops, SparseCore 0:
  12.9 156.4 all-reduce.1
  189.4 182.9 reduce-scatter.1
Sparse Core Ops, SparseCore 1:
  16.4 146.5 all-gather.3
  171.7 113.7 all-gather.5
where the time goes:
time: 385 us; the launch traced here: 384 us
  waiting for transfers between devices  299 us (78%)
  matrix products  28.1 us (7%)
  blocking collectives  27.4 us (7%)
  between operations  15.7 us (4%)
  other arithmetic  7.3 us (2%)
  local copies, waits for them, and re-layouts  6.35 us (2%)
    psum x1, waiting for transfers between devices, local(): lax.psum(head_terms.reshape(-1).astype(jnp.bfloat16), 'tensor')  123 us
    all_gather x1, waiting for transfers between devices, local(): every_grad = lax.all_gather(example_grad, 'dp', axis=0, tiled=True)  96.2 us
    reduce_scatter x1, waiting for transfers between devices, local(): lax.psum_scatter(partial_sum.astype(jnp.bfloat16), 'tensor', scatter_dime...  79.1 us
    all_gather x1, blocking collectives, local(): lax.all_gather(local_sketch.reshape(-1), 'tensor', axis=0, tiled=True)  27.4 us
    dot_general x1, matrix products, local(): lax.dot_general(cot_local, lax.all_gather(w_local, 'dp', axis=0, tiled=Tr...  17.6 us
  transfers between devices with their start and end apart: 4, of which 3 were waited for; matrix products, arithmetic and copies ran while one was open for 9% of the time, Pallas kernels for 0%

commit v1 on v0

v1 whole, which is shorter than its diff:
```python
import functools

import jax
import jax.numpy as jnp
from jax import lax
from jax.experimental import pallas as pl
from jax.experimental.pallas import tpu as pltpu
from jax.sharding import PartitionSpec as P

EPSILON = 1e-05
BF = jnp.bfloat16
F32 = jnp.float32
VMEM_LIMIT = 48 * 1024 * 1024

NX, NZ, NC, NY, NL = 4, 4, 2, 4, 2
TOK = 64


def along_x(v, step):
    return lax.ppermute(v, "dp", [(i, (i // 8 + step) % NX * 8 + i % 8) for i in range(32)])


def along_z(v, step):
    return lax.ppermute(
        v, "dp", [(i, i // 8 * 8 + (i // 2 + step) % NZ * 2 + i % 2) for i in range(32)]
    )


def other_core(v):
    return lax.ppermute(v, "dp", [(i, i ^ 1) for i in range(32)])


def along_y(v, step):
    return lax.ppermute(v, "tensor", [(t, (t // 2 + step) % NY * 2 + t % 2) for t in range(8)])


def swap_l(v):
    return lax.ppermute(v, "tensor", [(t, t ^ 1) for t in range(8)])


def prepare_kernel(where, dq, dk, dv, cot):
    cot[:, :1024] = dq[...]
    cot[:, 1024:1152] = dk[...]
    cot[:, 1152:] = dv[...]


def prepare(where, dq, dk, dv):
    rows = lambda b, where: (where[b], 0)
    return pl.pallas_call(
        prepare_kernel,
        grid_spec=pltpu.PrefetchScalarGridSpec(
            num_scalar_prefetch=1,
            grid=(8,),
            in_specs=[
                pl.BlockSpec((TOK, 1024), rows),
                pl.BlockSpec((TOK, 128), rows),
                pl.BlockSpec((TOK, 128), rows),
            ],
            out_specs=pl.BlockSpec((TOK, 1280), lambda b, where: (b, 0)),
        ),
        out_shape=jax.ShapeDtypeStruct((512, 1280), BF),
        compiler_params=pltpu.CompilerParams(vmem_limit_bytes=VMEM_LIMIT),
        cost_estimate=pl.CostEstimate(flops=1, bytes_accessed=1, transcendentals=0),
    )(where, dq, dk, dv)


def side_by_side_kernel(q, k, v, out, sems):
    copies = []
    for ref, col in ((q, 0), (k, 1024), (v, 1152)):
        to = out.at[:, col : col + ref.shape[1]]
        copies.append(pltpu.make_async_copy(ref, to, sems.at[len(copies)]))
    for copy in copies:
        copy.start()
    for copy in copies:
        copy.wait()


def copied(kernel, rows, args, copies, scalars=()):
    hbm = pl.BlockSpec(memory_space=pltpu.HBM)
    return pl.pallas_call(
        kernel,
        in_specs=[pl.BlockSpec(memory_space=pltpu.SMEM)] * len(scalars) + [hbm] * len(args),
        out_specs=hbm,
        out_shape=shape(rows, 1280),
        scratch_shapes=[pltpu.SemaphoreType.DMA((copies,))],
        compiler_params=pltpu.CompilerParams(vmem_limit_bytes=VMEM_LIMIT),
        cost_estimate=pl.CostEstimate(flops=1, bytes_accessed=1, transcendentals=0),
    )(*scalars, *args)


def call(kernel, shapes, args, scratch=(), scalars=()):
    vmem = pl.BlockSpec(memory_space=pltpu.VMEM)
    return pl.pallas_call(
        kernel,
        in_specs=[pl.BlockSpec(memory_space=pltpu.SMEM)] * len(scalars) + [vmem] * len(args),
        out_specs=[vmem] * len(shapes),
        out_shape=list(shapes),
        scratch_shapes=list(scratch),
        compiler_params=pltpu.CompilerParams(vmem_limit_bytes=VMEM_LIMIT),
        cost_estimate=pl.CostEstimate(flops=1, bytes_accessed=1, transcendentals=0),
    )(*scalars, *args)


def shape(*dims):
    return jax.ShapeDtypeStruct(dims, BF)


def dot_t(left, right):
    return lax.dot_general(left, right, (((1,), (1,)), ((), ())), preferred_element_type=F32)


def head_kernel(where, d, pq, pk, pv, head):
    for m, (p, lo, hi) in enumerate(((pq, 0, 1024), (pk, 1024, 1152), (pv, 1152, 1280))):
        found = dot_t(d[:, lo:hi], p[...]).astype(BF)
        for b in range(8):
            rows = pl.ds(pl.multiple_of(where[b] * TOK, TOK), TOK)
            head[rows, m * 64 : m * 64 + 64] = found[b * TOK : b * TOK + TOK]


def sketch_kernel(hidden, gain, proj, out):
    rows = hidden[...].astype(F32)
    inv = lax.rsqrt(jnp.mean(rows * rows, axis=1, keepdims=True) + EPSILON)
    normed = (rows * inv * gain[...]).astype(BF)
    out[...] = dot_t(normed, proj[...]).astype(BF)


def outer_kernel(live, tokens, heads, out):
    head = heads[0:128].astype(F32)
    for t in range(1, 4):
        head = head + heads[t * 128 : t * 128 + 128].astype(F32)
    at = lax.broadcasted_iota(jnp.int32, (128, 192), 0)
    head = jnp.where(at < live[0], head, 0.0)
    to = lax.broadcasted_iota(jnp.int32, (64, 64), 1)
    source = jnp.where(to < 32, 2 * to, 2 * to - 63)
    pick = (lax.broadcasted_iota(jnp.int32, (64, 64), 0) == source).astype(F32).astype(BF)
    ordered = jnp.dot(tokens[...], pick, preferred_element_type=F32)
    for m in range(3):
        part = lax.dot_general(
            ordered,
            head[:, m * 64 : m * 64 + 64],
            (((0,), (0,)), ((), ())),
            precision=lax.Precision.HIGHEST,
            preferred_element_type=F32,
        ).astype(BF)
        for t in range(4):
            out[t, m * 32 : m * 32 + 32, :64] = part[:32]
            out[t, m * 32 : m * 32 + 32, 64:] = part[32:]


STAGE1 = [(j, r) for j in (0, 1, 3) for r in (0, 1, 3)]
STAGE2 = [(2, r) for r in (0, 1, 3, 2)] + [(j, 2) for j in (0, 1, 3)]
COLS1, COLS2 = 256 * len(STAGE1), 256 * len(STAGE2)


def product(blocks, js, rs, hs, ks, ds, ws, outs, left):
    n = 0
    for j in js:
        for k in ks:
            left[n * 128 : n * 128 + 128] = ds[j][k * 128 : k * 128 + 128]
            n += 1
    for h in hs:
        for r in rs:
            found = dot_t(left[: n * 128], ws[r][h][...]).astype(BF)
            m = 0
            for j in js:
                col = blocks.index((j, r)) * 256
                for k in ks:
                    outs[k][h][:, col : col + 256] = found[m * 128 : m * 128 + 128]
                    m += 1


def far1_kernel(h, d0, d1, d3, w0, w1, w3, out, left):
    ws = {r: {h: w} for r, w in ((0, w0), (1, w1), (3, w3))}
    product(STAGE1, (0, 1, 3), (0, 1, 3), (h,), (2,), {0: d0, 1: d1, 3: d3}, ws, {2: {h: out}}, left)


def near1_kernel(d0, d1, d3, w0, o0, w1, o1, w3, o3, one, three, own, left):
    ws = {0: (w0, o0), 1: (w1, o1), 3: (w3, o3)}
    outs = {k: (out.at[0], out.at[1]) for k, out in ((1, one), (3, three), (0, own))}
    product(STAGE1, (0, 1, 3), (0, 1, 3), (0, 1), (1, 3, 0), {0: d0, 1: d1, 3: d3}, ws, outs, left)


def stage2_kernel(d0, d1, d3, d2, w0, o0, w1, o1, w3, o3, w2, o2, far0, far1, one, three, own, left):
    ds = {0: d0, 1: d1, 3: d3, 2: d2}
    ws = {0: (w0, o0), 1: (w1, o1), 3: (w3, o3), 2: (w2, o2)}
    outs = {k: (out.at[0], out.at[1]) for k, out in ((1, one), (3, three), (0, own))}
    outs[2] = (far0, far1)
    product(STAGE2, (2,), (0, 1, 3, 2), (0, 1), (2, 1, 3, 0), ds, ws, outs, left)
    product(STAGE2, (0, 1, 3), (2,), (0, 1), (2, 1, 3, 0), ds, ws, outs, left)


def finish_kernel(pos, hidden, gain, e0, e1, e3, f0, f1, f3, f2, out):
    x, z, c = pos[0], pos[1], pos[2]
    rows = hidden[...].astype(F32)
    inv = lax.rsqrt(jnp.mean(rows * rows, axis=1, keepdims=True) + EPSILON)
    places = {(2, r): (f2, i * 256) for i, r in enumerate((0, 1, 3, 2))}
    for j, first, second in ((0, e0, f0), (1, e1, f1), (3, e3, f3)):
        places.update({(j, r): (first, i * 256) for i, r in enumerate((0, 1, 3))})
        places[j, 2] = (second, 0)

    def blocks():
        for (j, r), (ref, col) in places.items():
            for h in range(2):
                block = lax.rem(x + 4 - j, 4) * 8 + lax.rem(z + r, 4) * 2 + lax.rem(c + h, 2)
                cols = pl.ds(pl.multiple_of(block * 256, 256), 256)
                grad = ref[h, :, col : col + 256].astype(F32) * gain[:, cols]
                yield cols, grad, hidden[:, cols].astype(F32) * inv

    total = jnp.zeros((TOK, 256), F32)
    for cols, grad, unit in blocks():
        total += grad * unit
    mean = jnp.sum(total, axis=1, keepdims=True) * (1.0 / 8192)
    for cols, grad, unit in blocks():
        out[:, cols] = (inv * (grad - unit * mean)).astype(BF)


def add(*terms):
    total = terms[0].astype(F32)
    for term in terms[1:]:
        total = total + term.astype(F32)
    return total.astype(BF)


def second_kernel(far_up, far_down, one, three, up, down):
    up[0] = add(one[0], far_up[...])
    up[1] = one[1]
    down[0] = three[0]
    down[1] = add(three[1], far_down[...])


def second2_kernel(far_up, far_down, one, three, up2, down2, up3, down3):
    for up, down, lo, hi in ((up2, down2, 0, 1024), (up3, down3, 1024, 1792)):
        up[0] = add(one[0, :, lo:hi], far_up[:, lo:hi])
        up[1] = one[1, :, lo:hi]
        down[0] = three[0, :, lo:hi]
        down[1] = add(three[1, :, lo:hi], far_down[:, lo:hi])


def third_kernel(own, up, down, keep, send, col=0):
    cols = slice(col, col + up.shape[2])
    keep[...] = add(own[:, :TOK, cols], up[:, :TOK], down[:, :TOK])
    send[...] = add(own[:, TOK:, cols], up[:, TOK:], down[:, TOK:])


def split_kernel(keep, got, *outs):
    col = 0
    for out in outs:
        end = col + out.shape[2]
        out[...] = add(keep[:, :, col:end], got[:, :, col:end])
        col = end


def to_all(v, groups):
    copies = jnp.broadcast_to(v[None], (len(groups[0]), *v.shape))
    v = lax.all_to_all(copies, "dp", 0, 0, axis_index_groups=groups)
    return v.reshape(-1, 96, 128)


def local(
    hidden,
    norm_gain,
    w_query,
    w_key,
    w_value,
    d_query,
    d_key,
    d_value,
    lengths,
    proj_in,
    proj_query,
    proj_key,
    proj_value,
    queries,
):
    dp, tensor = lax.axis_index("dp"), lax.axis_index("tensor")
    x, z, c, y, low = dp // 8, dp // 2 % 4, dp % 2, tensor // 2, tensor % 2
    gain = norm_gain.reshape(1, -1)

    (tokens,) = call(sketch_kernel, [shape(TOK, 64)], [hidden, gain, proj_in.T])
    d_query, w_query, tokens = lax.optimization_barrier((d_query, w_query, tokens))
    other = swap_l(tokens)

    where = jnp.stack([(y + k) % 4 * 2 + (low + l) % 2 for k in range(4) for l in range(2)])
    where = where.astype(jnp.int32)
    d0 = prepare(where, d_query, d_key, d_value)
    d1, d3 = along_x(d0, -1), along_x(d0, 1)
    w0 = copied(side_by_side_kernel, 256, [w_query, w_key, w_value], 3)
    w0, other = lax.optimization_barrier((w0, other))
    tokens = jnp.concatenate([jnp.where(low == 0, tokens, other), jnp.where(low == 0, other, tokens)])

    w1, w3 = along_z(w0, -1), along_z(w0, 1)
    o0 = other_core(w0)

    (head,) = call(
        head_kernel,
        [shape(512, 192)],
        [d0, proj_query.T, proj_key.T, proj_value.T],
        scalars=[where],
    )
    over_y = dict(axis_index_groups=[[0, 2, 4, 6], [1, 3, 5, 7]], tiled=True)
    heads = lax.all_to_all(head, "tensor", 0, 0, **over_y)
    live = (lengths[y // 2] - y % 2 * 128).reshape(1)
    (outer,) = call(outer_kernel, [shape(4, 96, 128)], [tokens, heads], scalars=[live])
    outer = lax.all_to_all(outer, "tensor", 0, 0, **over_y)
    grads = jnp.sum(outer.reshape(2, 2, 96, 128).astype(F32), axis=1)

    d0, w0, o0, d1, d3, w1, w3, grads = lax.optimization_barrier((d0, w0, o0, d1, d3, w1, w3, grads))
    d2, w2 = along_x(d0, 2), along_z(w0, 2)
    grads = (grads + swap_l(grads)).astype(BF)
    o1, o3 = other_core(w1), other_core(w3)

    far0, far1 = (
        call(
            functools.partial(far1_kernel, h),
            [shape(128, COLS1)],
            [d0, d1, d3, *ws],
            [pltpu.VMEM((384, 1280), BF)],
        )[0]
        for h, ws in enumerate(((w0, w1, w3), (o0, o1, o3)))
    )
    grads, _ = lax.optimization_barrier((grads, far1))
    grads = to_all(grads, [[x * 8 + i for i in range(8)] for x in range(4)])
    far0, far1 = along_y(far0, 1), along_y(far1, -1)
    one, three, own = call(
        near1_kernel,
        [shape(2, 128, COLS1)] * 3,
        [d0, d1, d3, w0, o0, w1, o1, w3, o3],
        [pltpu.VMEM((1152, 1280), BF)],
    )
    steps = shape(2, 128, COLS1)
    up, down = call(second_kernel, [steps] * 2, [far0, far1, one, three])
    d2, w2, _, _ = lax.optimization_barrier((d2, w2, up, down))
    up, down = along_y(up, 1), along_y(down, -1)

    o2 = other_core(w2)
    steps = shape(2, 128, COLS2)
    far0, far1, one2, three2, own2 = call(
        stage2_kernel,
        [shape(128, COLS2)] * 2 + [steps] * 3,
        [d0, d1, d3, d2, w0, o0, w1, o1, w3, o3, w2, o2],
        [pltpu.VMEM((1536, 1280), BF)],
    )
    grads, _ = lax.optimization_barrier((grads, far1))
    grads = to_all(grads, [[x * 8 + i for x in range(4)] for i in range(8)])
    far0, far1 = along_y(far0, 1), along_y(far1, -1)

    up, down, far0, far1 = lax.optimization_barrier((up, down, far0, far1))
    mid, low_cols = shape(2, 128, 1024), shape(2, 128, 768)
    up2, down2, up3, down3 = call(
        second2_kernel, [mid, mid, low_cols, low_cols], [far0, far1, one2, three2]
    )
    up2, down2 = along_y(up2, 1), along_y(down2, -1)
    up3, down3 = along_y(up3, 1), along_y(down3, -1)
    keep, send = call(third_kernel, [shape(2, TOK, COLS1)] * 2, [own, up, down])
    got = swap_l(send)
    e0, e1, e3 = call(split_kernel, [shape(2, TOK, 768)] * 3, [keep, got])
    e1, e3 = along_x(e1, 1), along_x(e3, -1)
    keep, send = call(third_kernel, [shape(2, TOK, 1024)] * 2, [own2, up2, down2])
    (f2,) = call(split_kernel, [shape(2, TOK, 1024)], [keep, swap_l(send)])
    f2 = along_x(f2, 2)
    up3, down3, _, _ = lax.optimization_barrier((up3, down3, up2, down2))
    keep, send = call(
        functools.partial(third_kernel, col=1024), [shape(2, TOK, 768)] * 2, [own2, up3, down3]
    )
    f0, f1, f3 = call(split_kernel, [shape(2, TOK, 256)] * 3, [keep, swap_l(send)])
    f1, f3 = along_x(f1, 1), along_x(f3, -1)
    scores = dot_t(grads.reshape(64, 12288), queries)

    pos = jnp.stack([x, z, c]).astype(jnp.int32)
    (grad_hidden,) = call(
        finish_kernel,
        [shape(TOK, 8192)],
        [hidden, gain, e0, e1, e3, f0, f1, f3, f2],
        scalars=[pos],
    )
    return scores, grad_hidden


def solution(mesh):
    placed = (
        P(("dp", "tensor"), None),
        P(),
        P("dp", "tensor"),
        P("dp", "tensor"),
        P("dp", "tensor"),
        P("dp", "tensor"),
        P("dp", "tensor"),
        P("dp", "tensor"),
        P("dp"),
        P(),
        P("tensor", None),
        P("tensor", None),
        P("tensor", None),
        P(("dp", "tensor"), None),
    )
    return jax.shard_map(
        local,
        mesh=mesh,
        in_specs=placed,
        out_specs=(P(None, ("dp", "tensor")), P(("dp", "tensor"), None)),
        check_vma=False,
    )
```

time: 385 us -> 177 us (0.46)
  waiting for transfers between devices: 299 us -> 43.5 us
  Pallas kernels: 0 us -> 49.9 us
  starting transfers between devices: 0.17 us -> 50 us
  matrix products: 28.1 us -> 3.32 us
  blocking collectives: 27.4 us -> 8.18 us
  between operations: 15.7 us -> 1.67 us
  local copies, waits for them, and re-layouts: 6.35 us -> 17 us
  other arithmetic: 7.3 us -> 0.12 us
    psum x1 -> x0, waiting for transfers between devices: 123 us -> none  [local(): lax.psum(head_terms.reshape(-1).astype(jnp.bfloat16), 'tensor')]
    all_gather x2 -> x0, waiting for transfers between devices: 96.2 us -> none  [the longest x1 96.2 us: local(): every_grad = lax.all_gather(example_grad, 'dp', axis=0, tiled=True)]
    reduce_scatter x1 -> x0, waiting for transfers between devices: 79.1 us -> none  [local(): lax.psum_scatter(partial_sum.astype(jnp.bfloat16), 'tensor', scatter_dime...]
    pallas_call x0 -> x18, Pallas kernels: none -> 49.9 us  [the longest x16 45.7 us: call(): pl.pallas_call(kernel, in_specs=[pl.BlockSpec(memory_space=pltpu.SMEM)] *...]
    ppermute x0 -> x30, waiting for transfers between devices: none -> 39.4 us  [the longest x10 25.2 us: along_y(): lax.ppermute(v, 'tensor', [(t, (t // 2 + step) % NY * 2 + t % 2) for t in...]
    ppermute x0 -> x30, starting transfers between devices: none -> 33 us  [the longest x10 10.6 us: along_y(): lax.ppermute(v, 'tensor', [(t, (t // 2 + step) % NY * 2 + t % 2) for t in...]
    all_gather x1 -> x0, blocking collectives: 27.4 us -> none  [local(): lax.all_gather(local_sketch.reshape(-1), 'tensor', axis=0, tiled=True)]
    dot_general x7 -> x1, matrix products: 28.1 us -> 3.32 us  [dot_t(): lax.dot_general(left, right, (((1,), (1,)), ((), ())), preferred_element_...]
  transfers between devices with their start and end apart: 4 -> 33, of which waited for: 3 -> 14; matrix products, arithmetic and copies ran while one was open for 9% -> 5% of each run, Pallas kernels for 0% -> 25%
where the time goes in v1:
time: 177 us; the launch traced here: 174 us
  starting transfers between devices  50 us (28%)
  Pallas kernels  49.9 us (28%)
  waiting for transfers between devices  43.5 us (25%)
  local copies, waits for them, and re-layouts  17 us (10%)
  blocking collectives  8.18 us (5%)
  matrix products  3.32 us (2%)
    pallas_call x16, Pallas kernels, call(): pl.pallas_call(kernel, in_specs=[pl.BlockSpec(memory_space=pltpu.SMEM)] *...  45.7 us
    ppermute x10, waiting for transfers between devices, along_y(): lax.ppermute(v, 'tensor', [(t, (t // 2 + step) % NY * 2 + t % 2) for t in...  25.2 us
    unnamed x62, local copies, waits for them, and re-layouts  12.3 us
    all_to_all x2, starting transfers between devices, to_all(): v = lax.all_to_all(copies, 'dp', 0, 0, axis_index_groups=groups)  12.1 us
    ppermute x10, starting transfers between devices, along_y(): lax.ppermute(v, 'tensor', [(t, (t // 2 + step) % NY * 2 + t % 2) for t in...  10.6 us
    ppermute x3, starting transfers between devices, along_z(): lax.ppermute(v, 'dp', [(i, i // 8 * 8 + (i // 2 + step) % NZ * 2 + i % 2)...  9.92 us
    ppermute x8, starting transfers between devices, along_x(): lax.ppermute(v, 'dp', [(i, (i // 8 + step) % NX * 8 + i % 8) for i in ran...  9.79 us
    all_to_all x1, blocking collectives, local(): outer = lax.all_to_all(outer, 'tensor', 0, 0, **over_y)  8.18 us
  transfers between devices with their start and end apart: 33, of which 14 were waited for; matrix products, arithmetic and copies ran while one was open for 5% of the time, Pallas kernels for 25%

profile of v1, /device:TPU:14, one launch (start us, length us, event | category | flops | bytes accessed | tf_op | source)
XLA Modules:
  0.0 173.8 jit_solution(12303879736769154655)
XLA Ops:
  0.8 1.4 copy-done.5
  2.2 1.2 copy-done.10
  5.0 1.2 copy-done.11
  6.3 3.4 %shard_map.150.d.d0 = bf16[512,1280]{1,0:T(8,128)(2,1)} custom-call(s32[8]{0:T(128)S(1)} %stack.47.where, bf16[512,1024]{1,0:T(8,128)(2,1)S(1)} %copy-done.11, bf16[512,128]{1,0:T(8,128)(2,1)S(1)} %copy-done.23, bf16[512,128]{1,0:T(8,128)(2,1)S(1)} %copy-done.24), custom_call_target="tpu_custom_call" | custom-call | flops 1 | bytes 1 | tf_op jit(solution)/shard_map/pallas_call | solution.py:49
  10.2 1.5 collective-permute-start.2
  11.7 1.9 %collective-permute-start = (bf16[64,64]{1,0:T(8,128)(2,1)S(1)}, bf16[64,64]{1,0:T(8,128)(2,1)S(1)}, u32[]{:S(2)}, u32[]{:S(2)}) collective-permute-start(bf16[64,64]{1,0:T(8,128)(2,1)S(1)} %shard_map.149), channel_id=1, source_target_pairs={{0,1},{1,0},{2,3},{3,2},{4,5},{5,4},{6,7},{7,6},{8,9},{9,8},{10,11... | collective-permute-start | bytes 24584 | tf_op jit(solution)/shard_map/ppermute | solution.py:38
  15.4 3.3 %collective-permute-start.5 = (bf16[256,1280]{1,0:T(8,128)(2,1)}, bf16[256,1280]{1,0:T(8,128)(2,1)}, u32[]{:S(2)}, u32[]{:S(2)}) collective-permute-start(bf16[256,1280]{1,0:T(8,128)(2,1)} %shard_map.151.w0), channel_id=1, source_target_pairs={{0,16},{8,24},{16,32},{24,40},{32,48},{40,56},{48,0},{56,8},{64,80... | collective-permute-start | bytes 1966088 | tf_op jit(solution)/shard_map/ppermute | solution.py:24
  18.7 3.0 %collective-permute-start.4 = (bf16[256,1280]{1,0:T(8,128)(2,1)}, bf16[256,1280]{1,0:T(8,128)(2,1)}, u32[]{:S(2)}, u32[]{:S(2)}) collective-permute-start(bf16[256,1280]{1,0:T(8,128)(2,1)} %shard_map.151.w0), channel_id=1, source_target_pairs={{0,48},{8,56},{16,0},{24,8},{32,16},{40,24},{48,32},{56,40},{64,11... | collective-permute-start | bytes 1966088 | tf_op jit(solution)/shard_map/ppermute | solution.py:24
  21.8 1.8 %shard_map.152 = bf16[512,192]{1,0:T(8,128)(2,1)S(1)} custom-call(s32[8]{0:T(128)S(1)} %stack.47.where, bf16[512,1280]{1,0:T(8,128)(2,1)} %shard_map.150.d.d0, bf16[64,1024]{1,0:T(8,128)(2,1)S(1)} %bitcast.35, bf16[64,128]{1,0:T(8,128)(2,1)S(1)} %bitcast.36, bf16[64,128]{1,0:T(8,128)(2,1)S(1)} %bitcast.37), custom_call_target="tpu_custom_call" | custom-call | flops 1 | bytes 1 | tf_op jit(solution)/shard_map/pallas_call | solution.py:93
  24.4 4.9 %all-to-all-start = ((bf16[4,128,192]{1,2,0:T(8,128)(2,1)}), bf16[4,128,192]{1,2,0:T(8,128)(2,1)}, u32[]{:S(2)}, u32[]{:S(2)}) async-start(bf16[4,128,192]{1,2,0:T(8,128)(2,1)} %copy.16), calls=%async_computation | async-start | bytes 393216 | tf_op jit(solution)/shard_map/all_to_all | solution.py:301
  30.6 4.0 %all-to-all-done = bf16[4,128,192]{1,2,0:T(8,128)(2,1)} async-done(((bf16[4,128,192]{1,2,0:T(8,128)(2,1)}), bf16[4,128,192]{1,2,0:T(8,128)(2,1)}, u32[]{:S(2)}, u32[]{:S(2)}) %all-to-all-start) | async-done | bytes 196640 | tf_op jit(solution)/shard_map/all_to_all | solution.py:301
  36.2 8.2 %all_to_all.26 = bf16[4,96,128]{2,1,0:T(8,128)(2,1)S(1)} all-to-all(bf16[4,96,128]{2,1,0:T(8,128)(2,1)S(1)} %shard_map.153), channel_id=1, replica_groups={{0,2,4,6},{1,3,5,7},{8,10,12,14},{9,11,13,15},{16,18,20,22},{17,19,21,2..., dimensions={0} | all-to-all | bytes 196608 | tf_op jit(solution)/shard_map/all_to_all | solution.py:304
  44.5 6.3 %collective-permute-done.4.w1 = bf16[256,1280]{1,0:T(8,128)(2,1)} collective-permute-done((bf16[256,1280]{1,0:T(8,128)(2,1)}, bf16[256,1280]{1,0:T(8,128)(2,1)}, u32[]{:S(2)}, u32[]{:S(2)}) %collective-permute-start.4) | collective-permute-done | bytes 655392 | tf_op jit(solution)/shard_map/ppermute | solution.py:24
  50.7 1.5 collective-permute-start.9
  52.7 3.6 %collective-permute-start.10 = (bf16[256,1280]{1,0:T(8,128)(2,1)}, bf16[256,1280]{1,0:T(8,128)(2,1)}, u32[]{:S(2)}, u32[]{:S(2)}) collective-permute-start(bf16[256,1280]{1,0:T(8,128)(2,1)} %shard_map.151.w0), channel_id=1, source_target_pairs={{0,32},{8,40},{16,48},{24,56},{32,0},{40,8},{48,16},{56,24},{64,96... | collective-permute-start | bytes 1966088 | tf_op jit(solution)/shard_map/ppermute | solution.py:24
  56.4 3.6 %shard_map.155 = bf16[128,2304]{1,0:T(8,128)(2,1)S(1)} custom-call(bf16[512,1280]{1,0:T(8,128)(2,1)} %shard_map.150.d.d0, bf16[512,1280]{1,0:T(8,128)(2,1)} %collective-permute-done.2.d1, bf16[512,1280]{1,0:T(8,128)(2,1)} %collective-permute-done.3.d3, bf16[256,1280]{1,0:T(8,128)(2,1)} %shard_map.151.w0, bf16[256,1280]{1,0:T(8,128)(2,1)} %collective-permute-done.4.w1, ...), custom_call_target="tpu_custom_call" | custom-call | flops 1 | bytes 1 | tf_op jit(solution)/shard_map/pallas_call | solution.py:93
  60.0 1.7 collective-permute-start.11
  61.7 3.7 %shard_map.154 = bf16[128,2304]{1,0:T(8,128)(2,1)S(1)} custom-call(bf16[512,1280]{1,0:T(8,128)(2,1)} %shard_map.150.d.d0, bf16[512,1280]{1,0:T(8,128)(2,1)} %collective-permute-done.2.d1, bf16[512,1280]{1,0:T(8,128)(2,1)} %collective-permute-done.3.d3, bf16[256,1280]{1,0:T(8,128)(2,1)} %collective-permute-done.1.w0.o0, ...), custom_call_target="tpu_custom_call" | custom-call | flops 1 | bytes 1 | tf_op jit(solution)/shard_map/pallas_call | solution.py:93
  65.9 9.1 %shard_map.156 = (bf16[2,128,2304]{2,1,0:T(8,128)(2,1)S(1)}, bf16[2,128,2304]{2,1,0:T(8,128)(2,1)}, bf16[2,128,2304]{2,1,0:T(8,128)(2,1)}) custom-call(bf16[512,1280]{1,0:T(8,128)(2,1)} %shard_map.150.d.d0, bf16[512,1280]{1,0:T(8,128)(2,1)} %collective-permute-done.2.d1, bf16[512,1280]{1,0:T(8,128)(2,1)} %collective-permute-done.3.d3, ...), custom_call_target="tpu_custom_call" | custom-call | flops 1 | bytes 1 | tf_op jit(solution)/shard_map/pallas_call | solution.py:93
  75.0 5.1 %collective-permute-done.12.far_down = bf16[128,2304]{1,0:T(8,128)(2,1)S(1)} collective-permute-done((bf16[128,2304]{1,0:T(8,128)(2,1)S(1)}, bf16[128,2304]{1,0:T(8,128)(2,1)S(1)}, u32[]{:S(2)}, u32[]{:S(2)}) %collective-permute-start.12) | collective-permute-done | bytes 589856 | tf_op jit(solution)/shard_map/ppermute | solution.py:34
  80.1 1.3 copy-done.9
  81.4 1.6 shard_map.157
  83.0 1.3 collective-permute-start.14
  85.1 1.9 %collective-permute-done.6 = f32[2,96,128]{2,1,0:T(8,128)S(1)} collective-permute-done((f32[2,96,128]{2,1,0:T(8,128)S(1)}, f32[2,96,128]{2,1,0:T(8,128)S(1)}, u32[]{:S(2)}, u32[]{:S(2)}) %collective-permute-start.6) | collective-permute-done | bytes 98336 | tf_op jit(solution)/shard_map/ppermute | solution.py:38
  87.8 5.7 %all-to-all-start.2 = ((bf16[8,2,96,128]{3,2,1,0:T(8,128)(2,1)}), bf16[8,2,96,128]{3,2,1,0:T(8,128)(2,1)S(1)}, u32[]{:S(2)}, u32[]{:S(2)}) async-start(bf16[8,2,96,128]{3,2,1,0:T(8,128)(2,1)} %broadcast_in_dim.4), calls=%async_computation.2 | async-start | bytes 786432 | tf_op jit(solution)/shard_map/all_to_all | solution.py:255
  95.7 10.3 %shard_map.158 = (bf16[128,1792]{1,0:T(8,128)(2,1)}, bf16[128,1792]{1,0:T(8,128)(2,1)}, bf16[2,128,1792]{2,1,0:T(8,128)(2,1)}, bf16[2,128,1792]{2,1,0:T(8,128)(2,1)}, bf16[2,128,1792]{2,1,0:T(8,128)(2,1)}) custom-call(bf16[512,1280]{1,0:T(8,128)(2,1)} %shard_map.150.d.d0, bf16[512,1280]{1,0:T(8,128)(2,1)} %collective-permute-done.2.d1, ...), custom_call_target="tpu_custom_call" | custom-call | flops 1 | bytes 1 | tf_op jit(solution)/shard_map/pallas_call | solution.py:93
  106.0 1.6 collective-permute-start.16
  108.1 1.4 broadcast_in_dim.5
  109.6 6.4 %all-to-all-start.3 = ((bf16[4,16,96,128]{3,2,1,0:T(8,128)(2,1)}), bf16[4,16,96,128]{3,2,1,0:T(8,128)(2,1)}, u32[]{:S(2)}, u32[]{:S(2)}) async-start(bf16[4,16,96,128]{3,2,1,0:T(8,128)(2,1)} %broadcast_in_dim.5), calls=%async_computation.3 | async-start | bytes 3145728 | tf_op jit(solution)/shard_map/all_to_all | solution.py:255
  116.0 3.7 %collective-permute-done.16.far_up = bf16[128,1792]{1,0:T(8,128)(2,1)} collective-permute-done((bf16[128,1792]{1,0:T(8,128)(2,1)}, bf16[128,1792]{1,0:T(8,128)(2,1)}, u32[]{:S(2)}, u32[]{:S(2)}) %collective-permute-start.16) | collective-permute-done | bytes 458784 | tf_op jit(solution)/shard_map/ppermute | solution.py:34
  123.0 1.5 shard_map.161
  124.5 1.9 %collective-permute-start.23 = (bf16[2,128,1024]{2,1,0:T(8,128)(2,1)S(1)}, bf16[2,128,1024]{2,1,0:T(8,128)(2,1)S(1)}, u32[]{:S(2)}, u32[]{:S(2)}) collective-permute-start(bf16[2,128,1024]{2,1,0:T(8,128)(2,1)S(1)} %get-tuple-element.89), channel_id=1, source_target_pairs={{0,2},{1,3},{2,4},{3,5},{4,6},{5,7},{6,0},{7,1},{8,10},{9,11},{10,... | collective-permute-start | bytes 1572872 | tf_op jit(solution)/shard_map/ppermute | solution.py:34
  126.8 1.6 collective-permute-start.21
  128.9 2.7 %shard_map.159 = (bf16[2,64,2304]{2,1,0:T(8,128)(2,1)S(1)}, bf16[2,64,2304]{2,1,0:T(8,128)(2,1)}) custom-call(bf16[2,128,2304]{2,1,0:T(8,128)(2,1)S(1)} %copy-done.8, bf16[2,128,2304]{2,1,0:T(8,128)(2,1)} %collective-permute-done.14.up, bf16[2,128,2304]{2,1,0:T(8,128)(2,1)} %collective-permute-done.15.down), custom_call_target="tpu_custom_call" | custom-call | flops 1 | bytes 1 | tf_op jit(solution)/shard_map/pallas_call | solution.py:93
  131.9 7.8 %collective-permute-done.23.up = bf16[2,128,1024]{2,1,0:T(8,128)(2,1)S(1)} collective-permute-done((bf16[2,128,1024]{2,1,0:T(8,128)(2,1)S(1)}, bf16[2,128,1024]{2,1,0:T(8,128)(2,1)S(1)}, u32[]{:S(2)}, u32[]{:S(2)}) %collective-permute-start.23) | collective-permute-done | bytes 524320 | tf_op jit(solution)/shard_map/ppermute | solution.py:34
  139.7 1.6 collective-permute-done.24.down
  142.1 4.5 %collective-permute-done.21.up = bf16[2,128,768]{2,1,0:T(8,128)(2,1)S(1)} collective-permute-done((bf16[2,128,768]{2,1,0:T(8,128)(2,1)S(1)}, bf16[2,128,768]{2,1,0:T(8,128)(2,1)S(1)}, u32[]{:S(2)}, u32[]{:S(2)}) %collective-permute-start.21) | collective-permute-done | bytes 393248 | tf_op jit(solution)/shard_map/ppermute | solution.py:34
  146.6 1.5 collective-permute-done.22.down
  150.7 1.9 %shard_map.160 = (bf16[2,64,768]{2,1,0:T(8,128)(2,1)S(1)}, bf16[2,64,768]{2,1,0:T(8,128)(2,1)}, bf16[2,64,768]{2,1,0:T(8,128)(2,1)}) custom-call(bf16[2,64,2304]{2,1,0:T(8,128)(2,1)S(1)} %copy-done.15, bf16[2,64,2304]{2,1,0:T(8,128)(2,1)} %collective-permute-done.18.got), custom_call_target="tpu_custom_call" | custom-call | flops 1 | bytes 1 | tf_op jit(solution)/shard_map/pallas_call | solution.py:93
  152.6 2.1 %collective-permute-start.19 = (bf16[2,64,768]{2,1,0:T(8,128)(2,1)}, bf16[2,64,768]{2,1,0:T(8,128)(2,1)}, u32[]{:S(2)}, u32[]{:S(2)}) collective-permute-start(bf16[2,64,768]{2,1,0:T(8,128)(2,1)} %get-tuple-element.80), channel_id=1, source_target_pairs={{0,64},{8,72},{16,80},{24,88},{32,96},{40,104},{48,112},{56,120},{... | collective-permute-start | bytes 589832 | tf_op jit(solution)/shard_map/ppermute | solution.py:20
  154.7 1.2 collective-permute-done.25.got
  155.9 1.6 shard_map.163
  157.5 2.1 %collective-permute-start.26 = (bf16[2,64,256]{2,1,0:T(8,128)(2,1)}, bf16[2,64,256]{2,1,0:T(8,128)(2,1)S(1)}, u32[]{:S(2)}, u32[]{:S(2)}) collective-permute-start(bf16[2,64,256]{2,1,0:T(8,128)(2,1)} %get-tuple-element.96), channel_id=1, source_target_pairs={{0,64},{8,72},{16,80},{24,88},{32,96},{40,104},{48,112},{56,120},{... | collective-permute-start | bytes 196616 | tf_op jit(solution)/shard_map/ppermute | solution.py:20
  159.6 1.7 shard_map.165
  161.3 2.1 %collective-permute-start.29 = (bf16[2,64,1024]{2,1,0:T(8,128)(2,1)}, bf16[2,64,1024]{2,1,0:T(8,128)(2,1)S(1)}, u32[]{:S(2)}, u32[]{:S(2)}) collective-permute-start(bf16[2,64,1024]{2,1,0:T(8,128)(2,1)} %shard_map.165), channel_id=1, source_target_pairs={{0,128},{8,136},{16,144},{24,152},{32,160},{40,168},{48,176},{56,1... | collective-permute-start | bytes 786440 | tf_op jit(solution)/shard_map/ppermute | solution.py:20
  163.4 3.3 %fusion = f32[64,128]{1,0:T(8,128)} fusion(bf16[128,12288]{1,0:T(8,128)(2,1)S(1)} %copy-done, bf16[8,8,96,128]{3,2,1,0:T(8,128)(2,1)} %bitcast.24), kind=kOutput, calls=%fused_computation | convolution fusion | flops 201326592 | bytes 4751360 | tf_op jit(solution)/shard_map/dot_general | solution.py:109
  166.7 3.8 %collective-permute-done.27.f3 = bf16[2,64,256]{2,1,0:T(8,128)(2,1)} collective-permute-done((bf16[2,64,256]{2,1,0:T(8,128)(2,1)}, bf16[2,64,256]{2,1,0:T(8,128)(2,1)}, u32[]{:S(2)}, u32[]{:S(2)}) %collective-permute-start.27) | collective-permute-done | bytes 65568 | tf_op jit(solution)/shard_map/ppermute | solution.py:20
  170.6 3.3 %shard_map.166 = bf16[64,8192]{1,0:T(8,128)(2,1)} custom-call(s32[3]{0:T(128)S(1)} %pad_add_fusion.pos, bf16[64,8192]{1,0:T(8,128)(2,1)S(1)} %copy-done.6, f32[1,8192]{1,0:T(1,128)S(1)} %bitcast.34, bf16[2,64,768]{2,1,0:T(8,128)(2,1)S(1)} %copy-done.20, bf16[2,64,768]{2,1,0:T(8,128)(2,1)} %collective-permute-done.19.e1, ...), custom_call_target="tpu_custom_call" | custom-call | flops 1 | bytes 1 | tf_op jit(solution)/shard_map/pallas_call | solution.py:93
  (111 shorter events, 20.4 us)
Async XLA Ops:
  0.6 162.7 %copy-start = (bf16[128,12288]{1,0:T(8,128)(2,1)S(1)}, bf16[128,12288]{1,0:T(8,128)(2,1)}, u32[]{:S(2)}) copy-start(bf16[128,12288]{1,0:T(8,128)(2,1)} %param.27) | copy-start | bytes 9437188
  6.3 7.4 %copy-start.16 = (bf16[256,1024]{1,0:T(8,128)(2,1)S(1)}, bf16[256,1024]{1,0:T(8,128)(2,1)}, u32[]{:S(2)}) copy-start(bf16[256,1024]{1,0:T(8,128)(2,1)} %q) | copy-start | bytes 1572868
  6.3 7.4 %copy-start.26 = (bf16[256,128]{1,0:T(8,128)(2,1)S(1)}, bf16[256,128]{1,0:T(8,128)(2,1)}, u32[]{:S(2)}) copy-start(bf16[256,128]{1,0:T(8,128)(2,1)} %k.1) | copy-start | bytes 196612
  6.3 7.4 %copy-start.27 = (bf16[256,128]{1,0:T(8,128)(2,1)S(1)}, bf16[256,128]{1,0:T(8,128)(2,1)}, u32[]{:S(2)}) copy-start(bf16[256,128]{1,0:T(8,128)(2,1)} %v.1) | copy-start | bytes 196612
  9.6 12.1 %copy-start.25 = (bf16[1024,64]{0,1:T(8,128)(2,1)S(1)}, bf16[1024,64]{0,1:T(8,128)(2,1)}, u32[]{:S(2)}) copy-start(bf16[1024,64]{0,1:T(8,128)(2,1)} %param.24) | copy-start | bytes 393220
  9.6 12.1 %copy-start.28 = (bf16[128,64]{0,1:T(8,128)(2,1)S(1)}, bf16[128,64]{0,1:T(8,128)(2,1)}, u32[]{:S(2)}) copy-start(bf16[128,64]{0,1:T(8,128)(2,1)} %param.25) | copy-start | bytes 49156
  9.6 12.1 %copy-start.29 = (bf16[128,64]{0,1:T(8,128)(2,1)S(1)}, bf16[128,64]{0,1:T(8,128)(2,1)}, u32[]{:S(2)}) copy-start(bf16[128,64]{0,1:T(8,128)(2,1)} %param.26) | copy-start | bytes 49156
  9.6 41.1 %collective-permute-start.3 = (bf16[512,1280]{1,0:T(8,128)(2,1)}, bf16[512,1280]{1,0:T(8,128)(2,1)}, u32[]{:S(2)}, u32[]{:S(2)}) collective-permute-start(bf16[512,1280]{1,0:T(8,128)(2,1)} %shard_map.150.d.d0), channel_id=1, source_target_pairs={{0,64},{8,72},{16,80},{24,88},{32,96},{40,104},{48,112},{56,120},{... | collective-permute-start | bytes 3932168 | tf_op jit(solution)/shard_map/ppermute | solution.py:20
  10.2 40.6 %collective-permute-start.2 = (bf16[512,1280]{1,0:T(8,128)(2,1)}, bf16[512,1280]{1,0:T(8,128)(2,1)}, u32[]{:S(2)}, u32[]{:S(2)}) collective-permute-start(bf16[512,1280]{1,0:T(8,128)(2,1)} %shard_map.150.d.d0), channel_id=1, source_target_pairs={{0,192},{8,200},{16,208},{24,216},{32,224},{40,232},{48,240},{56,2... | collective-permute-start | bytes 3932168 | tf_op jit(solution)/shard_map/ppermute | solution.py:20
  11.7 3.7 %collective-permute-start = (bf16[64,64]{1,0:T(8,128)(2,1)S(1)}, bf16[64,64]{1,0:T(8,128)(2,1)S(1)}, u32[]{:S(2)}, u32[]{:S(2)}) collective-permute-start(bf16[64,64]{1,0:T(8,128)(2,1)S(1)} %shard_map.149), channel_id=1, source_target_pairs={{0,1},{1,0},{2,3},{3,2},{4,5},{5,4},{6,7},{7,6},{8,9},{9,8},{10,11... | collective-permute-start | bytes 24584 | tf_op jit(solution)/shard_map/ppermute | solution.py:38
  15.4 29.0 %collective-permute-start.5 = (bf16[256,1280]{1,0:T(8,128)(2,1)}, bf16[256,1280]{1,0:T(8,128)(2,1)}, u32[]{:S(2)}, u32[]{:S(2)}) collective-permute-start(bf16[256,1280]{1,0:T(8,128)(2,1)} %shard_map.151.w0), channel_id=1, source_target_pairs={{0,16},{8,24},{16,32},{24,40},{32,48},{40,56},{48,0},{56,8},{64,80... | collective-permute-start | bytes 1966088 | tf_op jit(solution)/shard_map/ppermute | solution.py:24
  18.7 32.0 %collective-permute-start.4 = (bf16[256,1280]{1,0:T(8,128)(2,1)}, bf16[256,1280]{1,0:T(8,128)(2,1)}, u32[]{:S(2)}, u32[]{:S(2)}) collective-permute-start(bf16[256,1280]{1,0:T(8,128)(2,1)} %shard_map.151.w0), channel_id=1, source_target_pairs={{0,48},{8,56},{16,0},{24,8},{32,16},{40,24},{48,32},{56,40},{64,11... | collective-permute-start | bytes 1966088 | tf_op jit(solution)/shard_map/ppermute | solution.py:24
  21.7 29.0 %collective-permute-start.1 = (bf16[256,1280]{1,0:T(8,128)(2,1)}, bf16[256,1280]{1,0:T(8,128)(2,1)}, u32[]{:S(2)}, u32[]{:S(2)}) collective-permute-start(bf16[256,1280]{1,0:T(8,128)(2,1)} %shard_map.151.w0), channel_id=1, source_target_pairs={{0,8},{8,0},{16,24},{24,16},{32,40},{40,32},{48,56},{56,48},{64,72... | collective-permute-start | bytes 1966088 | tf_op jit(solution)/shard_map/ppermute | solution.py:30
  21.8 7.6 %copy-start.30 = (s32[2]{0:T(128)S(1)}, s32[2]{0:T(128)}, u32[]{:S(2)}) copy-start(s32[2]{0:T(128)} %param.22) | copy-start | bytes 28
  24.4 10.2 %all-to-all-start = ((bf16[4,128,192]{1,2,0:T(8,128)(2,1)}), bf16[4,128,192]{1,2,0:T(8,128)(2,1)}, u32[]{:S(2)}, u32[]{:S(2)}) async-start(bf16[4,128,192]{1,2,0:T(8,128)(2,1)} %copy.16), calls=%async_computation | async-start | bytes 393216 | tf_op jit(solution)/shard_map/all_to_all | solution.py:301
  50.7 34.3 %collective-permute-start.9 = (bf16[512,1280]{1,0:T(8,128)(2,1)}, bf16[512,1280]{1,0:T(8,128)(2,1)}, u32[]{:S(2)}, u32[]{:S(2)}) collective-permute-start(bf16[512,1280]{1,0:T(8,128)(2,1)} %shard_map.150.d.d0), channel_id=1, source_target_pairs={{0,128},{8,136},{16,144},{24,152},{32,160},{40,168},{48,176},{56,1... | collective-permute-start | bytes 3932168 | tf_op jit(solution)/shard_map/ppermute | solution.py:20
  52.2 9.4 %collective-permute-start.7 = (bf16[256,1280]{1,0:T(8,128)(2,1)}, bf16[256,1280]{1,0:T(8,128)(2,1)S(1)}, u32[]{:S(2)}, u32[]{:S(2)}) collective-permute-start(bf16[256,1280]{1,0:T(8,128)(2,1)} %collective-permute-done.4.w1), channel_id=1, source_target_pairs={{0,8},{8,0},{16,24},{24,16},{32,40},{40,32},{48,56},{56,48},{64,72... | collective-permute-start | bytes 1966088 | tf_op jit(solution)/shard_map/ppermute | solution.py:30
  52.2 9.4 %collective-permute-start.8 = (bf16[256,1280]{1,0:T(8,128)(2,1)}, bf16[256,1280]{1,0:T(8,128)(2,1)S(1)}, u32[]{:S(2)}, u32[]{:S(2)}) collective-permute-start(bf16[256,1280]{1,0:T(8,128)(2,1)} %collective-permute-done.5.w3), channel_id=1, source_target_pairs={{0,8},{8,0},{16,24},{24,16},{32,40},{40,32},{48,56},{56,48},{64,72... | collective-permute-start | bytes 1966088 | tf_op jit(solution)/shard_map/ppermute | solution.py:30
  52.7 32.3 %collective-permute-start.10 = (bf16[256,1280]{1,0:T(8,128)(2,1)}, bf16[256,1280]{1,0:T(8,128)(2,1)}, u32[]{:S(2)}, u32[]{:S(2)}) collective-permute-start(bf16[256,1280]{1,0:T(8,128)(2,1)} %shard_map.151.w0), channel_id=1, source_target_pairs={{0,32},{8,40},{16,48},{24,56},{32,0},{40,8},{48,16},{56,24},{64,96... | collective-permute-start | bytes 1966088 | tf_op jit(solution)/shard_map/ppermute | solution.py:24
  60.0 15.0 %collective-permute-start.11 = (bf16[128,2304]{1,0:T(8,128)(2,1)S(1)}, bf16[128,2304]{1,0:T(8,128)(2,1)S(1)}, u32[]{:S(2)}, u32[]{:S(2)}) collective-permute-start(bf16[128,2304]{1,0:T(8,128)(2,1)S(1)} %shard_map.155), channel_id=1, source_target_pairs={{0,2},{1,3},{2,4},{3,5},{4,6},{5,7},{6,0},{7,1},{8,10},{9,11},{10,... | collective-permute-start | bytes 1769480 | tf_op jit(solution)/shard_map/ppermute | solution.py:34
  65.4 14.7 %collective-permute-start.12 = (bf16[128,2304]{1,0:T(8,128)(2,1)S(1)}, bf16[128,2304]{1,0:T(8,128)(2,1)S(1)}, u32[]{:S(2)}, u32[]{:S(2)}) collective-permute-start(bf16[128,2304]{1,0:T(8,128)(2,1)S(1)} %shard_map.154), channel_id=1, source_target_pairs={{0,6},{1,7},{2,0},{3,1},{4,2},{5,3},{6,4},{7,5},{8,14},{9,15},{10,... | collective-permute-start | bytes 1769480 | tf_op jit(solution)/shard_map/ppermute | solution.py:34
  65.9 21.1 %collective-permute-start.6 = (f32[2,96,128]{2,1,0:T(8,128)S(1)}, f32[2,96,128]{2,1,0:T(8,128)S(1)}, u32[]{:S(2)}, u32[]{:S(2)}) collective-permute-start(f32[2,96,128]{2,1,0:T(8,128)S(1)} %convert_reduce_fusion), channel_id=1, source_target_pairs={{0,1},{1,0},{2,3},{3,2},{4,5},{5,4},{6,7},{7,6},{8,9},{9,8},{10,11... | collective-permute-start | bytes 294920 | tf_op jit(solution)/shard_map/ppermute | solution.py:38
  83.0 37.6 %collective-permute-start.14 = (bf16[2,128,2304]{2,1,0:T(8,128)(2,1)}, bf16[2,128,2304]{2,1,0:T(8,128)(2,1)}, u32[]{:S(2)}, u32[]{:S(2)}) collective-permute-start(bf16[2,128,2304]{2,1,0:T(8,128)(2,1)} %get-tuple-element.67), channel_id=1, source_target_pairs={{0,2},{1,3},{2,4},{3,5},{4,6},{5,7},{6,0},{7,1},{8,10},{9,11},{10,... | collective-permute-start | bytes 3538952 | tf_op jit(solution)/shard_map/ppermute | solution.py:34
  84.3 36.4 %collective-permute-start.15 = (bf16[2,128,2304]{2,1,0:T(8,128)(2,1)}, bf16[2,128,2304]{2,1,0:T(8,128)(2,1)}, u32[]{:S(2)}, u32[]{:S(2)}) collective-permute-start(bf16[2,128,2304]{2,1,0:T(8,128)(2,1)} %get-tuple-element.68), channel_id=1, source_target_pairs={{0,6},{1,7},{2,0},{3,1},{4,2},{5,3},{6,4},{7,5},{8,14},{9,15},{10,... | collective-permute-start | bytes 3538952 | tf_op jit(solution)/shard_map/ppermute | solution.py:34
  85.0 8.4 %collective-permute-start.13 = (bf16[256,1280]{1,0:T(8,128)(2,1)}, bf16[256,1280]{1,0:T(8,128)(2,1)}, u32[]{:S(2)}, u32[]{:S(2)}) collective-permute-start(bf16[256,1280]{1,0:T(8,128)(2,1)} %collective-permute-done.10.w2), channel_id=1, source_target_pairs={{0,8},{8,0},{16,24},{24,16},{32,40},{40,32},{48,56},{56,48},{64,72... | collective-permute-start | bytes 1966088 | tf_op jit(solution)/shard_map/ppermute | solution.py:30
  87.8 20.3 %all-to-all-start.2 = ((bf16[8,2,96,128]{3,2,1,0:T(8,128)(2,1)}), bf16[8,2,96,128]{3,2,1,0:T(8,128)(2,1)S(1)}, u32[]{:S(2)}, u32[]{:S(2)}) async-start(bf16[8,2,96,128]{3,2,1,0:T(8,128)(2,1)} %broadcast_in_dim.4), calls=%async_computation.2 | async-start | bytes 786432 | tf_op jit(solution)/shard_map/all_to_all | solution.py:255
  106.0 13.7 %collective-permute-start.16 = (bf16[128,1792]{1,0:T(8,128)(2,1)}, bf16[128,1792]{1,0:T(8,128)(2,1)}, u32[]{:S(2)}, u32[]{:S(2)}) collective-permute-start(bf16[128,1792]{1,0:T(8,128)(2,1)} %get-tuple-element.74), channel_id=1, source_target_pairs={{0,2},{1,3},{2,4},{3,5},{4,6},{5,7},{6,0},{7,1},{8,10},{9,11},{10,... | collective-permute-start | bytes 1376264 | tf_op jit(solution)/shard_map/ppermute | solution.py:34
  107.6 13.1 %collective-permute-start.17 = (bf16[128,1792]{1,0:T(8,128)(2,1)}, bf16[128,1792]{1,0:T(8,128)(2,1)}, u32[]{:S(2)}, u32[]{:S(2)}) collective-permute-start(bf16[128,1792]{1,0:T(8,128)(2,1)} %get-tuple-element.71), channel_id=1, source_target_pairs={{0,6},{1,7},{2,0},{3,1},{4,2},{5,3},{6,4},{7,5},{8,14},{9,15},{10,... | collective-permute-start | bytes 1376264 | tf_op jit(solution)/shard_map/ppermute | solution.py:34
  109.6 53.8 %all-to-all-start.3 = ((bf16[4,16,96,128]{3,2,1,0:T(8,128)(2,1)}), bf16[4,16,96,128]{3,2,1,0:T(8,128)(2,1)}, u32[]{:S(2)}, u32[]{:S(2)}) async-start(bf16[4,16,96,128]{3,2,1,0:T(8,128)(2,1)} %broadcast_in_dim.5), calls=%async_computation.3 | async-start | bytes 3145728 | tf_op jit(solution)/shard_map/all_to_all | solution.py:255
  123.0 5.8 %copy-start.8 = (bf16[2,128,2304]{2,1,0:T(8,128)(2,1)S(1)}, bf16[2,128,2304]{2,1,0:T(8,128)(2,1)}, u32[]{:S(2)}) copy-start(bf16[2,128,2304]{2,1,0:T(8,128)(2,1)} %get-tuple-element.73.own) | copy-start | bytes 3538948
  124.5 15.2 %collective-permute-start.23 = (bf16[2,128,1024]{2,1,0:T(8,128)(2,1)S(1)}, bf16[2,128,1024]{2,1,0:T(8,128)(2,1)S(1)}, u32[]{:S(2)}, u32[]{:S(2)}) collective-permute-start(bf16[2,128,1024]{2,1,0:T(8,128)(2,1)S(1)} %get-tuple-element.89), channel_id=1, source_target_pairs={{0,2},{1,3},{2,4},{3,5},{4,6},{5,7},{6,0},{7,1},{8,10},{9,11},{10,... | collective-permute-start | bytes 1572872 | tf_op jit(solution)/shard_map/ppermute | solution.py:34
  126.4 14.9 %collective-permute-start.24 = (bf16[2,128,1024]{2,1,0:T(8,128)(2,1)S(1)}, bf16[2,128,1024]{2,1,0:T(8,128)(2,1)S(1)}, u32[]{:S(2)}, u32[]{:S(2)}) collective-permute-start(bf16[2,128,1024]{2,1,0:T(8,128)(2,1)S(1)} %get-tuple-element.90), channel_id=1, source_target_pairs={{0,6},{1,7},{2,0},{3,1},{4,2},{5,3},{6,4},{7,5},{8,14},{9,15},{10,... | collective-permute-start | bytes 1572872 | tf_op jit(solution)/shard_map/ppermute | solution.py:34
  126.8 19.8 %collective-permute-start.21 = (bf16[2,128,768]{2,1,0:T(8,128)(2,1)S(1)}, bf16[2,128,768]{2,1,0:T(8,128)(2,1)S(1)}, u32[]{:S(2)}, u32[]{:S(2)}) collective-permute-start(bf16[2,128,768]{2,1,0:T(8,128)(2,1)S(1)} %get-tuple-element.87), channel_id=1, source_target_pairs={{0,2},{1,3},{2,4},{3,5},{4,6},{5,7},{6,0},{7,1},{8,10},{9,11},{10,... | collective-permute-start | bytes 1179656 | tf_op jit(solution)/shard_map/ppermute | solution.py:34
  128.5 19.7 %collective-permute-start.22 = (bf16[2,128,768]{2,1,0:T(8,128)(2,1)S(1)}, bf16[2,128,768]{2,1,0:T(8,128)(2,1)S(1)}, u32[]{:S(2)}, u32[]{:S(2)}) collective-permute-start(bf16[2,128,768]{2,1,0:T(8,128)(2,1)S(1)} %get-tuple-element.88), channel_id=1, source_target_pairs={{0,6},{1,7},{2,0},{3,1},{4,2},{5,3},{6,4},{7,5},{8,14},{9,15},{10,... | collective-permute-start | bytes 1179656 | tf_op jit(solution)/shard_map/ppermute | solution.py:34
  128.9 12.4 %copy-start.7 = (bf16[2,128,1792]{2,1,0:T(8,128)(2,1)S(1)}, bf16[2,128,1792]{2,1,0:T(8,128)(2,1)}, u32[]{:S(2)}) copy-start(bf16[2,128,1792]{2,1,0:T(8,128)(2,1)} %get-tuple-element.82.own) | copy-start | bytes 2752516
  131.6 17.3 %copy-start.14 = (bf16[2,64,2304]{2,1,0:T(8,128)(2,1)}, bf16[2,64,2304]{2,1,0:T(8,128)(2,1)S(1)}, u32[]{:S(2)}) copy-start(bf16[2,64,2304]{2,1,0:T(8,128)(2,1)S(1)} %get-tuple-element.77.keep) | copy-start | bytes 1769476
  131.6 18.0 %collective-permute-start.18 = (bf16[2,64,2304]{2,1,0:T(8,128)(2,1)}, bf16[2,64,2304]{2,1,0:T(8,128)(2,1)}, u32[]{:S(2)}, u32[]{:S(2)}) collective-permute-start(bf16[2,64,2304]{2,1,0:T(8,128)(2,1)} %get-tuple-element.78), channel_id=1, source_target_pairs={{0,1},{1,0},{2,3},{3,2},{4,5},{5,4},{6,7},{7,6},{8,9},{9,8},{10,11... | collective-permute-start | bytes 1769480 | tf_op jit(solution)/shard_map/ppermute | solution.py:38
  142.1 17.4 %collective-permute-start.28 = (bf16[2,64,1024]{2,1,0:T(8,128)(2,1)}, bf16[2,64,1024]{2,1,0:T(8,128)(2,1)}, u32[]{:S(2)}, u32[]{:S(2)}) collective-permute-start(bf16[2,64,1024]{2,1,0:T(8,128)(2,1)} %get-tuple-element.99), channel_id=1, source_target_pairs={{0,1},{1,0},{2,3},{3,2},{4,5},{5,4},{6,7},{7,6},{8,9},{9,8},{10,11... | collective-permute-start | bytes 786440 | tf_op jit(solution)/shard_map/ppermute | solution.py:38
  149.5 6.4 %collective-permute-start.25 = (bf16[2,64,768]{2,1,0:T(8,128)(2,1)}, bf16[2,64,768]{2,1,0:T(8,128)(2,1)}, u32[]{:S(2)}, u32[]{:S(2)}) collective-permute-start(bf16[2,64,768]{2,1,0:T(8,128)(2,1)} %get-tuple-element.94), channel_id=1, source_target_pairs={{0,1},{1,0},{2,3},{3,2},{4,5},{5,4},{6,7},{7,6},{8,9},{9,8},{10,11... | collective-permute-start | bytes 589832 | tf_op jit(solution)/shard_map/ppermute | solution.py:38
  152.6 8.7 %copy-start.19 = (bf16[2,64,768]{2,1,0:T(8,128)(2,1)}, bf16[2,64,768]{2,1,0:T(8,128)(2,1)S(1)}, u32[]{:S(2)}) copy-start(bf16[2,64,768]{2,1,0:T(8,128)(2,1)S(1)} %get-tuple-element.79.e0) | copy-start | bytes 589828
  152.6 17.9 %collective-permute-start.19 = (bf16[2,64,768]{2,1,0:T(8,128)(2,1)}, bf16[2,64,768]{2,1,0:T(8,128)(2,1)}, u32[]{:S(2)}, u32[]{:S(2)}) collective-permute-start(bf16[2,64,768]{2,1,0:T(8,128)(2,1)} %get-tuple-element.80), channel_id=1, source_target_pairs={{0,64},{8,72},{16,80},{24,88},{32,96},{40,104},{48,112},{56,120},{... | collective-permute-start | bytes 589832 | tf_op jit(solution)/shard_map/ppermute | solution.py:20
  154.7 15.8 %collective-permute-start.20 = (bf16[2,64,768]{2,1,0:T(8,128)(2,1)}, bf16[2,64,768]{2,1,0:T(8,128)(2,1)}, u32[]{:S(2)}, u32[]{:S(2)}) collective-permute-start(bf16[2,64,768]{2,1,0:T(8,128)(2,1)} %get-tuple-element.81), channel_id=1, source_target_pairs={{0,192},{8,200},{16,208},{24,216},{32,224},{40,232},{48,240},{56,2... | collective-permute-start | bytes 589832 | tf_op jit(solution)/shard_map/ppermute | solution.py:20
  157.5 9.2 %collective-permute-start.26 = (bf16[2,64,256]{2,1,0:T(8,128)(2,1)}, bf16[2,64,256]{2,1,0:T(8,128)(2,1)S(1)}, u32[]{:S(2)}, u32[]{:S(2)}) collective-permute-start(bf16[2,64,256]{2,1,0:T(8,128)(2,1)} %get-tuple-element.96), channel_id=1, source_target_pairs={{0,64},{8,72},{16,80},{24,88},{32,96},{40,104},{48,112},{56,120},{... | collective-permute-start | bytes 196616 | tf_op jit(solution)/shard_map/ppermute | solution.py:20
  159.6 10.9 %collective-permute-start.27 = (bf16[2,64,256]{2,1,0:T(8,128)(2,1)}, bf16[2,64,256]{2,1,0:T(8,128)(2,1)}, u32[]{:S(2)}, u32[]{:S(2)}) collective-permute-start(bf16[2,64,256]{2,1,0:T(8,128)(2,1)} %get-tuple-element.97), channel_id=1, source_target_pairs={{0,192},{8,200},{16,208},{24,216},{32,224},{40,232},{48,240},{56,2... | collective-permute-start | bytes 196616 | tf_op jit(solution)/shard_map/ppermute | solution.py:20
  161.3 9.2 %collective-permute-start.29 = (bf16[2,64,1024]{2,1,0:T(8,128)(2,1)}, bf16[2,64,1024]{2,1,0:T(8,128)(2,1)S(1)}, u32[]{:S(2)}, u32[]{:S(2)}) collective-permute-start(bf16[2,64,1024]{2,1,0:T(8,128)(2,1)} %shard_map.165), channel_id=1, source_target_pairs={{0,128},{8,136},{16,144},{24,152},{32,160},{40,168},{48,176},{56,1... | collective-permute-start | bytes 786440 | tf_op jit(solution)/shard_map/ppermute | solution.py:20
  163.4 7.2 %copy-start.6 = (bf16[64,8192]{1,0:T(8,128)(2,1)S(1)}, bf16[64,8192]{1,0:T(8,128)(2,1)}, u32[]{:S(2)}) copy-start(bf16[64,8192]{1,0:T(8,128)(2,1)} %hidden.3) | copy-start | bytes 3145732
  163.4 7.2 %copy-start.20 = (bf16[2,64,768]{2,1,0:T(8,128)(2,1)S(1)}, bf16[2,64,768]{2,1,0:T(8,128)(2,1)}, u32[]{:S(2)}) copy-start(bf16[2,64,768]{2,1,0:T(8,128)(2,1)} %copy-done.19) | copy-start | bytes 589828
  163.4 7.2 %copy-start.22 = (f32[8192]{0:T(1024)S(1)}, f32[8192]{0:T(1024)}, u32[]{:S(2)}) copy-start(f32[8192]{0:T(1024)} %param.15) | copy-start | bytes 98308
  (16 other events, 31.1 us)

commit v2 on v1

--- a/solution.py
+++ b/solution.py
@@ -11,6 +11,7 @@
 BF = jnp.bfloat16
 F32 = jnp.float32
 VMEM_LIMIT = 48 * 1024 * 1024
+VMEM_ALL = 60 * 1024 * 1024
 
 NX, NZ, NC, NY, NL = 4, 4, 2, 4, 2
 TOK = 64
@@ -38,57 +39,59 @@
     return lax.ppermute(v, "tensor", [(t, t ^ 1) for t in range(8)])
 
 
-def prepare_kernel(where, dq, dk, dv, cot):
-    cot[:, :1024] = dq[...]
-    cot[:, 1024:1152] = dk[...]
-    cot[:, 1152:] = dv[...]
-
-
-def prepare(where, dq, dk, dv):
-    rows = lambda b, where: (where[b], 0)
-    return pl.pallas_call(
-        prepare_kernel,
-        grid_spec=pltpu.PrefetchScalarGridSpec(
-            num_scalar_prefetch=1,
-            grid=(8,),
-            in_specs=[
-                pl.BlockSpec((TOK, 1024), rows),
-                pl.BlockSpec((TOK, 128), rows),
-                pl.BlockSpec((TOK, 128), rows),
-            ],
-            out_specs=pl.BlockSpec((TOK, 1280), lambda b, where: (b, 0)),
-        ),
-        out_shape=jax.ShapeDtypeStruct((512, 1280), BF),
-        compiler_params=pltpu.CompilerParams(vmem_limit_bytes=VMEM_LIMIT),
-        cost_estimate=pl.CostEstimate(flops=1, bytes_accessed=1, transcendentals=0),
-    )(where, dq, dk, dv)
-
-
-def side_by_side_kernel(q, k, v, out, sems):
-    copies = []
-    for ref, col in ((q, 0), (k, 1024), (v, 1152)):
-        to = out.at[:, col : col + ref.shape[1]]
-        copies.append(pltpu.make_async_copy(ref, to, sems.at[len(copies)]))
-    for copy in copies:
+def prepare_kernel(place, dq, dk, dv, out, held, came, went):
+    arrivals, departures = [], []
+    for b in range(8):
+        low = lax.rem(place[1] + b % 2, 2)
+        rows = pl.ds(pl.multiple_of((place[0] + b // 2) % 4 * 128 + low * TOK, TOK), TOK)
+        to = slice(b * TOK, b * TOK + TOK)
+        for i, (ref, col) in enumerate(((dq, 0), (dk, 1024), (dv, 1152))):
+            part = held.at[to, col : col + ref.shape[1]]
+            arrivals.append(pltpu.make_async_copy(ref.at[rows], part, came.at[3 * b + i]))
+        departures.append(pltpu.make_async_copy(held.at[to], out.at[to], went.at[b]))
+    send_on(arrivals, departures)
+
+
+def side_by_side_kernel(q, k, v, out, held, came, went):
+    arrivals, departures = [], []
+    for b in range(4):
+        rows = slice(b * 64, b * 64 + 64)
+        for i, (ref, col) in enumerate(((q, 0), (k, 1024), (v, 1152))):
+            part = held.at[rows, col : col + ref.shape[1]]
+            arrivals.append(pltpu.make_async_copy(ref.at[rows], part, came.at[3 * b + i]))
+        departures.append(pltpu.make_async_copy(held.at[rows], out.at[rows], went.at[b]))
+    send_on(arrivals, departures)
+
+
+def send_on(arrivals, departures):
+    for copy in arrivals:
         copy.start()
-    for copy in copies:
+    for b, copy in enumerate(departures):
+        for arrival in arrivals[3 * b : 3 * b + 3]:
+            arrival.wait()
+        copy.start()
+    for copy in departures:
         copy.wait()
 
 
-def copied(kernel, rows, args, copies, scalars=()):
+def copied(kernel, rows, blocks, args, scalars=()):
     hbm = pl.BlockSpec(memory_space=pltpu.HBM)
     return pl.pallas_call(
         kernel,
         in_specs=[pl.BlockSpec(memory_space=pltpu.SMEM)] * len(scalars) + [hbm] * len(args),
         out_specs=hbm,
         out_shape=shape(rows, 1280),
-        scratch_shapes=[pltpu.SemaphoreType.DMA((copies,))],
-        compiler_params=pltpu.CompilerParams(vmem_limit_bytes=VMEM_LIMIT),
+        scratch_shapes=[
+            pltpu.VMEM((rows, 1280), BF),
+            pltpu.SemaphoreType.DMA((3 * blocks,)),
+            pltpu.SemaphoreType.DMA((blocks,)),
+        ],
+        compiler_params=pltpu.CompilerParams(vmem_limit_bytes=VMEM_ALL),
         cost_estimate=pl.CostEstimate(flops=1, bytes_accessed=1, transcendentals=0),
     )(*scalars, *args)
 
 
-def call(kernel, shapes, args, scratch=(), scalars=()):
+def call(kernel, shapes, args, scratch=(), scalars=(), vmem_limit=VMEM_LIMIT, flops=1):
     vmem = pl.BlockSpec(memory_space=pltpu.VMEM)
     return pl.pallas_call(
         kernel,
@@ -96,8 +99,8 @@
         out_specs=[vmem] * len(shapes),
         out_shape=list(shapes),
         scratch_shapes=list(scratch),
-        compiler_params=pltpu.CompilerParams(vmem_limit_bytes=VMEM_LIMIT),
-        cost_estimate=pl.CostEstimate(flops=1, bytes_accessed=1, transcendentals=0),
+        compiler_params=pltpu.CompilerParams(vmem_limit_bytes=vmem_limit),
+        cost_estimate=pl.CostEstimate(flops=flops, bytes_accessed=1, transcendentals=0),
     )(*scalars, *args)
 
 
@@ -109,12 +112,14 @@
     return lax.dot_general(left, right, (((1,), (1,)), ((), ())), preferred_element_type=F32)
 
 
-def head_kernel(where, d, pq, pk, pv, head):
+def head_kernel(place, d, pq, pk, pv, head):
     for m, (p, lo, hi) in enumerate(((pq, 0, 1024), (pk, 1024, 1152), (pv, 1152, 1280))):
         found = dot_t(d[:, lo:hi], p[...]).astype(BF)
         for b in range(8):
-            rows = pl.ds(pl.multiple_of(where[b] * TOK, TOK), TOK)
-            head[rows, m * 64 : m * 64 + 64] = found[b * TOK : b * TOK + TOK]
+            to = (place[0] + b // 2) % 4 * 128 + (place[1] + b % 2) % 2 * TOK
+            head[pl.ds(pl.multiple_of(to, TOK), TOK), m * 64 : m * 64 + 64] = found[
+                b * TOK : b * TOK + TOK
+            ]
 
 
 def sketch_kernel(hidden, gain, proj, out):
@@ -169,9 +174,28 @@
                     m += 1
 
 
-def far1_kernel(h, d0, d1, d3, w0, w1, w3, out, left):
-    ws = {r: {h: w} for r, w in ((0, w0), (1, w1), (3, w3))}
-    product(STAGE1, (0, 1, 3), (0, 1, 3), (h,), (2,), {0: d0, 1: d1, 3: d3}, ws, {2: {h: out}}, left)
+def far1_kernel(d0, d1, d3, w0, w1, w3, out, left):
+    for n, ref in enumerate((d0, d1, d3)):
+        left[n * 128 : n * 128 + 128] = ref[...]
+    for i, w in enumerate((w0, w1, w3)):
+        found = dot_t(left[...], w[...]).astype(BF)
+        for n in range(3):
+            col = (3 * n + i) * 256
+            out[:, col : col + 256] = found[n * 128 : n * 128 + 128]
+
+
+def far1_terms(ds, ws):
+    return pl.pallas_call(
+        far1_kernel,
+        grid=(1,),
+        in_specs=[pl.BlockSpec((128, 1280), lambda i: (2, 0))] * 3
+        + [pl.BlockSpec((256, 1280), lambda i: (0, 0))] * 3,
+        out_specs=pl.BlockSpec((128, COLS1), lambda i: (0, 0)),
+        out_shape=shape(128, COLS1),
+        scratch_shapes=[pltpu.VMEM((384, 1280), BF)],
+        compiler_params=pltpu.CompilerParams(vmem_limit_bytes=VMEM_ALL),
+        cost_estimate=pl.CostEstimate(flops=1, bytes_accessed=1, transcendentals=0),
+    )(*ds, *ws)
 
 
 def near1_kernel(d0, d1, d3, w0, o0, w1, o1, w3, o3, one, three, own, left):
@@ -189,8 +213,8 @@
     product(STAGE2, (0, 1, 3), (2,), (0, 1), (2, 1, 3, 0), ds, ws, outs, left)
 
 
-def finish_kernel(pos, hidden, gain, e0, e1, e3, f0, f1, f3, f2, out):
-    x, z, c = pos[0], pos[1], pos[2]
+def finish_kernel(place, hidden, gain, e0, e1, e3, f0, f1, f3, f2, out):
+    x, z, c = place[2], place[3], place[4]
     rows = hidden[...].astype(F32)
     inv = lax.rsqrt(jnp.mean(rows * rows, axis=1, keepdims=True) + EPSILON)
     places = {(2, r): (f2, i * 256) for i, r in enumerate((0, 1, 3, 2))}
@@ -276,26 +300,25 @@
     x, z, c, y, low = dp // 8, dp // 2 % 4, dp % 2, tensor // 2, tensor % 2
     gain = norm_gain.reshape(1, -1)
 
-    (tokens,) = call(sketch_kernel, [shape(TOK, 64)], [hidden, gain, proj_in.T])
-    d_query, w_query, tokens = lax.optimization_barrier((d_query, w_query, tokens))
+    (tokens,) = call(
+        sketch_kernel, [shape(TOK, 64)], [hidden, gain, proj_in.T], vmem_limit=VMEM_ALL
+    )
     other = swap_l(tokens)
 
-    where = jnp.stack([(y + k) % 4 * 2 + (low + l) % 2 for k in range(4) for l in range(2)])
-    where = where.astype(jnp.int32)
-    d0 = prepare(where, d_query, d_key, d_value)
-    d1, d3 = along_x(d0, -1), along_x(d0, 1)
-    w0 = copied(side_by_side_kernel, 256, [w_query, w_key, w_value], 3)
+    place = jnp.stack([y, low, x, z, c]).astype(jnp.int32)
+    w0 = copied(side_by_side_kernel, 256, 4, [w_query, w_key, w_value])
     w0, other = lax.optimization_barrier((w0, other))
     tokens = jnp.concatenate([jnp.where(low == 0, tokens, other), jnp.where(low == 0, other, tokens)])
-
     w1, w3 = along_z(w0, -1), along_z(w0, 1)
+    d0 = copied(prepare_kernel, 512, 8, [d_query, d_key, d_value], scalars=[place])
+    d1, d3 = along_x(d0, -1), along_x(d0, 1)
     o0 = other_core(w0)
 
     (head,) = call(
         head_kernel,
         [shape(512, 192)],
         [d0, proj_query.T, proj_key.T, proj_value.T],
-        scalars=[where],
+        scalars=[place],
     )
     over_y = dict(axis_index_groups=[[0, 2, 4, 6], [1, 3, 5, 7]], tiled=True)
     heads = lax.all_to_all(head, "tensor", 0, 0, **over_y)
@@ -309,15 +332,7 @@
     grads = (grads + swap_l(grads)).astype(BF)
     o1, o3 = other_core(w1), other_core(w3)
 
-    far0, far1 = (
-        call(
-            functools.partial(far1_kernel, h),
-            [shape(128, COLS1)],
-            [d0, d1, d3, *ws],
-            [pltpu.VMEM((384, 1280), BF)],
-        )[0]
-        for h, ws in enumerate(((w0, w1, w3), (o0, o1, o3)))
-    )
+    far0, far1 = (far1_terms([d0, d1, d3], ws) for ws in ([w0, w1, w3], [o0, o1, o3]))
     grads, _ = lax.optimization_barrier((grads, far1))
     grads = to_all(grads, [[x * 8 + i for i in range(8)] for x in range(4)])
     far0, far1 = along_y(far0, 1), along_y(far1, -1)
@@ -344,34 +359,38 @@
     grads = to_all(grads, [[x * 8 + i for x in range(4)] for i in range(8)])
     far0, far1 = along_y(far0, 1), along_y(far1, -1)
 
-    up, down, far0, far1 = lax.optimization_barrier((up, down, far0, far1))
-    mid, low_cols = shape(2, 128, 1024), shape(2, 128, 768)
+    keep, send = call(third_kernel, [shape(2, TOK, COLS1)] * 2, [own, up, down])
+    got = swap_l(send)
+    far0, far1, _ = lax.optimization_barrier((far0, far1, send))
+    wide, narrow = shape(2, 128, 1024), shape(2, 128, 768)
     up2, down2, up3, down3 = call(
-        second2_kernel, [mid, mid, low_cols, low_cols], [far0, far1, one2, three2]
+        second2_kernel, [wide, wide, narrow, narrow], [far0, far1, one2, three2]
     )
     up2, down2 = along_y(up2, 1), along_y(down2, -1)
     up3, down3 = along_y(up3, 1), along_y(down3, -1)
-    keep, send = call(third_kernel, [shape(2, TOK, COLS1)] * 2, [own, up, down])
-    got = swap_l(send)
     e0, e1, e3 = call(split_kernel, [shape(2, TOK, 768)] * 3, [keep, got])
+    up2, down2, _ = lax.optimization_barrier((up2, down2, e1))
     e1, e3 = along_x(e1, 1), along_x(e3, -1)
-    keep, send = call(third_kernel, [shape(2, TOK, 1024)] * 2, [own2, up2, down2])
-    (f2,) = call(split_kernel, [shape(2, TOK, 1024)], [keep, swap_l(send)])
+    keep2, send = call(third_kernel, [shape(2, TOK, 1024)] * 2, [own2, up2, down2])
+    got2 = swap_l(send)
+    up3, down3, _ = lax.optimization_barrier((up3, down3, send))
+    keep3, send = call(
+        functools.partial(third_kernel, col=1024), [shape(2, TOK, 768)] * 2, [own2, up3, down3]
+    )
+    got3 = swap_l(send)
+    (f2,) = call(split_kernel, [shape(2, TOK, 1024)], [keep2, got2])
+    scores = dot_t(grads.reshape(64, 12288), queries)
+    keep3, scores, _ = lax.optimization_barrier((keep3, scores, f2))
     f2 = along_x(f2, 2)
-    up3, down3, _, _ = lax.optimization_barrier((up3, down3, up2, down2))
-    keep, send = call(
-        functools.partial(third_kernel, col=1024), [shape(2, TOK, 768)] * 2, [own2, up3, down3]
-    )
-    f0, f1, f3 = call(split_kernel, [shape(2, TOK, 256)] * 3, [keep, swap_l(send)])
+    f0, f1, f3 = call(split_kernel, [shape(2, TOK, 256)] * 3, [keep3, got3])
     f1, f3 = along_x(f1, 1), along_x(f3, -1)
-    scores = dot_t(grads.reshape(64, 12288), queries)
-
-    pos = jnp.stack([x, z, c]).astype(jnp.int32)
+
     (grad_hidden,) = call(
         finish_kernel,
         [shape(TOK, 8192)],
         [hidden, gain, e0, e1, e3, f0, f1, f3, f2],
-        scalars=[pos],
+        scalars=[place],
+        vmem_limit=VMEM_ALL,
     )
     return scores, grad_hidden
 

time: 177 us -> 170 us (0.960)
  local copies, waits for them, and re-layouts: 17 us -> 11.5 us
    ppermute x10, waiting for transfers between devices: 25.2 us -> 9.76 us  [along_y(): lax.ppermute(v, 'tensor', [(t, (t // 2 + step) % NY * 2 + t % 2) for t in...]
    ppermute x3, waiting for transfers between devices: 6.28 us -> 15.5 us  [along_z(): lax.ppermute(v, 'dp', [(i, i // 8 * 8 + (i // 2 + step) % NZ * 2 + i % 2)...]
    pallas_call x16 -> x14, Pallas kernels: 45.7 us -> 37.3 us  [call(): pl.pallas_call(kernel, in_specs=[pl.BlockSpec(memory_space=pltpu.SMEM)] *...]
    unnamed x62 -> x42, local copies, waits for them, and re-layouts: 12.3 us -> 6.23 us
    ppermute x5, starting transfers between devices: 2.2 us -> 8.14 us  [swap_l(): return lax.ppermute(v, 'tensor', [(t, t ^ 1) for t in range(8)])]
    pallas_call x1 -> x2, Pallas kernels: 0.86 us -> 5.21 us  [copied(): pl.pallas_call(kernel, in_specs=[pl.BlockSpec(memory_space=pltpu.SMEM)] *...]
    pallas_call x1 -> x2, Pallas kernels: 3.37 us -> 7.21 us  [far1_terms(): pl.pallas_call(far1_kernel, grid=(1,), in_specs=[pl.BlockSpec((128, 1280)...]
    ppermute x3, starting transfers between devices: 9.92 us -> 6.73 us  [along_z(): lax.ppermute(v, 'dp', [(i, i // 8 * 8 + (i // 2 + step) % NZ * 2 + i % 2)...]
where the time goes in v2:
time: 170 us; the launch traced here: 169 us
  starting transfers between devices  51 us (30%)
  Pallas kernels  49.7 us (29%)
  waiting for transfers between devices  43.4 us (26%)
  local copies, waits for them, and re-layouts  11.5 us (7%)
  blocking collectives  8.18 us (5%)
  matrix products  3.26 us (2%)
    pallas_call x14, Pallas kernels, call(): pl.pallas_call(kernel, in_specs=[pl.BlockSpec(memory_space=pltpu.SMEM)] *...  37.3 us
    ppermute x3, waiting for transfers between devices, along_z(): lax.ppermute(v, 'dp', [(i, i // 8 * 8 + (i // 2 + step) % NZ * 2 + i % 2)...  15.5 us
    ppermute x8, starting transfers between devices, along_x(): lax.ppermute(v, 'dp', [(i, (i // 8 + step) % NX * 8 + i % 8) for i in ran...  10.6 us
    ppermute x10, starting transfers between devices, along_y(): lax.ppermute(v, 'tensor', [(t, (t // 2 + step) % NY * 2 + t % 2) for t in...  10.2 us
    all_to_all x2, starting transfers between devices, to_all(): v = lax.all_to_all(copies, 'dp', 0, 0, axis_index_groups=groups)  9.87 us
    ppermute x10, waiting for transfers between devices, along_y(): lax.ppermute(v, 'tensor', [(t, (t // 2 + step) % NY * 2 + t % 2) for t in...  9.76 us
    all_to_all x1, blocking collectives, local(): outer = lax.all_to_all(outer, 'tensor', 0, 0, **over_y)  8.18 us
    ppermute x5, starting transfers between devices, swap_l(): return lax.ppermute(v, 'tensor', [(t, t ^ 1) for t in range(8)])  8.14 us
  transfers between devices with their start and end apart: 33, of which 14 were waited for; matrix products, arithmetic and copies ran while one was open for 5% of the time, Pallas kernels for 25%

profile of v2, /device:TPU:14, one launch (start us, length us, event | category | flops | bytes accessed | tf_op | source)
XLA Modules:
  0.0 168.5 jit_solution(12868838616951289518)
XLA Ops:
  1.3 3.2 %shard_map.149.d.d0 = bf16[512,1280]{1,0:T(8,128)(2,1)} custom-call(s32[5]{0:T(128)} %stack.23.place, bf16[512,1024]{1,0:T(8,128)(2,1)} %dq.1, bf16[512,128]{1,0:T(8,128)(2,1)} %dk.1, bf16[512,128]{1,0:T(8,128)(2,1)} %dv.1), custom_call_target="tpu_custom_call" | custom-call | flops 1 | bytes 1 | tf_op jit(solution)/shard_map/pallas_call | solution.py:79
  5.4 2.4 %collective-permute-start.3 = (bf16[512,1280]{1,0:T(8,128)(2,1)}, bf16[512,1280]{1,0:T(8,128)(2,1)}, u32[]{:S(2)}, u32[]{:S(2)}) collective-permute-start(bf16[512,1280]{1,0:T(8,128)(2,1)} %shard_map.149.d.d0), channel_id=1, source_target_pairs={{0,64},{8,72},{16,80},{24,88},{32,96},{40,104},{48,112},{56,120},{... | collective-permute-start | bytes 3932168 | tf_op jit(solution)/shard_map/ppermute | solution.py:21
  7.8 2.9 %shard_map.151 = bf16[64,64]{1,0:T(8,128)(2,1)} custom-call(bf16[64,8192]{1,0:T(8,128)(2,1)} %hidden.3, f32[1,8192]{1,0:T(1,128)} %bitcast.31, bf16[64,8192]{1,0:T(8,128)(2,1)} %bitcast.30), custom_call_target="tpu_custom_call" | custom-call | flops 1 | bytes 1 | tf_op jit(solution)/shard_map/pallas_call | solution.py:96
  10.8 1.9 %collective-permute-start = (bf16[64,64]{1,0:T(8,128)(2,1)}, bf16[64,64]{1,0:T(8,128)(2,1)S(1)}, u32[]{:S(2)}, u32[]{:S(2)}) collective-permute-start(bf16[64,64]{1,0:T(8,128)(2,1)} %shard_map.151), channel_id=1, source_target_pairs={{0,1},{1,0},{2,3},{3,2},{4,5},{5,4},{6,7},{7,6},{8,9},{9,8},{10,11... | collective-permute-start | bytes 24584 | tf_op jit(solution)/shard_map/ppermute | solution.py:39
  12.7 2.0 %shard_map.150.w0 = bf16[256,1280]{1,0:T(8,128)(2,1)} custom-call(bf16[256,1024]{1,0:T(8,128)(2,1)} %q.1, bf16[256,128]{1,0:T(8,128)(2,1)} %k.1, bf16[256,128]{1,0:T(8,128)(2,1)} %v.1), custom_call_target="tpu_custom_call" | custom-call | flops 1 | bytes 1 | tf_op jit(solution)/shard_map/pallas_call | solution.py:79
  14.8 6.2 %collective-permute-start.4 = (bf16[256,1280]{1,0:T(8,128)(2,1)}, bf16[256,1280]{1,0:T(8,128)(2,1)}, u32[]{:S(2)}, u32[]{:S(2)}) collective-permute-start(bf16[256,1280]{1,0:T(8,128)(2,1)} %shard_map.150.w0), channel_id=1, source_target_pairs={{0,48},{8,56},{16,0},{24,8},{32,16},{40,24},{48,32},{56,40},{64,11... | collective-permute-start | bytes 1966088 | tf_op jit(solution)/shard_map/ppermute | solution.py:25
  21.1 1.3 copy-done.1
  24.3 4.9 %all-to-all-start = ((bf16[4,128,192]{1,2,0:T(8,128)(2,1)}), bf16[4,128,192]{1,2,0:T(8,128)(2,1)}, u32[]{:S(2)}, u32[]{:S(2)}) async-start(bf16[4,128,192]{1,2,0:T(8,128)(2,1)} %copy.16), calls=%async_computation | async-start | bytes 393216 | tf_op jit(solution)/shard_map/all_to_all | solution.py:324
  30.3 3.8 %all-to-all-done = bf16[4,128,192]{1,2,0:T(8,128)(2,1)} async-done(((bf16[4,128,192]{1,2,0:T(8,128)(2,1)}), bf16[4,128,192]{1,2,0:T(8,128)(2,1)}, u32[]{:S(2)}, u32[]{:S(2)}) %all-to-all-start) | async-done | bytes 196640 | tf_op jit(solution)/shard_map/all_to_all | solution.py:324
  35.8 8.2 %all_to_all.26 = bf16[4,96,128]{2,1,0:T(8,128)(2,1)S(1)} all-to-all(bf16[4,96,128]{2,1,0:T(8,128)(2,1)S(1)} %shard_map.153), channel_id=1, replica_groups={{0,2,4,6},{1,3,5,7},{8,10,12,14},{9,11,13,15},{16,18,20,22},{17,19,21,2..., dimensions={0} | all-to-all | bytes 196608 | tf_op jit(solution)/shard_map/all_to_all | solution.py:327
  44.0 6.1 %collective-permute-done.4.w1 = bf16[256,1280]{1,0:T(8,128)(2,1)} collective-permute-done((bf16[256,1280]{1,0:T(8,128)(2,1)}, bf16[256,1280]{1,0:T(8,128)(2,1)}, u32[]{:S(2)}, u32[]{:S(2)}) %collective-permute-start.4) | collective-permute-done | bytes 655392 | tf_op jit(solution)/shard_map/ppermute | solution.py:25
  50.1 3.8 %collective-permute-done.5.w3 = bf16[256,1280]{1,0:T(8,128)(2,1)} collective-permute-done((bf16[256,1280]{1,0:T(8,128)(2,1)}, bf16[256,1280]{1,0:T(8,128)(2,1)}, u32[]{:S(2)}, u32[]{:S(2)}) %collective-permute-start.5) | collective-permute-done | bytes 655392 | tf_op jit(solution)/shard_map/ppermute | solution.py:25
  55.1 3.6 %shard_map.154 = bf16[128,2304]{1,0:T(8,128)(2,1)} custom-call(bf16[512,1280]{1,0:T(8,128)(2,1)} %shard_map.149.d.d0, bf16[512,1280]{1,0:T(8,128)(2,1)} %collective-permute-done.2.d1, bf16[512,1280]{1,0:T(8,128)(2,1)} %collective-permute-done.3.d3, bf16[256,1280]{1,0:T(8,128)(2,1)} %shard_map.150.w0, bf16[256,1280]{1,0:T(8,128)(2,1)} %collective-permute-done.4.w1, ...), custom_call_target="tpu_custom_call" | custom-call | flops 1 | bytes 1 | tf_op jit(solution)/shard_map/pallas_call | solution.py:188
  58.7 1.6 collective-permute-start.8
  60.3 3.6 %shard_map.155 = bf16[128,2304]{1,0:T(8,128)(2,1)} custom-call(bf16[512,1280]{1,0:T(8,128)(2,1)} %shard_map.149.d.d0, bf16[512,1280]{1,0:T(8,128)(2,1)} %collective-permute-done.2.d1, bf16[512,1280]{1,0:T(8,128)(2,1)} %collective-permute-done.3.d3, bf16[256,1280]{1,0:T(8,128)(2,1)} %collective-permute-done.1.w0.o0, ...), custom_call_target="tpu_custom_call" | custom-call | flops 1 | bytes 1 | tf_op jit(solution)/shard_map/pallas_call | solution.py:188
  64.4 2.4 %collective-permute-start.22 = (f32[2,96,128]{2,1,0:T(8,128)S(1)}, f32[2,96,128]{2,1,0:T(8,128)S(1)}, u32[]{:S(2)}, u32[]{:S(2)}) collective-permute-start(f32[2,96,128]{2,1,0:T(8,128)S(1)} %convert_reduce_fusion), channel_id=1, source_target_pairs={{0,1},{1,0},{2,3},{3,2},{4,5},{5,4},{6,7},{7,6},{8,9},{9,8},{10,11... | collective-permute-start | bytes 294920 | tf_op jit(solution)/shard_map/ppermute | solution.py:39
  66.8 9.2 %shard_map.156 = (bf16[2,128,2304]{2,1,0:T(8,128)(2,1)S(1)}, bf16[2,128,2304]{2,1,0:T(8,128)(2,1)}, bf16[2,128,2304]{2,1,0:T(8,128)(2,1)}) custom-call(bf16[512,1280]{1,0:T(8,128)(2,1)} %shard_map.149.d.d0, bf16[512,1280]{1,0:T(8,128)(2,1)} %collective-permute-done.2.d1, bf16[512,1280]{1,0:T(8,128)(2,1)} %collective-permute-done.3.d3, ...), custom_call_target="tpu_custom_call" | custom-call | flops 1 | bytes 1 | tf_op jit(solution)/shard_map/pallas_call | solution.py:96
  76.0 2.8 %collective-permute-done.11.far_down = bf16[128,2304]{1,0:T(8,128)(2,1)S(1)} collective-permute-done((bf16[128,2304]{1,0:T(8,128)(2,1)}, bf16[128,2304]{1,0:T(8,128)(2,1)S(1)}, u32[]{:S(2)}, u32[]{:S(2)}) %collective-permute-start.11) | collective-permute-done | bytes 589856 | tf_op jit(solution)/shard_map/ppermute | solution.py:35
  78.8 1.3 copy-done.6
  80.1 2.8 %shard_map.157 = (bf16[2,128,2304]{2,1,0:T(8,128)(2,1)}, bf16[2,128,2304]{2,1,0:T(8,128)(2,1)}) custom-call(bf16[128,2304]{1,0:T(8,128)(2,1)} %collective-permute-done.8.far_up, bf16[128,2304]{1,0:T(8,128)(2,1)S(1)} %collective-permute-done.11.far_down, bf16[2,128,2304]{2,1,0:T(8,128)(2,1)S(1)} %get-tuple-element.59.one, bf16[2,128,2304]{2,1,0:T(8,128)(2,1)S(1)} %copy-done.6), custom_call_target="tpu_custom_call" | custom-call | flops 1 | bytes 1 | tf_op jit(solution)/shard_map/pallas_call | solution.py:96
  82.9 1.3 collective-permute-start.15
  84.9 5.6 %collective-permute-done.7.w2 = bf16[256,1280]{1,0:T(8,128)(2,1)} collective-permute-done((bf16[256,1280]{1,0:T(8,128)(2,1)}, bf16[256,1280]{1,0:T(8,128)(2,1)}, u32[]{:S(2)}, u32[]{:S(2)}) %collective-permute-start.7) | collective-permute-done | bytes 655392 | tf_op jit(solution)/shard_map/ppermute | solution.py:25
  91.3 3.5 %all-to-all-start.2 = ((bf16[8,2,96,128]{3,2,1,0:T(8,128)(2,1)}), bf16[8,2,96,128]{3,2,1,0:T(8,128)(2,1)S(1)}, u32[]{:S(2)}, u32[]{:S(2)}) async-start(bf16[8,2,96,128]{3,2,1,0:T(8,128)(2,1)} %broadcast_in_dim.4), calls=%async_computation.2 | async-start | bytes 786432 | tf_op jit(solution)/shard_map/all_to_all | solution.py:279
  94.8 1.1 copy-done.3
  95.9 10.5 %shard_map.158 = (bf16[128,1792]{1,0:T(8,128)(2,1)}, bf16[128,1792]{1,0:T(8,128)(2,1)}, bf16[2,128,1792]{2,1,0:T(8,128)(2,1)}, bf16[2,128,1792]{2,1,0:T(8,128)(2,1)}, bf16[2,128,1792]{2,1,0:T(8,128)(2,1)}) custom-call(bf16[512,1280]{1,0:T(8,128)(2,1)} %shard_map.149.d.d0, bf16[512,1280]{1,0:T(8,128)(2,1)} %collective-permute-done.2.d1, ...), custom_call_target="tpu_custom_call" | custom-call | flops 1 | bytes 1 | tf_op jit(solution)/shard_map/pallas_call | solution.py:96
  106.4 1.6 collective-permute-start.13
  108.4 1.6 all-to-all-done.2
  110.0 1.4 broadcast_in_dim.5
  111.4 6.4 %all-to-all-start.3 = ((bf16[4,16,96,128]{3,2,1,0:T(8,128)(2,1)}), bf16[4,16,96,128]{3,2,1,0:T(8,128)(2,1)}, u32[]{:S(2)}, u32[]{:S(2)}) async-start(bf16[4,16,96,128]{3,2,1,0:T(8,128)(2,1)} %broadcast_in_dim.5), calls=%async_computation.3 | async-start | bytes 3145728 | tf_op jit(solution)/shard_map/all_to_all | solution.py:279
  117.8 1.3 copy-done.5
  119.1 2.2 %shard_map.159 = (bf16[2,64,2304]{2,1,0:T(8,128)(2,1)S(1)}, bf16[2,64,2304]{2,1,0:T(8,128)(2,1)S(1)}) custom-call(bf16[2,128,2304]{2,1,0:T(8,128)(2,1)S(1)} %copy-done.5, bf16[2,128,2304]{2,1,0:T(8,128)(2,1)} %collective-permute-done.15.up, bf16[2,128,2304]{2,1,0:T(8,128)(2,1)} %collective-permute-done.16.down), custom_call_target="tpu_custom_call" | custom-call | flops 1 | bytes 1 | tf_op jit(solution)/shard_map/pallas_call | solution.py:96
  121.2 1.3 collective-permute-start.21
  122.6 1.5 shard_map.160
  124.0 1.6 collective-permute-start.19
  126.1 1.6 collective-permute-start.17
  128.2 6.7 %collective-permute-done.21.got = bf16[2,64,2304]{2,1,0:T(8,128)(2,1)S(1)} collective-permute-done((bf16[2,64,2304]{2,1,0:T(8,128)(2,1)S(1)}, bf16[2,64,2304]{2,1,0:T(8,128)(2,1)S(1)}, u32[]{:S(2)}, u32[]{:S(2)}) %collective-permute-start.21) | collective-permute-done | bytes 589856 | tf_op jit(solution)/shard_map/ppermute | solution.py:39
  135.7 3.3 %collective-permute-done.19.up = bf16[2,128,1024]{2,1,0:T(8,128)(2,1)S(1)} collective-permute-done((bf16[2,128,1024]{2,1,0:T(8,128)(2,1)S(1)}, bf16[2,128,1024]{2,1,0:T(8,128)(2,1)S(1)}, u32[]{:S(2)}, u32[]{:S(2)}) %collective-permute-start.19) | collective-permute-done | bytes 524320 | tf_op jit(solution)/shard_map/ppermute | solution.py:35
  139.0 1.6 collective-permute-done.20.down
  140.7 1.1 collective-permute-start.23
  141.9 1.5 collective-permute-start.24
  144.1 1.3 collective-permute-done.18.down
  146.2 1.4 collective-permute-start.26
  148.9 2.5 %collective-permute-start.29 = (bf16[2,64,1024]{2,1,0:T(8,128)(2,1)S(1)}, bf16[2,64,1024]{2,1,0:T(8,128)(2,1)}, u32[]{:S(2)}, u32[]{:S(2)}) collective-permute-start(bf16[2,64,1024]{2,1,0:T(8,128)(2,1)S(1)} %shard_map.164), channel_id=1, source_target_pairs={{0,128},{8,136},{16,144},{24,152},{32,160},{40,168},{48,176},{56,1... | collective-permute-start | bytes 786440 | tf_op jit(solution)/shard_map/ppermute | solution.py:21
  151.3 3.3 %fusion = f32[64,128]{1,0:T(8,128)} fusion(bf16[128,12288]{1,0:T(8,128)(2,1)S(1)} %copy-done, bf16[8,8,96,128]{3,2,1,0:T(8,128)(2,1)} %bitcast.18), kind=kOutput, calls=%fused_computation | convolution fusion | flops 201326592 | bytes 4751360 | tf_op jit(solution)/shard_map/dot_general | solution.py:112
  156.2 2.4 %collective-permute-start.27 = (bf16[2,64,256]{2,1,0:T(8,128)(2,1)S(1)}, bf16[2,64,256]{2,1,0:T(8,128)(2,1)S(1)}, u32[]{:S(2)}, u32[]{:S(2)}) collective-permute-start(bf16[2,64,256]{2,1,0:T(8,128)(2,1)S(1)} %get-tuple-element.96), channel_id=1, source_target_pairs={{0,64},{8,72},{16,80},{24,88},{32,96},{40,104},{48,112},{56,120},{... | collective-permute-start | bytes 196616 | tf_op jit(solution)/shard_map/ppermute | solution.py:21
  158.6 1.9 %collective-permute-done.27.f1 = bf16[2,64,256]{2,1,0:T(8,128)(2,1)S(1)} collective-permute-done((bf16[2,64,256]{2,1,0:T(8,128)(2,1)S(1)}, bf16[2,64,256]{2,1,0:T(8,128)(2,1)S(1)}, u32[]{:S(2)}, u32[]{:S(2)}) %collective-permute-start.27) | collective-permute-done | bytes 65568 | tf_op jit(solution)/shard_map/ppermute | solution.py:21
  160.5 3.6 %collective-permute-done.28.f3 = bf16[2,64,256]{2,1,0:T(8,128)(2,1)S(1)} collective-permute-done((bf16[2,64,256]{2,1,0:T(8,128)(2,1)S(1)}, bf16[2,64,256]{2,1,0:T(8,128)(2,1)S(1)}, u32[]{:S(2)}, u32[]{:S(2)}) %collective-permute-start.28) | collective-permute-done | bytes 65568 | tf_op jit(solution)/shard_map/ppermute | solution.py:21
  164.7 3.8 %shard_map.166 = bf16[64,8192]{1,0:T(8,128)(2,1)} custom-call(s32[5]{0:T(128)} %stack.23.place, bf16[64,8192]{1,0:T(8,128)(2,1)} %hidden.3, f32[1,8192]{1,0:T(1,128)} %bitcast.32, bf16[2,64,768]{2,1,0:T(8,128)(2,1)} %copy-done.11, bf16[2,64,768]{2,1,0:T(8,128)(2,1)} %collective-permute-done.24.e1, bf16[2,64,768]{2,1,0:T(8,128)(2,1)} %collective-permute-done.25.e3, ...), custom_call_target="tpu_custom_call" | custom-call | flops 1 | bytes 1 | tf_op jit(solution)/shard_map/pallas_call | solution.py:96
  (90 shorter events, 16.4 us)
Async XLA Ops:
  0.6 150.7 %copy-start = (bf16[128,12288]{1,0:T(8,128)(2,1)S(1)}, bf16[128,12288]{1,0:T(8,128)(2,1)}, u32[]{:S(2)}) copy-start(bf16[128,12288]{1,0:T(8,128)(2,1)} %param.27) | copy-start | bytes 9437188
  4.5 49.4 %collective-permute-start.2 = (bf16[512,1280]{1,0:T(8,128)(2,1)}, bf16[512,1280]{1,0:T(8,128)(2,1)}, u32[]{:S(2)}, u32[]{:S(2)}) collective-permute-start(bf16[512,1280]{1,0:T(8,128)(2,1)} %shard_map.149.d.d0), channel_id=1, source_target_pairs={{0,192},{8,200},{16,208},{24,216},{32,224},{40,232},{48,240},{56,2... | collective-permute-start | bytes 3932168 | tf_op jit(solution)/shard_map/ppermute | solution.py:21
  5.4 48.5 %collective-permute-start.3 = (bf16[512,1280]{1,0:T(8,128)(2,1)}, bf16[512,1280]{1,0:T(8,128)(2,1)}, u32[]{:S(2)}, u32[]{:S(2)}) collective-permute-start(bf16[512,1280]{1,0:T(8,128)(2,1)} %shard_map.149.d.d0), channel_id=1, source_target_pairs={{0,64},{8,72},{16,80},{24,88},{32,96},{40,104},{48,112},{56,120},{... | collective-permute-start | bytes 3932168 | tf_op jit(solution)/shard_map/ppermute | solution.py:21
  7.8 13.2 %copy-start.12 = (bf16[1024,64]{0,1:T(8,128)(2,1)S(1)}, bf16[1024,64]{0,1:T(8,128)(2,1)}, u32[]{:S(2)}) copy-start(bf16[1024,64]{0,1:T(8,128)(2,1)} %param.24) | copy-start | bytes 393220
  7.8 13.2 %copy-start.14 = (bf16[128,64]{0,1:T(8,128)(2,1)S(1)}, bf16[128,64]{0,1:T(8,128)(2,1)}, u32[]{:S(2)}) copy-start(bf16[128,64]{0,1:T(8,128)(2,1)} %param.25) | copy-start | bytes 49156
  7.8 13.2 %copy-start.15 = (bf16[128,64]{0,1:T(8,128)(2,1)S(1)}, bf16[128,64]{0,1:T(8,128)(2,1)}, u32[]{:S(2)}) copy-start(bf16[128,64]{0,1:T(8,128)(2,1)} %param.26) | copy-start | bytes 49156
  7.8 13.2 %copy-start.16 = (s32[5]{0:T(128)S(1)}, s32[5]{0:T(128)}, u32[]{:S(2)}) copy-start(s32[5]{0:T(128)} %stack.23.place) | copy-start | bytes 64
  10.8 3.9 %collective-permute-start = (bf16[64,64]{1,0:T(8,128)(2,1)}, bf16[64,64]{1,0:T(8,128)(2,1)S(1)}, u32[]{:S(2)}, u32[]{:S(2)}) collective-permute-start(bf16[64,64]{1,0:T(8,128)(2,1)} %shard_map.151), channel_id=1, source_target_pairs={{0,1},{1,0},{2,3},{3,2},{4,5},{5,4},{6,7},{7,6},{8,9},{9,8},{10,11... | collective-permute-start | bytes 24584 | tf_op jit(solution)/shard_map/ppermute | solution.py:39
  14.7 29.3 %collective-permute-start.1 = (bf16[256,1280]{1,0:T(8,128)(2,1)}, bf16[256,1280]{1,0:T(8,128)(2,1)}, u32[]{:S(2)}, u32[]{:S(2)}) collective-permute-start(bf16[256,1280]{1,0:T(8,128)(2,1)} %shard_map.150.w0), channel_id=1, source_target_pairs={{0,8},{8,0},{16,24},{24,16},{32,40},{40,32},{48,56},{56,48},{64,72... | collective-permute-start | bytes 1966088 | tf_op jit(solution)/shard_map/ppermute | solution.py:31
  14.8 35.3 %collective-permute-start.4 = (bf16[256,1280]{1,0:T(8,128)(2,1)}, bf16[256,1280]{1,0:T(8,128)(2,1)}, u32[]{:S(2)}, u32[]{:S(2)}) collective-permute-start(bf16[256,1280]{1,0:T(8,128)(2,1)} %shard_map.150.w0), channel_id=1, source_target_pairs={{0,48},{8,56},{16,0},{24,8},{32,16},{40,24},{48,32},{56,40},{64,11... | collective-permute-start | bytes 1966088 | tf_op jit(solution)/shard_map/ppermute | solution.py:25
  21.0 32.9 %collective-permute-start.5 = (bf16[256,1280]{1,0:T(8,128)(2,1)}, bf16[256,1280]{1,0:T(8,128)(2,1)}, u32[]{:S(2)}, u32[]{:S(2)}) collective-permute-start(bf16[256,1280]{1,0:T(8,128)(2,1)} %shard_map.150.w0), channel_id=1, source_target_pairs={{0,16},{8,24},{16,32},{24,40},{32,48},{40,56},{48,0},{56,8},{64,80... | collective-permute-start | bytes 1966088 | tf_op jit(solution)/shard_map/ppermute | solution.py:25
  22.4 6.8 %copy-start.20 = (s32[2]{0:T(128)S(1)}, s32[2]{0:T(128)}, u32[]{:S(2)}) copy-start(s32[2]{0:T(128)} %param.22) | copy-start | bytes 28
  22.4 7.9 %copy-start.17 = (bf16[64,64]{1,0:T(8,128)(2,1)S(1)}, bf16[64,64]{1,0:T(8,128)(2,1)}, u32[]{:S(2)}) copy-start(bf16[64,64]{1,0:T(8,128)(2,1)} %shard_map.151) | copy-start | bytes 24580
  24.3 9.9 %all-to-all-start = ((bf16[4,128,192]{1,2,0:T(8,128)(2,1)}), bf16[4,128,192]{1,2,0:T(8,128)(2,1)}, u32[]{:S(2)}, u32[]{:S(2)}) async-start(bf16[4,128,192]{1,2,0:T(8,128)(2,1)} %copy.16), calls=%async_computation | async-start | bytes 393216 | tf_op jit(solution)/shard_map/all_to_all | solution.py:324
  53.9 36.6 %collective-permute-start.6 = (bf16[512,1280]{1,0:T(8,128)(2,1)}, bf16[512,1280]{1,0:T(8,128)(2,1)}, u32[]{:S(2)}, u32[]{:S(2)}) collective-permute-start(bf16[512,1280]{1,0:T(8,128)(2,1)} %shard_map.149.d.d0), channel_id=1, source_target_pairs={{0,128},{8,136},{16,144},{24,152},{32,160},{40,168},{48,176},{56,1... | collective-permute-start | bytes 3932168 | tf_op jit(solution)/shard_map/ppermute | solution.py:21
  54.1 6.2 %collective-permute-start.10 = (bf16[256,1280]{1,0:T(8,128)(2,1)}, bf16[256,1280]{1,0:T(8,128)(2,1)}, u32[]{:S(2)}, u32[]{:S(2)}) collective-permute-start(bf16[256,1280]{1,0:T(8,128)(2,1)} %collective-permute-done.5.w3), channel_id=1, source_target_pairs={{0,8},{8,0},{16,24},{24,16},{32,40},{40,32},{48,56},{56,48},{64,72... | collective-permute-start | bytes 1966088 | tf_op jit(solution)/shard_map/ppermute | solution.py:31
  54.1 6.2 %collective-permute-start.9 = (bf16[256,1280]{1,0:T(8,128)(2,1)}, bf16[256,1280]{1,0:T(8,128)(2,1)}, u32[]{:S(2)}, u32[]{:S(2)}) collective-permute-start(bf16[256,1280]{1,0:T(8,128)(2,1)} %collective-permute-done.4.w1), channel_id=1, source_target_pairs={{0,8},{8,0},{16,24},{24,16},{32,40},{40,32},{48,56},{56,48},{64,72... | collective-permute-start | bytes 1966088 | tf_op jit(solution)/shard_map/ppermute | solution.py:31
  54.6 35.8 %collective-permute-start.7 = (bf16[256,1280]{1,0:T(8,128)(2,1)}, bf16[256,1280]{1,0:T(8,128)(2,1)}, u32[]{:S(2)}, u32[]{:S(2)}) collective-permute-start(bf16[256,1280]{1,0:T(8,128)(2,1)} %shard_map.150.w0), channel_id=1, source_target_pairs={{0,32},{8,40},{16,48},{24,56},{32,0},{40,8},{48,16},{56,24},{64,96... | collective-permute-start | bytes 1966088 | tf_op jit(solution)/shard_map/ppermute | solution.py:25
  58.7 8.0 %copy-start.2 = (bf16[256,1280]{1,0:T(8,128)(2,1)S(1)}, bf16[256,1280]{1,0:T(8,128)(2,1)}, u32[]{:S(2)}) copy-start(bf16[256,1280]{1,0:T(8,128)(2,1)} %shard_map.150.w0) | copy-start | bytes 1966084
  58.7 17.2 %collective-permute-start.8 = (bf16[128,2304]{1,0:T(8,128)(2,1)}, bf16[128,2304]{1,0:T(8,128)(2,1)}, u32[]{:S(2)}, u32[]{:S(2)}) collective-permute-start(bf16[128,2304]{1,0:T(8,128)(2,1)} %shard_map.154), channel_id=1, source_target_pairs={{0,2},{1,3},{2,4},{3,5},{4,6},{5,7},{6,0},{7,1},{8,10},{9,11},{10,... | collective-permute-start | bytes 1769480 | tf_op jit(solution)/shard_map/ppermute | solution.py:35
  63.9 14.9 %collective-permute-start.11 = (bf16[128,2304]{1,0:T(8,128)(2,1)}, bf16[128,2304]{1,0:T(8,128)(2,1)S(1)}, u32[]{:S(2)}, u32[]{:S(2)}) collective-permute-start(bf16[128,2304]{1,0:T(8,128)(2,1)} %shard_map.155), channel_id=1, source_target_pairs={{0,6},{1,7},{2,0},{3,1},{4,2},{5,3},{6,4},{7,5},{8,14},{9,15},{10,... | collective-permute-start | bytes 1769480 | tf_op jit(solution)/shard_map/ppermute | solution.py:35
  64.4 26.1 %collective-permute-start.22 = (f32[2,96,128]{2,1,0:T(8,128)S(1)}, f32[2,96,128]{2,1,0:T(8,128)S(1)}, u32[]{:S(2)}, u32[]{:S(2)}) collective-permute-start(f32[2,96,128]{2,1,0:T(8,128)S(1)} %convert_reduce_fusion), channel_id=1, source_target_pairs={{0,1},{1,0},{2,3},{3,2},{4,5},{5,4},{6,7},{7,6},{8,9},{9,8},{10,11... | collective-permute-start | bytes 294920 | tf_op jit(solution)/shard_map/ppermute | solution.py:39
  82.9 34.9 %collective-permute-start.15 = (bf16[2,128,2304]{2,1,0:T(8,128)(2,1)}, bf16[2,128,2304]{2,1,0:T(8,128)(2,1)}, u32[]{:S(2)}, u32[]{:S(2)}) collective-permute-start(bf16[2,128,2304]{2,1,0:T(8,128)(2,1)} %get-tuple-element.61), channel_id=1, source_target_pairs={{0,2},{1,3},{2,4},{3,5},{4,6},{5,7},{6,0},{7,1},{8,10},{9,11},{10,... | collective-permute-start | bytes 3538952 | tf_op jit(solution)/shard_map/ppermute | solution.py:35
  84.2 33.6 %collective-permute-start.16 = (bf16[2,128,2304]{2,1,0:T(8,128)(2,1)}, bf16[2,128,2304]{2,1,0:T(8,128)(2,1)}, u32[]{:S(2)}, u32[]{:S(2)}) collective-permute-start(bf16[2,128,2304]{2,1,0:T(8,128)(2,1)} %get-tuple-element.62), channel_id=1, source_target_pairs={{0,6},{1,7},{2,0},{3,1},{4,2},{5,3},{6,4},{7,5},{8,14},{9,15},{10,... | collective-permute-start | bytes 3538952 | tf_op jit(solution)/shard_map/ppermute | solution.py:35
  90.5 4.3 %collective-permute-start.12 = (bf16[256,1280]{1,0:T(8,128)(2,1)}, bf16[256,1280]{1,0:T(8,128)(2,1)}, u32[]{:S(2)}, u32[]{:S(2)}) collective-permute-start(bf16[256,1280]{1,0:T(8,128)(2,1)} %collective-permute-done.7.w2), channel_id=1, source_target_pairs={{0,8},{8,0},{16,24},{24,16},{32,40},{40,32},{48,56},{56,48},{64,72... | collective-permute-start | bytes 1966088 | tf_op jit(solution)/shard_map/ppermute | solution.py:31
  91.3 18.6 %all-to-all-start.2 = ((bf16[8,2,96,128]{3,2,1,0:T(8,128)(2,1)}), bf16[8,2,96,128]{3,2,1,0:T(8,128)(2,1)S(1)}, u32[]{:S(2)}, u32[]{:S(2)}) async-start(bf16[8,2,96,128]{3,2,1,0:T(8,128)(2,1)} %broadcast_in_dim.4), calls=%async_computation.2 | async-start | bytes 786432 | tf_op jit(solution)/shard_map/all_to_all | solution.py:279
  106.4 16.1 %collective-permute-start.13 = (bf16[128,1792]{1,0:T(8,128)(2,1)}, bf16[128,1792]{1,0:T(8,128)(2,1)}, u32[]{:S(2)}, u32[]{:S(2)}) collective-permute-start(bf16[128,1792]{1,0:T(8,128)(2,1)} %get-tuple-element.66), channel_id=1, source_target_pairs={{0,2},{1,3},{2,4},{3,5},{4,6},{5,7},{6,0},{7,1},{8,10},{9,11},{10,... | collective-permute-start | bytes 1376264 | tf_op jit(solution)/shard_map/ppermute | solution.py:35
  107.9 14.6 %collective-permute-start.14 = (bf16[128,1792]{1,0:T(8,128)(2,1)}, bf16[128,1792]{1,0:T(8,128)(2,1)}, u32[]{:S(2)}, u32[]{:S(2)}) collective-permute-start(bf16[128,1792]{1,0:T(8,128)(2,1)} %get-tuple-element.67), channel_id=1, source_target_pairs={{0,6},{1,7},{2,0},{3,1},{4,2},{5,3},{6,4},{7,5},{8,14},{9,15},{10,... | collective-permute-start | bytes 1376264 | tf_op jit(solution)/shard_map/ppermute | solution.py:35
  111.4 40.0 %all-to-all-start.3 = ((bf16[4,16,96,128]{3,2,1,0:T(8,128)(2,1)}), bf16[4,16,96,128]{3,2,1,0:T(8,128)(2,1)}, u32[]{:S(2)}, u32[]{:S(2)}) async-start(bf16[4,16,96,128]{3,2,1,0:T(8,128)(2,1)} %broadcast_in_dim.5), calls=%async_computation.3 | async-start | bytes 3145728 | tf_op jit(solution)/shard_map/all_to_all | solution.py:279
  119.1 3.5 %copy-start.7 = (bf16[2,128,1792]{2,1,0:T(8,128)(2,1)S(1)}, bf16[2,128,1792]{2,1,0:T(8,128)(2,1)}, u32[]{:S(2)}) copy-start(bf16[2,128,1792]{2,1,0:T(8,128)(2,1)} %get-tuple-element.72.one) | copy-start | bytes 2752516
  119.1 3.5 %copy-start.8 = (bf16[2,128,1792]{2,1,0:T(8,128)(2,1)S(1)}, bf16[2,128,1792]{2,1,0:T(8,128)(2,1)}, u32[]{:S(2)}) copy-start(bf16[2,128,1792]{2,1,0:T(8,128)(2,1)} %get-tuple-element.73.three) | copy-start | bytes 2752516
  121.2 13.6 %collective-permute-start.21 = (bf16[2,64,2304]{2,1,0:T(8,128)(2,1)S(1)}, bf16[2,64,2304]{2,1,0:T(8,128)(2,1)S(1)}, u32[]{:S(2)}, u32[]{:S(2)}) collective-permute-start(bf16[2,64,2304]{2,1,0:T(8,128)(2,1)S(1)} %get-tuple-element.69), channel_id=1, source_target_pairs={{0,1},{1,0},{2,3},{3,2},{4,5},{5,4},{6,7},{7,6},{8,9},{9,8},{10,11... | collective-permute-start | bytes 1769480 | tf_op jit(solution)/shard_map/ppermute | solution.py:39
  122.5 18.0 %copy-start.4 = (bf16[2,128,1792]{2,1,0:T(8,128)(2,1)S(1)}, bf16[2,128,1792]{2,1,0:T(8,128)(2,1)}, u32[]{:S(2)}) copy-start(bf16[2,128,1792]{2,1,0:T(8,128)(2,1)} %get-tuple-element.65.own) | copy-start | bytes 2752516
  124.0 14.9 %collective-permute-start.19 = (bf16[2,128,1024]{2,1,0:T(8,128)(2,1)S(1)}, bf16[2,128,1024]{2,1,0:T(8,128)(2,1)S(1)}, u32[]{:S(2)}, u32[]{:S(2)}) collective-permute-start(bf16[2,128,1024]{2,1,0:T(8,128)(2,1)S(1)} %get-tuple-element.76), channel_id=1, source_target_pairs={{0,2},{1,3},{2,4},{3,5},{4,6},{5,7},{6,0},{7,1},{8,10},{9,11},{10,... | collective-permute-start | bytes 1572872 | tf_op jit(solution)/shard_map/ppermute | solution.py:35
  125.7 14.9 %collective-permute-start.20 = (bf16[2,128,1024]{2,1,0:T(8,128)(2,1)S(1)}, bf16[2,128,1024]{2,1,0:T(8,128)(2,1)S(1)}, u32[]{:S(2)}, u32[]{:S(2)}) collective-permute-start(bf16[2,128,1024]{2,1,0:T(8,128)(2,1)S(1)} %get-tuple-element.77), channel_id=1, source_target_pairs={{0,6},{1,7},{2,0},{3,1},{4,2},{5,3},{6,4},{7,5},{8,14},{9,15},{10,... | collective-permute-start | bytes 1572872 | tf_op jit(solution)/shard_map/ppermute | solution.py:35
  126.1 18.0 %collective-permute-start.17 = (bf16[2,128,768]{2,1,0:T(8,128)(2,1)S(1)}, bf16[2,128,768]{2,1,0:T(8,128)(2,1)S(1)}, u32[]{:S(2)}, u32[]{:S(2)}) collective-permute-start(bf16[2,128,768]{2,1,0:T(8,128)(2,1)S(1)} %get-tuple-element.74), channel_id=1, source_target_pairs={{0,2},{1,3},{2,4},{3,5},{4,6},{5,7},{6,0},{7,1},{8,10},{9,11},{10,... | collective-permute-start | bytes 1179656 | tf_op jit(solution)/shard_map/ppermute | solution.py:35
  127.7 17.7 %collective-permute-start.18 = (bf16[2,128,768]{2,1,0:T(8,128)(2,1)S(1)}, bf16[2,128,768]{2,1,0:T(8,128)(2,1)S(1)}, u32[]{:S(2)}, u32[]{:S(2)}) collective-permute-start(bf16[2,128,768]{2,1,0:T(8,128)(2,1)S(1)} %get-tuple-element.75), channel_id=1, source_target_pairs={{0,6},{1,7},{2,0},{3,1},{4,2},{5,3},{6,4},{7,5},{8,14},{9,15},{10,... | collective-permute-start | bytes 1179656 | tf_op jit(solution)/shard_map/ppermute | solution.py:35
  135.7 10.5 %copy-start.11 = (bf16[2,64,768]{2,1,0:T(8,128)(2,1)}, bf16[2,64,768]{2,1,0:T(8,128)(2,1)S(1)}, u32[]{:S(2)}) copy-start(bf16[2,64,768]{2,1,0:T(8,128)(2,1)S(1)} %get-tuple-element.91.e0) | copy-start | bytes 589828
  140.7 8.1 %collective-permute-start.23 = (bf16[2,64,1024]{2,1,0:T(8,128)(2,1)S(1)}, bf16[2,64,1024]{2,1,0:T(8,128)(2,1)S(1)}, u32[]{:S(2)}, u32[]{:S(2)}) collective-permute-start(bf16[2,64,1024]{2,1,0:T(8,128)(2,1)S(1)} %get-tuple-element.82), channel_id=1, source_target_pairs={{0,1},{1,0},{2,3},{3,2},{4,5},{5,4},{6,7},{7,6},{8,9},{9,8},{10,11... | collective-permute-start | bytes 786440 | tf_op jit(solution)/shard_map/ppermute | solution.py:39
  141.9 16.7 %collective-permute-start.24 = (bf16[2,64,768]{2,1,0:T(8,128)(2,1)}, bf16[2,64,768]{2,1,0:T(8,128)(2,1)}, u32[]{:S(2)}, u32[]{:S(2)}) collective-permute-start(bf16[2,64,768]{2,1,0:T(8,128)(2,1)} %get-tuple-element.79), channel_id=1, source_target_pairs={{0,64},{8,72},{16,80},{24,88},{32,96},{40,104},{48,112},{56,120},{... | collective-permute-start | bytes 589832 | tf_op jit(solution)/shard_map/ppermute | solution.py:21
  146.2 2.7 %copy-start.9 = (bf16[2,64,768]{2,1,0:T(8,128)(2,1)}, bf16[2,64,768]{2,1,0:T(8,128)(2,1)S(1)}, u32[]{:S(2)}) copy-start(bf16[2,64,768]{2,1,0:T(8,128)(2,1)S(1)} %get-tuple-element.93.keep) | copy-start | bytes 589828
  146.2 8.4 %collective-permute-start.26 = (bf16[2,64,768]{2,1,0:T(8,128)(2,1)}, bf16[2,64,768]{2,1,0:T(8,128)(2,1)}, u32[]{:S(2)}, u32[]{:S(2)}) collective-permute-start(bf16[2,64,768]{2,1,0:T(8,128)(2,1)} %get-tuple-element.94), channel_id=1, source_target_pairs={{0,1},{1,0},{2,3},{3,2},{4,5},{5,4},{6,7},{7,6},{8,9},{9,8},{10,11... | collective-permute-start | bytes 589832 | tf_op jit(solution)/shard_map/ppermute | solution.py:39
  147.6 11.0 %collective-permute-start.25 = (bf16[2,64,768]{2,1,0:T(8,128)(2,1)}, bf16[2,64,768]{2,1,0:T(8,128)(2,1)}, u32[]{:S(2)}, u32[]{:S(2)}) collective-permute-start(bf16[2,64,768]{2,1,0:T(8,128)(2,1)} %get-tuple-element.92), channel_id=1, source_target_pairs={{0,192},{8,200},{16,208},{24,216},{32,224},{40,232},{48,240},{56,2... | collective-permute-start | bytes 589832 | tf_op jit(solution)/shard_map/ppermute | solution.py:21
  148.9 15.2 %collective-permute-start.29 = (bf16[2,64,1024]{2,1,0:T(8,128)(2,1)S(1)}, bf16[2,64,1024]{2,1,0:T(8,128)(2,1)}, u32[]{:S(2)}, u32[]{:S(2)}) collective-permute-start(bf16[2,64,1024]{2,1,0:T(8,128)(2,1)S(1)} %shard_map.164), channel_id=1, source_target_pairs={{0,128},{8,136},{16,144},{24,152},{32,160},{40,168},{48,176},{56,1... | collective-permute-start | bytes 786440 | tf_op jit(solution)/shard_map/ppermute | solution.py:21
  151.3 3.3 %copy-start.10 = (bf16[2,64,768]{2,1,0:T(8,128)(2,1)S(1)}, bf16[2,64,768]{2,1,0:T(8,128)(2,1)}, u32[]{:S(2)}) copy-start(bf16[2,64,768]{2,1,0:T(8,128)(2,1)} %copy-done.9) | copy-start | bytes 589828
  156.2 4.3 %collective-permute-start.27 = (bf16[2,64,256]{2,1,0:T(8,128)(2,1)S(1)}, bf16[2,64,256]{2,1,0:T(8,128)(2,1)S(1)}, u32[]{:S(2)}, u32[]{:S(2)}) collective-permute-start(bf16[2,64,256]{2,1,0:T(8,128)(2,1)S(1)} %get-tuple-element.96), channel_id=1, source_target_pairs={{0,64},{8,72},{16,80},{24,88},{32,96},{40,104},{48,112},{56,120},{... | collective-permute-start | bytes 196616 | tf_op jit(solution)/shard_map/ppermute | solution.py:21
  158.6 5.5 %collective-permute-start.28 = (bf16[2,64,256]{2,1,0:T(8,128)(2,1)S(1)}, bf16[2,64,256]{2,1,0:T(8,128)(2,1)S(1)}, u32[]{:S(2)}, u32[]{:S(2)}) collective-permute-start(bf16[2,64,256]{2,1,0:T(8,128)(2,1)S(1)} %get-tuple-element.97), channel_id=1, source_target_pairs={{0,192},{8,200},{16,208},{24,216},{32,224},{40,232},{48,240},{56,2... | collective-permute-start | bytes 196616 | tf_op jit(solution)/shard_map/ppermute | solution.py:21
  160.5 3.6 %copy-start.18 = (bf16[2,64,256]{2,1,0:T(8,128)(2,1)}, bf16[2,64,256]{2,1,0:T(8,128)(2,1)S(1)}, u32[]{:S(2)}) copy-start(bf16[2,64,256]{2,1,0:T(8,128)(2,1)S(1)} %collective-permute-done.27.f1) | copy-start | bytes 196612
  (6 other events, 6.2 us)

commit v3 on v2

--- a/solution.py
+++ b/solution.py
@@ -174,14 +174,15 @@
                     m += 1
 
 
-def far1_kernel(d0, d1, d3, w0, w1, w3, out, left):
+def far1_kernel(d0, d1, d3, w0, o0, w1, o1, w3, o3, far0, far1, left):
     for n, ref in enumerate((d0, d1, d3)):
         left[n * 128 : n * 128 + 128] = ref[...]
-    for i, w in enumerate((w0, w1, w3)):
-        found = dot_t(left[...], w[...]).astype(BF)
-        for n in range(3):
-            col = (3 * n + i) * 256
-            out[:, col : col + 256] = found[n * 128 : n * 128 + 128]
+    for out, ws in ((far0, (w0, w1, w3)), (far1, (o0, o1, o3))):
+        for i, w in enumerate(ws):
+            found = dot_t(left[...], w[...]).astype(BF)
+            for n in range(3):
+                col = (3 * n + i) * 256
+                out[:, col : col + 256] = found[n * 128 : n * 128 + 128]
 
 
 def far1_terms(ds, ws):
@@ -189,9 +190,9 @@
         far1_kernel,
         grid=(1,),
         in_specs=[pl.BlockSpec((128, 1280), lambda i: (2, 0))] * 3
-        + [pl.BlockSpec((256, 1280), lambda i: (0, 0))] * 3,
-        out_specs=pl.BlockSpec((128, COLS1), lambda i: (0, 0)),
-        out_shape=shape(128, COLS1),
+        + [pl.BlockSpec((256, 1280), lambda i: (0, 0))] * 6,
+        out_specs=[pl.BlockSpec((128, COLS1), lambda i: (0, 0))] * 2,
+        out_shape=[shape(128, COLS1)] * 2,
         scratch_shapes=[pltpu.VMEM((384, 1280), BF)],
         compiler_params=pltpu.CompilerParams(vmem_limit_bytes=VMEM_ALL),
         cost_estimate=pl.CostEstimate(flops=1, bytes_accessed=1, transcendentals=0),
@@ -327,12 +328,15 @@
     outer = lax.all_to_all(outer, "tensor", 0, 0, **over_y)
     grads = jnp.sum(outer.reshape(2, 2, 96, 128).astype(F32), axis=1)
 
-    d0, w0, o0, d1, d3, w1, w3, grads = lax.optimization_barrier((d0, w0, o0, d1, d3, w1, w3, grads))
+    w1, w3, grads = lax.optimization_barrier((w1, w3, grads))
+    o1, o3 = other_core(w1), other_core(w3)
+    d0, w0, o0, d1, d3, w1, w3, o1, o3, grads = lax.optimization_barrier(
+        (d0, w0, o0, d1, d3, w1, w3, o1, o3, grads)
+    )
     d2, w2 = along_x(d0, 2), along_z(w0, 2)
     grads = (grads + swap_l(grads)).astype(BF)
-    o1, o3 = other_core(w1), other_core(w3)
-
-    far0, far1 = (far1_terms([d0, d1, d3], ws) for ws in ([w0, w1, w3], [o0, o1, o3]))
+
+    far0, far1 = far1_terms([d0, d1, d3], [w0, o0, w1, o1, w3, o3])
     grads, _ = lax.optimization_barrier((grads, far1))
     grads = to_all(grads, [[x * 8 + i for i in range(8)] for x in range(4)])
     far0, far1 = along_y(far0, 1), along_y(far1, -1)
@@ -347,6 +351,8 @@
     d2, w2, _, _ = lax.optimization_barrier((d2, w2, up, down))
     up, down = along_y(up, 1), along_y(down, -1)
 
+    first = other_core(w2[:16, :128])
+    w2, first = lax.optimization_barrier((w2, first))
     o2 = other_core(w2)
     steps = shape(2, 128, COLS2)
     far0, far1, one2, three2, own2 = call(

time: 170 us -> 164 us (0.965)
  blocking collectives: 8.18 us -> 0 us
  starting transfers between devices: 51 us -> 56 us
  Pallas kernels: 49.7 us -> 46.9 us
    all_to_all x1 -> x0, blocking collectives: 8.18 us -> none  [local(): outer = lax.all_to_all(outer, 'tensor', 0, 0, **over_y)]
    ppermute x3, waiting for transfers between devices: 15.5 us -> 8.53 us  [along_z(): lax.ppermute(v, 'dp', [(i, i // 8 * 8 + (i // 2 + step) % NZ * 2 + i % 2)...]
    all_to_all x0 -> x1, starting transfers between devices: none -> 4.73 us  [local(): outer = lax.all_to_all(outer, 'tensor', 0, 0, **over_y)]
    all_to_all x0 -> x1, waiting for transfers between devices: none -> 4.34 us  [local(): outer = lax.all_to_all(outer, 'tensor', 0, 0, **over_y)]
    pallas_call x2 -> x1, Pallas kernels: 7.21 us -> 4.92 us  [far1_terms(): pl.pallas_call(far1_kernel, grid=(1,), in_specs=[pl.BlockSpec((128, 1280)...]
    ppermute x8, waiting for transfers between devices: 5.48 us -> 7.7 us  [along_x(): lax.ppermute(v, 'dp', [(i, (i // 8 + step) % NX * 8 + i % 8) for i in ran...]
    ppermute x5, starting transfers between devices: 8.14 us -> 6.25 us  [swap_l(): return lax.ppermute(v, 'tensor', [(t, t ^ 1) for t in range(8)])]
    ppermute x3, starting transfers between devices: 6.73 us -> 8.59 us  [along_z(): lax.ppermute(v, 'dp', [(i, i // 8 * 8 + (i // 2 + step) % NZ * 2 + i % 2)...]
  transfers between devices with their start and end apart: 33 -> 34, of which waited for: 14 -> 17; matrix products, arithmetic and copies ran while one was open for 5% -> 5% of each run, Pallas kernels for 25% -> 25%
where the time goes in v3:
time: 164 us; the launch traced here: 163 us
  starting transfers between devices  56 us (34%)
  Pallas kernels  46.9 us (29%)
  waiting for transfers between devices  43.5 us (27%)
  local copies, waits for them, and re-layouts  11.6 us (7%)
  matrix products  3.27 us (2%)
    pallas_call x14, Pallas kernels, call(): pl.pallas_call(kernel, in_specs=[pl.BlockSpec(memory_space=pltpu.SMEM)] *...  36.9 us
    ppermute x10, starting transfers between devices, along_y(): lax.ppermute(v, 'tensor', [(t, (t // 2 + step) % NY * 2 + t % 2) for t in...  10.6 us
    all_to_all x2, starting transfers between devices, to_all(): v = lax.all_to_all(copies, 'dp', 0, 0, axis_index_groups=groups)  10.5 us
    ppermute x8, starting transfers between devices, along_x(): lax.ppermute(v, 'dp', [(i, (i // 8 + step) % NX * 8 + i % 8) for i in ran...  9.93 us
    ppermute x3, starting transfers between devices, along_z(): lax.ppermute(v, 'dp', [(i, i // 8 * 8 + (i // 2 + step) % NZ * 2 + i % 2)...  8.59 us
    ppermute x3, waiting for transfers between devices, along_z(): lax.ppermute(v, 'dp', [(i, i // 8 * 8 + (i // 2 + step) % NZ * 2 + i % 2)...  8.53 us
    ppermute x5, waiting for transfers between devices, swap_l(): return lax.ppermute(v, 'tensor', [(t, t ^ 1) for t in range(8)])  8.39 us
    ppermute x10, waiting for transfers between devices, along_y(): lax.ppermute(v, 'tensor', [(t, (t // 2 + step) % NY * 2 + t % 2) for t in...  8.33 us
  transfers between devices with their start and end apart: 34, of which 17 were waited for; matrix products, arithmetic and copies ran while one was open for 5% of the time, Pallas kernels for 25%

profile of v3, /device:TPU:14, one launch (start us, length us, event | category | flops | bytes accessed | tf_op | source)
XLA Modules:
  0.0 162.9 jit_solution(3378479814698123854)
XLA Ops:
  0.6 3.0 %shard_map.151 = bf16[64,64]{1,0:T(8,128)(2,1)} custom-call(bf16[64,8192]{1,0:T(8,128)(2,1)} %hidden.3, f32[1,8192]{1,0:T(1,128)} %bitcast.31, bf16[64,8192]{1,0:T(8,128)(2,1)} %bitcast.30), custom_call_target="tpu_custom_call" | custom-call | flops 1 | bytes 1 | tf_op jit(solution)/shard_map/pallas_call | solution.py:96
  3.7 1.9 %collective-permute-start = (bf16[64,64]{1,0:T(8,128)(2,1)}, bf16[64,64]{1,0:T(8,128)(2,1)S(1)}, u32[]{:S(2)}, u32[]{:S(2)}) collective-permute-start(bf16[64,64]{1,0:T(8,128)(2,1)} %shard_map.151), channel_id=1, source_target_pairs={{0,1},{1,0},{2,3},{3,2},{4,5},{5,4},{6,7},{7,6},{8,9},{9,8},{10,11... | collective-permute-start | bytes 24584 | tf_op jit(solution)/shard_map/ppermute | solution.py:39
  5.6 2.0 %shard_map.150.w0 = bf16[256,1280]{1,0:T(8,128)(2,1)} custom-call(bf16[256,1024]{1,0:T(8,128)(2,1)} %q.1, bf16[256,128]{1,0:T(8,128)(2,1)} %k.1, bf16[256,128]{1,0:T(8,128)(2,1)} %v.1), custom_call_target="tpu_custom_call" | custom-call | flops 1 | bytes 1 | tf_op jit(solution)/shard_map/pallas_call | solution.py:79
  8.3 5.6 %collective-permute-start.4 = (bf16[256,1280]{1,0:T(8,128)(2,1)}, bf16[256,1280]{1,0:T(8,128)(2,1)}, u32[]{:S(2)}, u32[]{:S(2)}) collective-permute-start(bf16[256,1280]{1,0:T(8,128)(2,1)} %shard_map.150.w0), channel_id=1, source_target_pairs={{0,48},{8,56},{16,0},{24,8},{32,16},{40,24},{48,32},{56,40},{64,11... | collective-permute-start | bytes 1966088 | tf_op jit(solution)/shard_map/ppermute | solution.py:25
  13.9 3.1 %shard_map.149.d.d0 = bf16[512,1280]{1,0:T(8,128)(2,1)} custom-call(s32[5]{0:T(128)} %stack.23.place, bf16[512,1024]{1,0:T(8,128)(2,1)} %dq.1, bf16[512,128]{1,0:T(8,128)(2,1)} %dk.1, bf16[512,128]{1,0:T(8,128)(2,1)} %dv.1), custom_call_target="tpu_custom_call" | custom-call | flops 1 | bytes 1 | tf_op jit(solution)/shard_map/pallas_call | solution.py:79
  18.0 2.4 %collective-permute-start.3 = (bf16[512,1280]{1,0:T(8,128)(2,1)}, bf16[512,1280]{1,0:T(8,128)(2,1)}, u32[]{:S(2)}, u32[]{:S(2)}) collective-permute-start(bf16[512,1280]{1,0:T(8,128)(2,1)} %shard_map.149.d.d0), channel_id=1, source_target_pairs={{0,64},{8,72},{16,80},{24,88},{32,96},{40,104},{48,112},{56,120},{... | collective-permute-start | bytes 3932168 | tf_op jit(solution)/shard_map/ppermute | solution.py:21
  20.4 1.3 copy-done.1
  21.7 1.1 shard_map.152
  23.6 4.9 %all-to-all-start = ((bf16[4,128,192]{1,2,0:T(8,128)(2,1)}), bf16[4,128,192]{1,2,0:T(8,128)(2,1)}, u32[]{:S(2)}, u32[]{:S(2)}) async-start(bf16[4,128,192]{1,2,0:T(8,128)(2,1)} %copy.16), calls=%async_computation | async-start | bytes 393216 | tf_op jit(solution)/shard_map/all_to_all | solution.py:325
  29.9 3.6 %all-to-all-done = bf16[4,128,192]{1,2,0:T(8,128)(2,1)} async-done(((bf16[4,128,192]{1,2,0:T(8,128)(2,1)}), bf16[4,128,192]{1,2,0:T(8,128)(2,1)}, u32[]{:S(2)}, u32[]{:S(2)}) %all-to-all-start) | async-done | bytes 196640 | tf_op jit(solution)/shard_map/all_to_all | solution.py:325
  34.5 1.2 shard_map.153
  35.7 4.7 %all-to-all-start.1 = ((bf16[4,96,128]{2,1,0:T(8,128)(2,1)}), bf16[4,96,128]{2,1,0:T(8,128)(2,1)S(1)}, u32[]{:S(2)}, u32[]{:S(2)}) async-start(bf16[4,96,128]{2,1,0:T(8,128)(2,1)} %shard_map.153), calls=%async_computation.1 | async-start | bytes 196608 | tf_op jit(solution)/shard_map/all_to_all | solution.py:328
  40.5 4.3 %all-to-all-done.1 = bf16[4,96,128]{2,1,0:T(8,128)(2,1)S(1)} async-done(((bf16[4,96,128]{2,1,0:T(8,128)(2,1)}), bf16[4,96,128]{2,1,0:T(8,128)(2,1)S(1)}, u32[]{:S(2)}, u32[]{:S(2)}) %all-to-all-start.1) | async-done | bytes 98336 | tf_op jit(solution)/shard_map/all_to_all | solution.py:328
  46.3 2.2 %collective-permute-done.2.d1 = bf16[512,1280]{1,0:T(8,128)(2,1)} collective-permute-done((bf16[512,1280]{1,0:T(8,128)(2,1)}, bf16[512,1280]{1,0:T(8,128)(2,1)}, u32[]{:S(2)}, u32[]{:S(2)}) %collective-permute-start.2) | collective-permute-done | bytes 1310752 | tf_op jit(solution)/shard_map/ppermute | solution.py:21
  49.1 1.4 collective-permute-start.8
  50.5 3.0 %collective-permute-start.9 = (bf16[256,1280]{1,0:T(8,128)(2,1)}, bf16[256,1280]{1,0:T(8,128)(2,1)}, u32[]{:S(2)}, u32[]{:S(2)}) collective-permute-start(bf16[256,1280]{1,0:T(8,128)(2,1)} %shard_map.150.w0), channel_id=1, source_target_pairs={{0,32},{8,40},{16,48},{24,56},{32,0},{40,8},{48,16},{56,24},{64,96... | collective-permute-start | bytes 1966088 | tf_op jit(solution)/shard_map/ppermute | solution.py:25
  53.5 4.9 %shard_map.154 = (bf16[128,2304]{1,0:T(8,128)(2,1)}, bf16[128,2304]{1,0:T(8,128)(2,1)}) custom-call(bf16[512,1280]{1,0:T(8,128)(2,1)} %shard_map.149.d.d0, bf16[512,1280]{1,0:T(8,128)(2,1)} %collective-permute-done.2.d1, bf16[512,1280]{1,0:T(8,128)(2,1)} %collective-permute-done.3.d3, bf16[256,1280]{1,0:T(8,128)(2,1)} %shard_map.150.w0, ...), custom_call_target="tpu_custom_call" | custom-call | flops 1 | bytes 1 | tf_op jit(solution)/shard_map/pallas_call | solution.py:189
  58.5 1.6 collective-permute-start.10
  61.5 9.2 %shard_map.155 = (bf16[2,128,2304]{2,1,0:T(8,128)(2,1)S(1)}, bf16[2,128,2304]{2,1,0:T(8,128)(2,1)}, bf16[2,128,2304]{2,1,0:T(8,128)(2,1)}) custom-call(bf16[512,1280]{1,0:T(8,128)(2,1)} %shard_map.149.d.d0, bf16[512,1280]{1,0:T(8,128)(2,1)} %collective-permute-done.2.d1, bf16[512,1280]{1,0:T(8,128)(2,1)} %collective-permute-done.3.d3, ...), custom_call_target="tpu_custom_call" | custom-call | flops 1 | bytes 1 | tf_op jit(solution)/shard_map/pallas_call | solution.py:96
  70.7 1.6 %collective-permute-done.10.far_up = bf16[128,2304]{1,0:T(8,128)(2,1)S(1)} collective-permute-done((bf16[128,2304]{1,0:T(8,128)(2,1)}, bf16[128,2304]{1,0:T(8,128)(2,1)S(1)}, u32[]{:S(2)}, u32[]{:S(2)}) %collective-permute-start.10) | collective-permute-done | bytes 589856 | tf_op jit(solution)/shard_map/ppermute | solution.py:35
  72.6 1.3 copy-done.6
  73.9 1.6 %shard_map.156 = (bf16[2,128,2304]{2,1,0:T(8,128)(2,1)}, bf16[2,128,2304]{2,1,0:T(8,128)(2,1)}) custom-call(bf16[128,2304]{1,0:T(8,128)(2,1)S(1)} %collective-permute-done.10.far_up, bf16[128,2304]{1,0:T(8,128)(2,1)S(1)} %collective-permute-done.11.far_down, bf16[2,128,2304]{2,1,0:T(8,128)(2,1)S(1)} %get-tuple-element.73.one, bf16[2,128,2304]{2,1,0:T(8,128)(2,1)S(1)} %copy-done.6), custom_call_target="tpu_custom_call" | custom-call | flops 1 | bytes 1 | tf_op jit(solution)/shard_map/pallas_call | solution.py:96
  75.5 1.8 %collective-permute-start.15 = (bf16[2,128,2304]{2,1,0:T(8,128)(2,1)}, bf16[2,128,2304]{2,1,0:T(8,128)(2,1)}, u32[]{:S(2)}, u32[]{:S(2)}) collective-permute-start(bf16[2,128,2304]{2,1,0:T(8,128)(2,1)} %get-tuple-element.75), channel_id=1, source_target_pairs={{0,2},{1,3},{2,4},{3,5},{4,6},{5,7},{6,0},{7,1},{8,10},{9,11},{10,... | collective-permute-start | bytes 3538952 | tf_op jit(solution)/shard_map/ppermute | solution.py:35
  77.9 7.6 %collective-permute-done.9.w2 = bf16[256,1280]{1,0:T(8,128)(2,1)} collective-permute-done((bf16[256,1280]{1,0:T(8,128)(2,1)}, bf16[256,1280]{1,0:T(8,128)(2,1)}, u32[]{:S(2)}, u32[]{:S(2)}) %collective-permute-start.9) | collective-permute-done | bytes 655392 | tf_op jit(solution)/shard_map/ppermute | solution.py:25
  86.4 4.1 %all-to-all-start.2 = ((bf16[8,2,96,128]{3,2,1,0:T(8,128)(2,1)}), bf16[8,2,96,128]{3,2,1,0:T(8,128)(2,1)S(1)}, u32[]{:S(2)}, u32[]{:S(2)}) async-start(bf16[8,2,96,128]{3,2,1,0:T(8,128)(2,1)} %broadcast_in_dim.4), calls=%async_computation.2 | async-start | bytes 786432 | tf_op jit(solution)/shard_map/all_to_all | solution.py:280
  90.6 1.1 copy-done.3
  91.6 10.5 %shard_map.157 = (bf16[128,1792]{1,0:T(8,128)(2,1)}, bf16[128,1792]{1,0:T(8,128)(2,1)}, bf16[2,128,1792]{2,1,0:T(8,128)(2,1)}, bf16[2,128,1792]{2,1,0:T(8,128)(2,1)}, bf16[2,128,1792]{2,1,0:T(8,128)(2,1)}) custom-call(bf16[512,1280]{1,0:T(8,128)(2,1)} %shard_map.149.d.d0, bf16[512,1280]{1,0:T(8,128)(2,1)} %collective-permute-done.2.d1, ...), custom_call_target="tpu_custom_call" | custom-call | flops 1 | bytes 1 | tf_op jit(solution)/shard_map/pallas_call | solution.py:96
  102.1 1.8 %collective-permute-start.13 = (bf16[128,1792]{1,0:T(8,128)(2,1)}, bf16[128,1792]{1,0:T(8,128)(2,1)}, u32[]{:S(2)}, u32[]{:S(2)}) collective-permute-start(bf16[128,1792]{1,0:T(8,128)(2,1)} %get-tuple-element.80), channel_id=1, source_target_pairs={{0,2},{1,3},{2,4},{3,5},{4,6},{5,7},{6,0},{7,1},{8,10},{9,11},{10,... | collective-permute-start | bytes 1376264 | tf_op jit(solution)/shard_map/ppermute | solution.py:35
  104.2 1.9 %all-to-all-done.2 = bf16[8,2,96,128]{3,2,1,0:T(8,128)(2,1)S(1)} async-done(((bf16[8,2,96,128]{3,2,1,0:T(8,128)(2,1)}), bf16[8,2,96,128]{3,2,1,0:T(8,128)(2,1)S(1)}, u32[]{:S(2)}, u32[]{:S(2)}) %all-to-all-start.2) | async-done | bytes 393248 | tf_op jit(solution)/shard_map/all_to_all | solution.py:280
  106.1 1.4 broadcast_in_dim.5
  107.5 6.4 %all-to-all-start.3 = ((bf16[4,16,96,128]{3,2,1,0:T(8,128)(2,1)}), bf16[4,16,96,128]{3,2,1,0:T(8,128)(2,1)}, u32[]{:S(2)}, u32[]{:S(2)}) async-start(bf16[4,16,96,128]{3,2,1,0:T(8,128)(2,1)} %broadcast_in_dim.5), calls=%async_computation.3 | async-start | bytes 3145728 | tf_op jit(solution)/shard_map/all_to_all | solution.py:280
  113.9 1.3 copy-done.5
  115.2 2.2 %shard_map.158 = (bf16[2,64,2304]{2,1,0:T(8,128)(2,1)S(1)}, bf16[2,64,2304]{2,1,0:T(8,128)(2,1)S(1)}) custom-call(bf16[2,128,2304]{2,1,0:T(8,128)(2,1)S(1)} %copy-done.5, bf16[2,128,2304]{2,1,0:T(8,128)(2,1)} %collective-permute-done.15.up, bf16[2,128,2304]{2,1,0:T(8,128)(2,1)} %collective-permute-done.16.down), custom_call_target="tpu_custom_call" | custom-call | flops 1 | bytes 1 | tf_op jit(solution)/shard_map/pallas_call | solution.py:96
  117.3 1.1 collective-permute-start.21
  118.4 1.5 shard_map.159
  119.9 1.6 %collective-permute-start.19 = (bf16[2,128,1024]{2,1,0:T(8,128)(2,1)S(1)}, bf16[2,128,1024]{2,1,0:T(8,128)(2,1)S(1)}, u32[]{:S(2)}, u32[]{:S(2)}) collective-permute-start(bf16[2,128,1024]{2,1,0:T(8,128)(2,1)S(1)} %get-tuple-element.90), channel_id=1, source_target_pairs={{0,2},{1,3},{2,4},{3,5},{4,6},{5,7},{6,0},{7,1},{8,10},{9,11},{10,... | collective-permute-start | bytes 1572872 | tf_op jit(solution)/shard_map/ppermute | solution.py:35
  122.0 1.6 collective-permute-start.17
  124.1 6.7 %collective-permute-done.21.got = bf16[2,64,2304]{2,1,0:T(8,128)(2,1)S(1)} collective-permute-done((bf16[2,64,2304]{2,1,0:T(8,128)(2,1)S(1)}, bf16[2,64,2304]{2,1,0:T(8,128)(2,1)S(1)}, u32[]{:S(2)}, u32[]{:S(2)}) %collective-permute-start.21) | collective-permute-done | bytes 589856 | tf_op jit(solution)/shard_map/ppermute | solution.py:39
  131.5 3.3 %collective-permute-done.19.up = bf16[2,128,1024]{2,1,0:T(8,128)(2,1)S(1)} collective-permute-done((bf16[2,128,1024]{2,1,0:T(8,128)(2,1)S(1)}, bf16[2,128,1024]{2,1,0:T(8,128)(2,1)S(1)}, u32[]{:S(2)}, u32[]{:S(2)}) %collective-permute-start.19) | collective-permute-done | bytes 524320 | tf_op jit(solution)/shard_map/ppermute | solution.py:35
  134.9 1.6 collective-permute-done.20.down
  137.7 1.9 %collective-permute-start.25 = (bf16[2,64,768]{2,1,0:T(8,128)(2,1)}, bf16[2,64,768]{2,1,0:T(8,128)(2,1)}, u32[]{:S(2)}, u32[]{:S(2)}) collective-permute-start(bf16[2,64,768]{2,1,0:T(8,128)(2,1)} %get-tuple-element.106), channel_id=1, source_target_pairs={{0,192},{8,200},{16,208},{24,216},{32,224},{40,232},{48,240},{56,2... | collective-permute-start | bytes 589832 | tf_op jit(solution)/shard_map/ppermute | solution.py:21
  142.0 1.2 collective-permute-start.26
  143.2 1.7 %collective-permute-done.23.got = bf16[2,64,1024]{2,1,0:T(8,128)(2,1)S(1)} collective-permute-done((bf16[2,64,1024]{2,1,0:T(8,128)(2,1)S(1)}, bf16[2,64,1024]{2,1,0:T(8,128)(2,1)S(1)}, u32[]{:S(2)}, u32[]{:S(2)}) %collective-permute-start.23) | collective-permute-done | bytes 262176 | tf_op jit(solution)/shard_map/ppermute | solution.py:39
  145.9 3.3 %fusion = f32[64,128]{1,0:T(8,128)} fusion(bf16[128,12288]{1,0:T(8,128)(2,1)S(1)} %copy-done, bf16[8,8,96,128]{3,2,1,0:T(8,128)(2,1)} %bitcast.18), kind=kOutput, calls=%fused_computation | convolution fusion | flops 201326592 | bytes 4751360 | tf_op jit(solution)/shard_map/dot_general | solution.py:112
  150.8 2.3 %collective-permute-start.27 = (bf16[2,64,256]{2,1,0:T(8,128)(2,1)S(1)}, bf16[2,64,256]{2,1,0:T(8,128)(2,1)S(1)}, u32[]{:S(2)}, u32[]{:S(2)}) collective-permute-start(bf16[2,64,256]{2,1,0:T(8,128)(2,1)S(1)} %get-tuple-element.110), channel_id=1, source_target_pairs={{0,64},{8,72},{16,80},{24,88},{32,96},{40,104},{48,112},{56,120},{... | collective-permute-start | bytes 196616 | tf_op jit(solution)/shard_map/ppermute | solution.py:21
  153.1 2.0 %collective-permute-done.27.f1 = bf16[2,64,256]{2,1,0:T(8,128)(2,1)S(1)} collective-permute-done((bf16[2,64,256]{2,1,0:T(8,128)(2,1)S(1)}, bf16[2,64,256]{2,1,0:T(8,128)(2,1)S(1)}, u32[]{:S(2)}, u32[]{:S(2)}) %collective-permute-start.27) | collective-permute-done | bytes 65568 | tf_op jit(solution)/shard_map/ppermute | solution.py:21
  155.0 3.5 %collective-permute-done.28.f3 = bf16[2,64,256]{2,1,0:T(8,128)(2,1)S(1)} collective-permute-done((bf16[2,64,256]{2,1,0:T(8,128)(2,1)S(1)}, bf16[2,64,256]{2,1,0:T(8,128)(2,1)S(1)}, u32[]{:S(2)}, u32[]{:S(2)}) %collective-permute-start.28) | collective-permute-done | bytes 65568 | tf_op jit(solution)/shard_map/ppermute | solution.py:21
  159.1 3.8 %shard_map.165 = bf16[64,8192]{1,0:T(8,128)(2,1)} custom-call(s32[5]{0:T(128)} %stack.23.place, bf16[64,8192]{1,0:T(8,128)(2,1)} %hidden.3, f32[1,8192]{1,0:T(1,128)} %bitcast.32, bf16[2,64,768]{2,1,0:T(8,128)(2,1)} %copy-done.11, bf16[2,64,768]{2,1,0:T(8,128)(2,1)} %collective-permute-done.24.e1, bf16[2,64,768]{2,1,0:T(8,128)(2,1)} %collective-permute-done.25.e3, ...), custom_call_target="tpu_custom_call" | custom-call | flops 1 | bytes 1 | tf_op jit(solution)/shard_map/pallas_call | solution.py:96
  (90 shorter events, 18.2 us)
Async XLA Ops:
  0.6 145.3 %copy-start = (bf16[128,12288]{1,0:T(8,128)(2,1)S(1)}, bf16[128,12288]{1,0:T(8,128)(2,1)}, u32[]{:S(2)}) copy-start(bf16[128,12288]{1,0:T(8,128)(2,1)} %param.27) | copy-start | bytes 9437188
  3.7 4.6 %collective-permute-start = (bf16[64,64]{1,0:T(8,128)(2,1)}, bf16[64,64]{1,0:T(8,128)(2,1)S(1)}, u32[]{:S(2)}, u32[]{:S(2)}) collective-permute-start(bf16[64,64]{1,0:T(8,128)(2,1)} %shard_map.151), channel_id=1, source_target_pairs={{0,1},{1,0},{2,3},{3,2},{4,5},{5,4},{6,7},{7,6},{8,9},{9,8},{10,11... | collective-permute-start | bytes 24584 | tf_op jit(solution)/shard_map/ppermute | solution.py:39
  8.3 12.0 %copy-start.12 = (bf16[1024,64]{0,1:T(8,128)(2,1)S(1)}, bf16[1024,64]{0,1:T(8,128)(2,1)}, u32[]{:S(2)}) copy-start(bf16[1024,64]{0,1:T(8,128)(2,1)} %param.24) | copy-start | bytes 393220
  8.3 12.0 %copy-start.14 = (bf16[128,64]{0,1:T(8,128)(2,1)S(1)}, bf16[128,64]{0,1:T(8,128)(2,1)}, u32[]{:S(2)}) copy-start(bf16[128,64]{0,1:T(8,128)(2,1)} %param.25) | copy-start | bytes 49156
  8.3 12.0 %copy-start.15 = (bf16[128,64]{0,1:T(8,128)(2,1)S(1)}, bf16[128,64]{0,1:T(8,128)(2,1)}, u32[]{:S(2)}) copy-start(bf16[128,64]{0,1:T(8,128)(2,1)} %param.26) | copy-start | bytes 49156
  8.3 12.0 %copy-start.16 = (s32[5]{0:T(128)S(1)}, s32[5]{0:T(128)}, u32[]{:S(2)}) copy-start(s32[5]{0:T(128)} %stack.23.place) | copy-start | bytes 64
  8.3 36.5 %collective-permute-start.4 = (bf16[256,1280]{1,0:T(8,128)(2,1)}, bf16[256,1280]{1,0:T(8,128)(2,1)}, u32[]{:S(2)}, u32[]{:S(2)}) collective-permute-start(bf16[256,1280]{1,0:T(8,128)(2,1)} %shard_map.150.w0), channel_id=1, source_target_pairs={{0,48},{8,56},{16,0},{24,8},{32,16},{40,24},{48,32},{56,40},{64,11... | collective-permute-start | bytes 1966088 | tf_op jit(solution)/shard_map/ppermute | solution.py:25
  13.9 31.8 %collective-permute-start.5 = (bf16[256,1280]{1,0:T(8,128)(2,1)}, bf16[256,1280]{1,0:T(8,128)(2,1)}, u32[]{:S(2)}, u32[]{:S(2)}) collective-permute-start(bf16[256,1280]{1,0:T(8,128)(2,1)} %shard_map.150.w0), channel_id=1, source_target_pairs={{0,16},{8,24},{16,32},{24,40},{32,48},{40,56},{48,0},{56,8},{64,80... | collective-permute-start | bytes 1966088 | tf_op jit(solution)/shard_map/ppermute | solution.py:25
  17.0 31.4 %collective-permute-start.2 = (bf16[512,1280]{1,0:T(8,128)(2,1)}, bf16[512,1280]{1,0:T(8,128)(2,1)}, u32[]{:S(2)}, u32[]{:S(2)}) collective-permute-start(bf16[512,1280]{1,0:T(8,128)(2,1)} %shard_map.149.d.d0), channel_id=1, source_target_pairs={{0,192},{8,200},{16,208},{24,216},{32,224},{40,232},{48,240},{56,2... | collective-permute-start | bytes 3932168 | tf_op jit(solution)/shard_map/ppermute | solution.py:21
  18.0 30.5 %collective-permute-start.3 = (bf16[512,1280]{1,0:T(8,128)(2,1)}, bf16[512,1280]{1,0:T(8,128)(2,1)}, u32[]{:S(2)}, u32[]{:S(2)}) collective-permute-start(bf16[512,1280]{1,0:T(8,128)(2,1)} %shard_map.149.d.d0), channel_id=1, source_target_pairs={{0,64},{8,72},{16,80},{24,88},{32,96},{40,104},{48,112},{56,120},{... | collective-permute-start | bytes 3932168 | tf_op jit(solution)/shard_map/ppermute | solution.py:21
  21.7 6.8 %copy-start.20 = (s32[2]{0:T(128)S(1)}, s32[2]{0:T(128)}, u32[]{:S(2)}) copy-start(s32[2]{0:T(128)} %param.22) | copy-start | bytes 28
  21.7 8.1 %copy-start.17 = (bf16[64,64]{1,0:T(8,128)(2,1)S(1)}, bf16[64,64]{1,0:T(8,128)(2,1)}, u32[]{:S(2)}) copy-start(bf16[64,64]{1,0:T(8,128)(2,1)} %shard_map.151) | copy-start | bytes 24580
  23.6 9.9 %all-to-all-start = ((bf16[4,128,192]{1,2,0:T(8,128)(2,1)}), bf16[4,128,192]{1,2,0:T(8,128)(2,1)}, u32[]{:S(2)}, u32[]{:S(2)}) async-start(bf16[4,128,192]{1,2,0:T(8,128)(2,1)} %copy.16), calls=%async_computation | async-start | bytes 393216 | tf_op jit(solution)/shard_map/all_to_all | solution.py:325
  35.7 9.1 %all-to-all-start.1 = ((bf16[4,96,128]{2,1,0:T(8,128)(2,1)}), bf16[4,96,128]{2,1,0:T(8,128)(2,1)S(1)}, u32[]{:S(2)}, u32[]{:S(2)}) async-start(bf16[4,96,128]{2,1,0:T(8,128)(2,1)} %shard_map.153), calls=%async_computation.1 | async-start | bytes 196608 | tf_op jit(solution)/shard_map/all_to_all | solution.py:328
  40.5 5.8 %collective-permute-start.1 = (bf16[256,1280]{1,0:T(8,128)(2,1)}, bf16[256,1280]{1,0:T(8,128)(2,1)}, u32[]{:S(2)}, u32[]{:S(2)}) collective-permute-start(bf16[256,1280]{1,0:T(8,128)(2,1)} %shard_map.150.w0), channel_id=1, source_target_pairs={{0,8},{8,0},{16,24},{24,16},{32,40},{40,32},{48,56},{56,48},{64,72... | collective-permute-start | bytes 1966088 | tf_op jit(solution)/shard_map/ppermute | solution.py:31
  44.8 16.7 %copy-start.2 = (bf16[256,1280]{1,0:T(8,128)(2,1)S(1)}, bf16[256,1280]{1,0:T(8,128)(2,1)}, u32[]{:S(2)}) copy-start(bf16[256,1280]{1,0:T(8,128)(2,1)} %shard_map.150.w0) | copy-start | bytes 1966084
  45.8 2.8 %collective-permute-start.6 = (bf16[256,1280]{1,0:T(8,128)(2,1)}, bf16[256,1280]{1,0:T(8,128)(2,1)}, u32[]{:S(2)}, u32[]{:S(2)}) collective-permute-start(bf16[256,1280]{1,0:T(8,128)(2,1)} %collective-permute-done.4.w1), channel_id=1, source_target_pairs={{0,8},{8,0},{16,24},{24,16},{32,40},{40,32},{48,56},{56,48},{64,72... | collective-permute-start | bytes 1966088 | tf_op jit(solution)/shard_map/ppermute | solution.py:31
  45.8 3.4 %collective-permute-start.7 = (bf16[256,1280]{1,0:T(8,128)(2,1)}, bf16[256,1280]{1,0:T(8,128)(2,1)}, u32[]{:S(2)}, u32[]{:S(2)}) collective-permute-start(bf16[256,1280]{1,0:T(8,128)(2,1)} %collective-permute-done.5.w3), channel_id=1, source_target_pairs={{0,8},{8,0},{16,24},{24,16},{32,40},{40,32},{48,56},{56,48},{64,72... | collective-permute-start | bytes 1966088 | tf_op jit(solution)/shard_map/ppermute | solution.py:31
  49.1 36.4 %collective-permute-start.8 = (bf16[512,1280]{1,0:T(8,128)(2,1)}, bf16[512,1280]{1,0:T(8,128)(2,1)}, u32[]{:S(2)}, u32[]{:S(2)}) collective-permute-start(bf16[512,1280]{1,0:T(8,128)(2,1)} %shard_map.149.d.d0), channel_id=1, source_target_pairs={{0,128},{8,136},{16,144},{24,152},{32,160},{40,168},{48,176},{56,1... | collective-permute-start | bytes 3932168 | tf_op jit(solution)/shard_map/ppermute | solution.py:21
  50.5 35.0 %collective-permute-start.9 = (bf16[256,1280]{1,0:T(8,128)(2,1)}, bf16[256,1280]{1,0:T(8,128)(2,1)}, u32[]{:S(2)}, u32[]{:S(2)}) collective-permute-start(bf16[256,1280]{1,0:T(8,128)(2,1)} %shard_map.150.w0), channel_id=1, source_target_pairs={{0,32},{8,40},{16,48},{24,56},{32,0},{40,8},{48,16},{56,24},{64,96... | collective-permute-start | bytes 1966088 | tf_op jit(solution)/shard_map/ppermute | solution.py:25
  58.5 13.9 %collective-permute-start.10 = (bf16[128,2304]{1,0:T(8,128)(2,1)}, bf16[128,2304]{1,0:T(8,128)(2,1)S(1)}, u32[]{:S(2)}, u32[]{:S(2)}) collective-permute-start(bf16[128,2304]{1,0:T(8,128)(2,1)} %get-tuple-element.71), channel_id=1, source_target_pairs={{0,2},{1,3},{2,4},{3,5},{4,6},{5,7},{6,0},{7,1},{8,10},{9,11},{10,... | collective-permute-start | bytes 1769480 | tf_op jit(solution)/shard_map/ppermute | solution.py:35
  60.0 12.6 %collective-permute-start.11 = (bf16[128,2304]{1,0:T(8,128)(2,1)}, bf16[128,2304]{1,0:T(8,128)(2,1)S(1)}, u32[]{:S(2)}, u32[]{:S(2)}) collective-permute-start(bf16[128,2304]{1,0:T(8,128)(2,1)} %get-tuple-element.72), channel_id=1, source_target_pairs={{0,6},{1,7},{2,0},{3,1},{4,2},{5,3},{6,4},{7,5},{8,14},{9,15},{10,... | collective-permute-start | bytes 1769480 | tf_op jit(solution)/shard_map/ppermute | solution.py:35
  60.5 25.1 %collective-permute-start.22 = (f32[2,96,128]{2,1,0:T(8,128)S(1)}, f32[2,96,128]{2,1,0:T(8,128)S(1)}, u32[]{:S(2)}, u32[]{:S(2)}) collective-permute-start(f32[2,96,128]{2,1,0:T(8,128)S(1)} %convert_reduce_fusion), channel_id=1, source_target_pairs={{0,1},{1,0},{2,3},{3,2},{4,5},{5,4},{6,7},{7,6},{8,9},{9,8},{10,11... | collective-permute-start | bytes 294920 | tf_op jit(solution)/shard_map/ppermute | solution.py:39
  75.5 38.4 %collective-permute-start.15 = (bf16[2,128,2304]{2,1,0:T(8,128)(2,1)}, bf16[2,128,2304]{2,1,0:T(8,128)(2,1)}, u32[]{:S(2)}, u32[]{:S(2)}) collective-permute-start(bf16[2,128,2304]{2,1,0:T(8,128)(2,1)} %get-tuple-element.75), channel_id=1, source_target_pairs={{0,2},{1,3},{2,4},{3,5},{4,6},{5,7},{6,0},{7,1},{8,10},{9,11},{10,... | collective-permute-start | bytes 3538952 | tf_op jit(solution)/shard_map/ppermute | solution.py:35
  77.3 36.6 %collective-permute-start.16 = (bf16[2,128,2304]{2,1,0:T(8,128)(2,1)}, bf16[2,128,2304]{2,1,0:T(8,128)(2,1)}, u32[]{:S(2)}, u32[]{:S(2)}) collective-permute-start(bf16[2,128,2304]{2,1,0:T(8,128)(2,1)} %get-tuple-element.76), channel_id=1, source_target_pairs={{0,6},{1,7},{2,0},{3,1},{4,2},{5,3},{6,4},{7,5},{8,14},{9,15},{10,... | collective-permute-start | bytes 3538952 | tf_op jit(solution)/shard_map/ppermute | solution.py:35
  85.6 5.0 %collective-permute-start.12 = (bf16[256,1280]{1,0:T(8,128)(2,1)}, bf16[256,1280]{1,0:T(8,128)(2,1)}, u32[]{:S(2)}, u32[]{:S(2)}) collective-permute-start(bf16[256,1280]{1,0:T(8,128)(2,1)} %collective-permute-done.9.w2), channel_id=1, source_target_pairs={{0,8},{8,0},{16,24},{24,16},{32,40},{40,32},{48,56},{56,48},{64,72... | collective-permute-start | bytes 1966088 | tf_op jit(solution)/shard_map/ppermute | solution.py:31
  86.4 19.7 %all-to-all-start.2 = ((bf16[8,2,96,128]{3,2,1,0:T(8,128)(2,1)}), bf16[8,2,96,128]{3,2,1,0:T(8,128)(2,1)S(1)}, u32[]{:S(2)}, u32[]{:S(2)}) async-start(bf16[8,2,96,128]{3,2,1,0:T(8,128)(2,1)} %broadcast_in_dim.4), calls=%async_computation.2 | async-start | bytes 786432 | tf_op jit(solution)/shard_map/all_to_all | solution.py:280
  102.1 16.3 %collective-permute-start.13 = (bf16[128,1792]{1,0:T(8,128)(2,1)}, bf16[128,1792]{1,0:T(8,128)(2,1)}, u32[]{:S(2)}, u32[]{:S(2)}) collective-permute-start(bf16[128,1792]{1,0:T(8,128)(2,1)} %get-tuple-element.80), channel_id=1, source_target_pairs={{0,2},{1,3},{2,4},{3,5},{4,6},{5,7},{6,0},{7,1},{8,10},{9,11},{10,... | collective-permute-start | bytes 1376264 | tf_op jit(solution)/shard_map/ppermute | solution.py:35
  103.9 14.5 %collective-permute-start.14 = (bf16[128,1792]{1,0:T(8,128)(2,1)}, bf16[128,1792]{1,0:T(8,128)(2,1)}, u32[]{:S(2)}, u32[]{:S(2)}) collective-permute-start(bf16[128,1792]{1,0:T(8,128)(2,1)} %get-tuple-element.81), channel_id=1, source_target_pairs={{0,6},{1,7},{2,0},{3,1},{4,2},{5,3},{6,4},{7,5},{8,14},{9,15},{10,... | collective-permute-start | bytes 1376264 | tf_op jit(solution)/shard_map/ppermute | solution.py:35
  107.5 38.4 %all-to-all-start.3 = ((bf16[4,16,96,128]{3,2,1,0:T(8,128)(2,1)}), bf16[4,16,96,128]{3,2,1,0:T(8,128)(2,1)}, u32[]{:S(2)}, u32[]{:S(2)}) async-start(bf16[4,16,96,128]{3,2,1,0:T(8,128)(2,1)} %broadcast_in_dim.5), calls=%async_computation.3 | async-start | bytes 3145728 | tf_op jit(solution)/shard_map/all_to_all | solution.py:280
  115.2 3.3 %copy-start.7 = (bf16[2,128,1792]{2,1,0:T(8,128)(2,1)S(1)}, bf16[2,128,1792]{2,1,0:T(8,128)(2,1)}, u32[]{:S(2)}) copy-start(bf16[2,128,1792]{2,1,0:T(8,128)(2,1)} %get-tuple-element.86.one) | copy-start | bytes 2752516
  115.2 3.3 %copy-start.8 = (bf16[2,128,1792]{2,1,0:T(8,128)(2,1)S(1)}, bf16[2,128,1792]{2,1,0:T(8,128)(2,1)}, u32[]{:S(2)}) copy-start(bf16[2,128,1792]{2,1,0:T(8,128)(2,1)} %get-tuple-element.87.three) | copy-start | bytes 2752516
  117.3 13.4 %collective-permute-start.21 = (bf16[2,64,2304]{2,1,0:T(8,128)(2,1)S(1)}, bf16[2,64,2304]{2,1,0:T(8,128)(2,1)S(1)}, u32[]{:S(2)}, u32[]{:S(2)}) collective-permute-start(bf16[2,64,2304]{2,1,0:T(8,128)(2,1)S(1)} %get-tuple-element.83), channel_id=1, source_target_pairs={{0,1},{1,0},{2,3},{3,2},{4,5},{5,4},{6,7},{7,6},{8,9},{9,8},{10,11... | collective-permute-start | bytes 1769480 | tf_op jit(solution)/shard_map/ppermute | solution.py:39
  118.4 18.0 %copy-start.4 = (bf16[2,128,1792]{2,1,0:T(8,128)(2,1)S(1)}, bf16[2,128,1792]{2,1,0:T(8,128)(2,1)}, u32[]{:S(2)}) copy-start(bf16[2,128,1792]{2,1,0:T(8,128)(2,1)} %get-tuple-element.79.own) | copy-start | bytes 2752516
  119.9 14.9 %collective-permute-start.19 = (bf16[2,128,1024]{2,1,0:T(8,128)(2,1)S(1)}, bf16[2,128,1024]{2,1,0:T(8,128)(2,1)S(1)}, u32[]{:S(2)}, u32[]{:S(2)}) collective-permute-start(bf16[2,128,1024]{2,1,0:T(8,128)(2,1)S(1)} %get-tuple-element.90), channel_id=1, source_target_pairs={{0,2},{1,3},{2,4},{3,5},{4,6},{5,7},{6,0},{7,1},{8,10},{9,11},{10,... | collective-permute-start | bytes 1572872 | tf_op jit(solution)/shard_map/ppermute | solution.py:35
  121.6 14.9 %collective-permute-start.20 = (bf16[2,128,1024]{2,1,0:T(8,128)(2,1)S(1)}, bf16[2,128,1024]{2,1,0:T(8,128)(2,1)S(1)}, u32[]{:S(2)}, u32[]{:S(2)}) collective-permute-start(bf16[2,128,1024]{2,1,0:T(8,128)(2,1)S(1)} %get-tuple-element.91), channel_id=1, source_target_pairs={{0,6},{1,7},{2,0},{3,1},{4,2},{5,3},{6,4},{7,5},{8,14},{9,15},{10,... | collective-permute-start | bytes 1572872 | tf_op jit(solution)/shard_map/ppermute | solution.py:35
  122.0 18.3 %collective-permute-start.17 = (bf16[2,128,768]{2,1,0:T(8,128)(2,1)S(1)}, bf16[2,128,768]{2,1,0:T(8,128)(2,1)S(1)}, u32[]{:S(2)}, u32[]{:S(2)}) collective-permute-start(bf16[2,128,768]{2,1,0:T(8,128)(2,1)S(1)} %get-tuple-element.88), channel_id=1, source_target_pairs={{0,2},{1,3},{2,4},{3,5},{4,6},{5,7},{6,0},{7,1},{8,10},{9,11},{10,... | collective-permute-start | bytes 1179656 | tf_op jit(solution)/shard_map/ppermute | solution.py:35
  123.6 17.6 %collective-permute-start.18 = (bf16[2,128,768]{2,1,0:T(8,128)(2,1)S(1)}, bf16[2,128,768]{2,1,0:T(8,128)(2,1)S(1)}, u32[]{:S(2)}, u32[]{:S(2)}) collective-permute-start(bf16[2,128,768]{2,1,0:T(8,128)(2,1)S(1)} %get-tuple-element.89), channel_id=1, source_target_pairs={{0,6},{1,7},{2,0},{3,1},{4,2},{5,3},{6,4},{7,5},{8,14},{9,15},{10,... | collective-permute-start | bytes 1179656 | tf_op jit(solution)/shard_map/ppermute | solution.py:35
  131.5 10.4 %copy-start.11 = (bf16[2,64,768]{2,1,0:T(8,128)(2,1)}, bf16[2,64,768]{2,1,0:T(8,128)(2,1)S(1)}, u32[]{:S(2)}) copy-start(bf16[2,64,768]{2,1,0:T(8,128)(2,1)S(1)} %get-tuple-element.105.e0) | copy-start | bytes 589828
  136.6 8.3 %collective-permute-start.23 = (bf16[2,64,1024]{2,1,0:T(8,128)(2,1)S(1)}, bf16[2,64,1024]{2,1,0:T(8,128)(2,1)S(1)}, u32[]{:S(2)}, u32[]{:S(2)}) collective-permute-start(bf16[2,64,1024]{2,1,0:T(8,128)(2,1)S(1)} %get-tuple-element.96), channel_id=1, source_target_pairs={{0,1},{1,0},{2,3},{3,2},{4,5},{5,4},{6,7},{7,6},{8,9},{9,8},{10,11... | collective-permute-start | bytes 786440 | tf_op jit(solution)/shard_map/ppermute | solution.py:39
  137.6 15.4 %collective-permute-start.24 = (bf16[2,64,768]{2,1,0:T(8,128)(2,1)}, bf16[2,64,768]{2,1,0:T(8,128)(2,1)}, u32[]{:S(2)}, u32[]{:S(2)}) collective-permute-start(bf16[2,64,768]{2,1,0:T(8,128)(2,1)} %get-tuple-element.93), channel_id=1, source_target_pairs={{0,64},{8,72},{16,80},{24,88},{32,96},{40,104},{48,112},{56,120},{... | collective-permute-start | bytes 589832 | tf_op jit(solution)/shard_map/ppermute | solution.py:21
  137.7 15.3 %collective-permute-start.25 = (bf16[2,64,768]{2,1,0:T(8,128)(2,1)}, bf16[2,64,768]{2,1,0:T(8,128)(2,1)}, u32[]{:S(2)}, u32[]{:S(2)}) collective-permute-start(bf16[2,64,768]{2,1,0:T(8,128)(2,1)} %get-tuple-element.106), channel_id=1, source_target_pairs={{0,192},{8,200},{16,208},{24,216},{32,224},{40,232},{48,240},{56,2... | collective-permute-start | bytes 589832 | tf_op jit(solution)/shard_map/ppermute | solution.py:21
  142.0 7.2 %collective-permute-start.26 = (bf16[2,64,768]{2,1,0:T(8,128)(2,1)}, bf16[2,64,768]{2,1,0:T(8,128)(2,1)}, u32[]{:S(2)}, u32[]{:S(2)}) collective-permute-start(bf16[2,64,768]{2,1,0:T(8,128)(2,1)} %get-tuple-element.108), channel_id=1, source_target_pairs={{0,1},{1,0},{2,3},{3,2},{4,5},{5,4},{6,7},{7,6},{8,9},{9,8},{10,11... | collective-permute-start | bytes 589832 | tf_op jit(solution)/shard_map/ppermute | solution.py:39
  145.0 13.5 %collective-permute-start.29 = (bf16[2,64,1024]{2,1,0:T(8,128)(2,1)S(1)}, bf16[2,64,1024]{2,1,0:T(8,128)(2,1)}, u32[]{:S(2)}, u32[]{:S(2)}) collective-permute-start(bf16[2,64,1024]{2,1,0:T(8,128)(2,1)S(1)} %shard_map.163), channel_id=1, source_target_pairs={{0,128},{8,136},{16,144},{24,152},{32,160},{40,168},{48,176},{56,1... | collective-permute-start | bytes 786440 | tf_op jit(solution)/shard_map/ppermute | solution.py:21
  145.9 3.3 %copy-start.10 = (bf16[2,64,768]{2,1,0:T(8,128)(2,1)S(1)}, bf16[2,64,768]{2,1,0:T(8,128)(2,1)}, u32[]{:S(2)}) copy-start(bf16[2,64,768]{2,1,0:T(8,128)(2,1)} %copy-done.9) | copy-start | bytes 589828
  150.8 4.3 %collective-permute-start.27 = (bf16[2,64,256]{2,1,0:T(8,128)(2,1)S(1)}, bf16[2,64,256]{2,1,0:T(8,128)(2,1)S(1)}, u32[]{:S(2)}, u32[]{:S(2)}) collective-permute-start(bf16[2,64,256]{2,1,0:T(8,128)(2,1)S(1)} %get-tuple-element.110), channel_id=1, source_target_pairs={{0,64},{8,72},{16,80},{24,88},{32,96},{40,104},{48,112},{56,120},{... | collective-permute-start | bytes 196616 | tf_op jit(solution)/shard_map/ppermute | solution.py:21
  153.0 5.5 %collective-permute-start.28 = (bf16[2,64,256]{2,1,0:T(8,128)(2,1)S(1)}, bf16[2,64,256]{2,1,0:T(8,128)(2,1)S(1)}, u32[]{:S(2)}, u32[]{:S(2)}) collective-permute-start(bf16[2,64,256]{2,1,0:T(8,128)(2,1)S(1)} %get-tuple-element.111), channel_id=1, source_target_pairs={{0,192},{8,200},{16,208},{24,216},{32,224},{40,232},{48,240},{56,2... | collective-permute-start | bytes 196616 | tf_op jit(solution)/shard_map/ppermute | solution.py:21
  155.0 3.5 %copy-start.18 = (bf16[2,64,256]{2,1,0:T(8,128)(2,1)}, bf16[2,64,256]{2,1,0:T(8,128)(2,1)S(1)}, u32[]{:S(2)}) copy-start(bf16[2,64,256]{2,1,0:T(8,128)(2,1)S(1)} %collective-permute-done.27.f1) | copy-start | bytes 196612
  (7 other events, 9.2 us)

commit v4 on v3

--- a/solution.py
+++ b/solution.py
@@ -11,6 +11,7 @@
 BF = jnp.bfloat16
 F32 = jnp.float32
 VMEM_LIMIT = 48 * 1024 * 1024
+VMEM_LOW = 16 * 1024 * 1024
 VMEM_ALL = 60 * 1024 * 1024
 
 NX, NZ, NC, NY, NL = 4, 4, 2, 4, 2
@@ -345,6 +346,7 @@
         [shape(2, 128, COLS1)] * 3,
         [d0, d1, d3, w0, o0, w1, o1, w3, o3],
         [pltpu.VMEM((1152, 1280), BF)],
+        vmem_limit=VMEM_LOW,
     )
     steps = shape(2, 128, COLS1)
     up, down = call(second_kernel, [steps] * 2, [far0, far1, one, three])
@@ -360,6 +362,7 @@
         [shape(128, COLS2)] * 2 + [steps] * 3,
         [d0, d1, d3, d2, w0, o0, w1, o1, w3, o3, w2, o2],
         [pltpu.VMEM((1536, 1280), BF)],
+        vmem_limit=VMEM_ALL,
     )
     grads, _ = lax.optimization_barrier((grads, far1))
     grads = to_all(grads, [[x * 8 + i for x in range(4)] for i in range(8)])

time: 164 us -> 164 us (level)
  transfers between devices with their start and end apart: 34 -> 34, of which waited for: 17 -> 17; matrix products, arithmetic and copies ran while one was open for 5% -> 5% of each run, Pallas kernels for 25% -> 23%
where the time goes in v4:
time: 164 us
  starting transfers between devices  57.1 us (35%)
  Pallas kernels  45.3 us (28%)
  waiting for transfers between devices  44.8 us (27%)
  local copies, waits for them, and re-layouts  11.5 us (7%)
  matrix products  3.26 us (2%)
    pallas_call x14, Pallas kernels, call(): pl.pallas_call(kernel, in_specs=[pl.BlockSpec(memory_space=pltpu.SMEM)] *...  35.3 us
    ppermute x10, starting transfers between devices, along_y(): lax.ppermute(v, 'tensor', [(t, (t // 2 + step) % NY * 2 + t % 2) for t in...  10.8 us
    all_to_all x2, starting transfers between devices, to_all(): v = lax.all_to_all(copies, 'dp', 0, 0, axis_index_groups=groups)  10.8 us
    ppermute x8, starting transfers between devices, along_x(): lax.ppermute(v, 'dp', [(i, (i // 8 + step) % NX * 8 + i % 8) for i in ran...  10.3 us
    ppermute x3, waiting for transfers between devices, along_z(): lax.ppermute(v, 'dp', [(i, i // 8 * 8 + (i // 2 + step) % NZ * 2 + i % 2)...  9.52 us
    ppermute x3, starting transfers between devices, along_z(): lax.ppermute(v, 'dp', [(i, i // 8 * 8 + (i // 2 + step) % NZ * 2 + i % 2)...  8.68 us
    ppermute x5, waiting for transfers between devices, swap_l(): return lax.ppermute(v, 'tensor', [(t, t ^ 1) for t in range(8)])  8.49 us
    ppermute x8, waiting for transfers between devices, along_x(): lax.ppermute(v, 'dp', [(i, (i // 8 + step) % NX * 8 + i % 8) for i in ran...  7.7 us
  transfers between devices with their start and end apart: 34, of which 17 were waited for; matrix products, arithmetic and copies ran while one was open for 5% of the time, Pallas kernels for 23%

profile of v4, /device:TPU:14, one launch (start us, length us, event | category | flops | bytes accessed | tf_op | source)
XLA Modules:
  0.0 163.6 jit_solution(12744041651828377005)
XLA Ops:
  0.6 3.0 %shard_map.151 = bf16[64,64]{1,0:T(8,128)(2,1)} custom-call(bf16[64,8192]{1,0:T(8,128)(2,1)} %hidden.3, f32[1,8192]{1,0:T(1,128)} %bitcast.31, bf16[64,8192]{1,0:T(8,128)(2,1)} %bitcast.30), custom_call_target="tpu_custom_call" | custom-call | flops 1 | bytes 1 | tf_op jit(solution)/shard_map/pallas_call | solution.py:97
  3.7 1.9 %collective-permute-start = (bf16[64,64]{1,0:T(8,128)(2,1)}, bf16[64,64]{1,0:T(8,128)(2,1)S(1)}, u32[]{:S(2)}, u32[]{:S(2)}) collective-permute-start(bf16[64,64]{1,0:T(8,128)(2,1)} %shard_map.151), channel_id=1, source_target_pairs={{0,1},{1,0},{2,3},{3,2},{4,5},{5,4},{6,7},{7,6},{8,9},{9,8},{10,11... | collective-permute-start | bytes 24584 | tf_op jit(solution)/shard_map/ppermute | solution.py:40
  5.6 2.0 %shard_map.150.w0 = bf16[256,1280]{1,0:T(8,128)(2,1)} custom-call(bf16[256,1024]{1,0:T(8,128)(2,1)} %q.1, bf16[256,128]{1,0:T(8,128)(2,1)} %k.1, bf16[256,128]{1,0:T(8,128)(2,1)} %v.1), custom_call_target="tpu_custom_call" | custom-call | flops 1 | bytes 1 | tf_op jit(solution)/shard_map/pallas_call | solution.py:80
  8.3 5.7 %collective-permute-start.4 = (bf16[256,1280]{1,0:T(8,128)(2,1)}, bf16[256,1280]{1,0:T(8,128)(2,1)}, u32[]{:S(2)}, u32[]{:S(2)}) collective-permute-start(bf16[256,1280]{1,0:T(8,128)(2,1)} %shard_map.150.w0), channel_id=1, source_target_pairs={{0,48},{8,56},{16,0},{24,8},{32,16},{40,24},{48,32},{56,40},{64,11... | collective-permute-start | bytes 1966088 | tf_op jit(solution)/shard_map/ppermute | solution.py:26
  13.9 3.1 %shard_map.149.d.d0 = bf16[512,1280]{1,0:T(8,128)(2,1)} custom-call(s32[5]{0:T(128)} %stack.23.place, bf16[512,1024]{1,0:T(8,128)(2,1)} %dq.1, bf16[512,128]{1,0:T(8,128)(2,1)} %dk.1, bf16[512,128]{1,0:T(8,128)(2,1)} %dv.1), custom_call_target="tpu_custom_call" | custom-call | flops 1 | bytes 1 | tf_op jit(solution)/shard_map/pallas_call | solution.py:80
  18.0 2.4 %collective-permute-start.3 = (bf16[512,1280]{1,0:T(8,128)(2,1)}, bf16[512,1280]{1,0:T(8,128)(2,1)}, u32[]{:S(2)}, u32[]{:S(2)}) collective-permute-start(bf16[512,1280]{1,0:T(8,128)(2,1)} %shard_map.149.d.d0), channel_id=1, source_target_pairs={{0,64},{8,72},{16,80},{24,88},{32,96},{40,104},{48,112},{56,120},{... | collective-permute-start | bytes 3932168 | tf_op jit(solution)/shard_map/ppermute | solution.py:22
  20.4 1.3 copy-done.1
  21.7 1.1 shard_map.152
  23.6 4.9 %all-to-all-start = ((bf16[4,128,192]{1,2,0:T(8,128)(2,1)}), bf16[4,128,192]{1,2,0:T(8,128)(2,1)}, u32[]{:S(2)}, u32[]{:S(2)}) async-start(bf16[4,128,192]{1,2,0:T(8,128)(2,1)} %copy.16), calls=%async_computation | async-start | bytes 393216 | tf_op jit(solution)/shard_map/all_to_all | solution.py:326
  29.8 3.7 %all-to-all-done = bf16[4,128,192]{1,2,0:T(8,128)(2,1)} async-done(((bf16[4,128,192]{1,2,0:T(8,128)(2,1)}), bf16[4,128,192]{1,2,0:T(8,128)(2,1)}, u32[]{:S(2)}, u32[]{:S(2)}) %all-to-all-start) | async-done | bytes 196640 | tf_op jit(solution)/shard_map/all_to_all | solution.py:326
  33.5 1.1 copy.17
  34.6 1.2 shard_map.153
  35.7 4.7 %all-to-all-start.1 = ((bf16[4,96,128]{2,1,0:T(8,128)(2,1)}), bf16[4,96,128]{2,1,0:T(8,128)(2,1)S(1)}, u32[]{:S(2)}, u32[]{:S(2)}) async-start(bf16[4,96,128]{2,1,0:T(8,128)(2,1)} %shard_map.153), calls=%async_computation.1 | async-start | bytes 196608 | tf_op jit(solution)/shard_map/all_to_all | solution.py:329
  40.5 4.3 %all-to-all-done.1 = bf16[4,96,128]{2,1,0:T(8,128)(2,1)S(1)} async-done(((bf16[4,96,128]{2,1,0:T(8,128)(2,1)}), bf16[4,96,128]{2,1,0:T(8,128)(2,1)S(1)}, u32[]{:S(2)}, u32[]{:S(2)}) %all-to-all-start.1) | async-done | bytes 98336 | tf_op jit(solution)/shard_map/all_to_all | solution.py:329
  46.2 2.2 %collective-permute-done.2.d1 = bf16[512,1280]{1,0:T(8,128)(2,1)} collective-permute-done((bf16[512,1280]{1,0:T(8,128)(2,1)}, bf16[512,1280]{1,0:T(8,128)(2,1)}, u32[]{:S(2)}, u32[]{:S(2)}) %collective-permute-start.2) | collective-permute-done | bytes 1310752 | tf_op jit(solution)/shard_map/ppermute | solution.py:22
  49.0 1.4 collective-permute-start.8
  50.5 3.0 %collective-permute-start.9 = (bf16[256,1280]{1,0:T(8,128)(2,1)}, bf16[256,1280]{1,0:T(8,128)(2,1)}, u32[]{:S(2)}, u32[]{:S(2)}) collective-permute-start(bf16[256,1280]{1,0:T(8,128)(2,1)} %shard_map.150.w0), channel_id=1, source_target_pairs={{0,32},{8,40},{16,48},{24,56},{32,0},{40,8},{48,16},{56,24},{64,96... | collective-permute-start | bytes 1966088 | tf_op jit(solution)/shard_map/ppermute | solution.py:26
  53.5 4.9 %shard_map.154 = (bf16[128,2304]{1,0:T(8,128)(2,1)}, bf16[128,2304]{1,0:T(8,128)(2,1)}) custom-call(bf16[512,1280]{1,0:T(8,128)(2,1)} %shard_map.149.d.d0, bf16[512,1280]{1,0:T(8,128)(2,1)} %collective-permute-done.2.d1, bf16[512,1280]{1,0:T(8,128)(2,1)} %collective-permute-done.3.d3, bf16[256,1280]{1,0:T(8,128)(2,1)} %shard_map.150.w0, ...), custom_call_target="tpu_custom_call" | custom-call | flops 1 | bytes 1 | tf_op jit(solution)/shard_map/pallas_call | solution.py:190
  58.4 1.6 collective-permute-start.10
  61.4 1.3 copy-done.2
  62.7 7.4 %shard_map.155 = (bf16[2,128,2304]{2,1,0:T(8,128)(2,1)S(1)}, bf16[2,128,2304]{2,1,0:T(8,128)(2,1)S(1)}, bf16[2,128,2304]{2,1,0:T(8,128)(2,1)S(1)}) custom-call(bf16[512,1280]{1,0:T(8,128)(2,1)S(1)} %copy-done.2, bf16[512,1280]{1,0:T(8,128)(2,1)} %collective-permute-done.2.d1, bf16[512,1280]{1,0:T(8,128)(2,1)} %collective-permute-done.3.d3, ...), custom_call_target="tpu_custom_call" | custom-call | flops 1 | bytes 1 | tf_op jit(solution)/shard_map/pallas_call | solution.py:97
  71.2 1.2 collective-permute-done.10.far_up
  72.4 1.6 %shard_map.156 = (bf16[2,128,2304]{2,1,0:T(8,128)(2,1)}, bf16[2,128,2304]{2,1,0:T(8,128)(2,1)}) custom-call(bf16[128,2304]{1,0:T(8,128)(2,1)S(1)} %collective-permute-done.10.far_up, bf16[128,2304]{1,0:T(8,128)(2,1)S(1)} %collective-permute-done.11.far_down, bf16[2,128,2304]{2,1,0:T(8,128)(2,1)S(1)} %get-tuple-element.73.one, ...), custom_call_target="tpu_custom_call" | custom-call | flops 1 | bytes 1 | tf_op jit(solution)/shard_map/pallas_call | solution.py:97
  74.1 2.0 %collective-permute-start.15 = (bf16[2,128,2304]{2,1,0:T(8,128)(2,1)}, bf16[2,128,2304]{2,1,0:T(8,128)(2,1)}, u32[]{:S(2)}, u32[]{:S(2)}) collective-permute-start(bf16[2,128,2304]{2,1,0:T(8,128)(2,1)} %get-tuple-element.75), channel_id=1, source_target_pairs={{0,2},{1,3},{2,4},{3,5},{4,6},{5,7},{6,0},{7,1},{8,10},{9,11},{10,... | collective-permute-start | bytes 3538952 | tf_op jit(solution)/shard_map/ppermute | solution.py:36
  76.7 8.7 %collective-permute-done.9.w2 = bf16[256,1280]{1,0:T(8,128)(2,1)} collective-permute-done((bf16[256,1280]{1,0:T(8,128)(2,1)}, bf16[256,1280]{1,0:T(8,128)(2,1)}, u32[]{:S(2)}, u32[]{:S(2)}) %collective-permute-start.9) | collective-permute-done | bytes 655392 | tf_op jit(solution)/shard_map/ppermute | solution.py:26
  86.2 4.5 %all-to-all-start.2 = ((bf16[8,2,96,128]{3,2,1,0:T(8,128)(2,1)}), bf16[8,2,96,128]{3,2,1,0:T(8,128)(2,1)S(1)}, u32[]{:S(2)}, u32[]{:S(2)}) async-start(bf16[8,2,96,128]{3,2,1,0:T(8,128)(2,1)} %broadcast_in_dim.4), calls=%async_computation.2 | async-start | bytes 786432 | tf_op jit(solution)/shard_map/all_to_all | solution.py:281
  90.7 10.7 %shard_map.157 = (bf16[128,1792]{1,0:T(8,128)(2,1)}, bf16[128,1792]{1,0:T(8,128)(2,1)}, bf16[2,128,1792]{2,1,0:T(8,128)(2,1)}, bf16[2,128,1792]{2,1,0:T(8,128)(2,1)}, bf16[2,128,1792]{2,1,0:T(8,128)(2,1)}) custom-call(bf16[512,1280]{1,0:T(8,128)(2,1)} %shard_map.149.d.d0, bf16[512,1280]{1,0:T(8,128)(2,1)} %collective-permute-done.2.d1, ...), custom_call_target="tpu_custom_call" | custom-call | flops 1 | bytes 1 | tf_op jit(solution)/shard_map/pallas_call | solution.py:97
  101.4 1.5 collective-permute-start.13
  103.4 2.7 %all-to-all-done.2 = bf16[8,2,96,128]{3,2,1,0:T(8,128)(2,1)S(1)} async-done(((bf16[8,2,96,128]{3,2,1,0:T(8,128)(2,1)}), bf16[8,2,96,128]{3,2,1,0:T(8,128)(2,1)S(1)}, u32[]{:S(2)}, u32[]{:S(2)}) %all-to-all-start.2) | async-done | bytes 393248 | tf_op jit(solution)/shard_map/all_to_all | solution.py:281
  106.2 1.4 broadcast_in_dim.5
  107.6 6.3 %all-to-all-start.3 = ((bf16[4,16,96,128]{3,2,1,0:T(8,128)(2,1)}), bf16[4,16,96,128]{3,2,1,0:T(8,128)(2,1)}, u32[]{:S(2)}, u32[]{:S(2)}) async-start(bf16[4,16,96,128]{3,2,1,0:T(8,128)(2,1)} %broadcast_in_dim.5), calls=%async_computation.3 | async-start | bytes 3145728 | tf_op jit(solution)/shard_map/all_to_all | solution.py:281
  113.9 1.3 copy-done.6
  115.2 2.2 %shard_map.158 = (bf16[2,64,2304]{2,1,0:T(8,128)(2,1)S(1)}, bf16[2,64,2304]{2,1,0:T(8,128)(2,1)S(1)}) custom-call(bf16[2,128,2304]{2,1,0:T(8,128)(2,1)S(1)} %copy-done.6, bf16[2,128,2304]{2,1,0:T(8,128)(2,1)} %collective-permute-done.15.up, bf16[2,128,2304]{2,1,0:T(8,128)(2,1)} %collective-permute-done.16.down), custom_call_target="tpu_custom_call" | custom-call | flops 1 | bytes 1 | tf_op jit(solution)/shard_map/pallas_call | solution.py:97
  117.4 1.1 collective-permute-start.21
  118.5 1.5 shard_map.159
  119.9 1.6 collective-permute-start.19
  122.0 1.5 collective-permute-start.17
  124.1 6.0 %collective-permute-done.21.got = bf16[2,64,2304]{2,1,0:T(8,128)(2,1)S(1)} collective-permute-done((bf16[2,64,2304]{2,1,0:T(8,128)(2,1)S(1)}, bf16[2,64,2304]{2,1,0:T(8,128)(2,1)S(1)}, u32[]{:S(2)}, u32[]{:S(2)}) %collective-permute-start.21) | collective-permute-done | bytes 589856 | tf_op jit(solution)/shard_map/ppermute | solution.py:40
  130.9 4.0 %collective-permute-done.19.up = bf16[2,128,1024]{2,1,0:T(8,128)(2,1)S(1)} collective-permute-done((bf16[2,128,1024]{2,1,0:T(8,128)(2,1)S(1)}, bf16[2,128,1024]{2,1,0:T(8,128)(2,1)S(1)}, u32[]{:S(2)}, u32[]{:S(2)}) %collective-permute-start.19) | collective-permute-done | bytes 524320 | tf_op jit(solution)/shard_map/ppermute | solution.py:36
  134.9 1.5 collective-permute-done.20.down
  137.6 2.0 %collective-permute-start.25 = (bf16[2,64,768]{2,1,0:T(8,128)(2,1)}, bf16[2,64,768]{2,1,0:T(8,128)(2,1)}, u32[]{:S(2)}, u32[]{:S(2)}) collective-permute-start(bf16[2,64,768]{2,1,0:T(8,128)(2,1)} %get-tuple-element.106), channel_id=1, source_target_pairs={{0,192},{8,200},{16,208},{24,216},{32,224},{40,232},{48,240},{56,2... | collective-permute-start | bytes 589832 | tf_op jit(solution)/shard_map/ppermute | solution.py:22
  141.3 1.4 collective-permute-start.26
  142.7 2.4 %collective-permute-done.23.got = bf16[2,64,1024]{2,1,0:T(8,128)(2,1)S(1)} collective-permute-done((bf16[2,64,1024]{2,1,0:T(8,128)(2,1)S(1)}, bf16[2,64,1024]{2,1,0:T(8,128)(2,1)S(1)}, u32[]{:S(2)}, u32[]{:S(2)}) %collective-permute-start.23) | collective-permute-done | bytes 262176 | tf_op jit(solution)/shard_map/ppermute | solution.py:40
  145.3 3.3 %fusion = f32[64,128]{1,0:T(8,128)} fusion(bf16[128,12288]{1,0:T(8,128)(2,1)S(1)} %copy-done, bf16[8,8,96,128]{3,2,1,0:T(8,128)(2,1)} %bitcast.18), kind=kOutput, calls=%fused_computation | convolution fusion | flops 201326592 | bytes 4751360 | tf_op jit(solution)/shard_map/dot_general | solution.py:113
  150.2 3.5 %collective-permute-start.27 = (bf16[2,64,256]{2,1,0:T(8,128)(2,1)S(1)}, bf16[2,64,256]{2,1,0:T(8,128)(2,1)S(1)}, u32[]{:S(2)}, u32[]{:S(2)}) collective-permute-start(bf16[2,64,256]{2,1,0:T(8,128)(2,1)S(1)} %get-tuple-element.110), channel_id=1, source_target_pairs={{0,64},{8,72},{16,80},{24,88},{32,96},{40,104},{48,112},{56,120},{... | collective-permute-start | bytes 196616 | tf_op jit(solution)/shard_map/ppermute | solution.py:22
  153.7 1.9 %collective-permute-done.27.f1 = bf16[2,64,256]{2,1,0:T(8,128)(2,1)S(1)} collective-permute-done((bf16[2,64,256]{2,1,0:T(8,128)(2,1)S(1)}, bf16[2,64,256]{2,1,0:T(8,128)(2,1)S(1)}, u32[]{:S(2)}, u32[]{:S(2)}) %collective-permute-start.27) | collective-permute-done | bytes 65568 | tf_op jit(solution)/shard_map/ppermute | solution.py:22
  155.6 3.6 %collective-permute-done.28.f3 = bf16[2,64,256]{2,1,0:T(8,128)(2,1)S(1)} collective-permute-done((bf16[2,64,256]{2,1,0:T(8,128)(2,1)S(1)}, bf16[2,64,256]{2,1,0:T(8,128)(2,1)S(1)}, u32[]{:S(2)}, u32[]{:S(2)}) %collective-permute-start.28) | collective-permute-done | bytes 65568 | tf_op jit(solution)/shard_map/ppermute | solution.py:22
  159.8 3.8 %shard_map.165 = bf16[64,8192]{1,0:T(8,128)(2,1)} custom-call(s32[5]{0:T(128)} %stack.23.place, bf16[64,8192]{1,0:T(8,128)(2,1)} %hidden.3, f32[1,8192]{1,0:T(1,128)} %bitcast.32, bf16[2,64,768]{2,1,0:T(8,128)(2,1)} %copy-done.11, bf16[2,64,768]{2,1,0:T(8,128)(2,1)} %collective-permute-done.24.e1, bf16[2,64,768]{2,1,0:T(8,128)(2,1)} %collective-permute-done.25.e3, ...), custom_call_target="tpu_custom_call" | custom-call | flops 1 | bytes 1 | tf_op jit(solution)/shard_map/pallas_call | solution.py:97
  (90 shorter events, 16.7 us)
Async XLA Ops:
  0.6 144.7 %copy-start = (bf16[128,12288]{1,0:T(8,128)(2,1)S(1)}, bf16[128,12288]{1,0:T(8,128)(2,1)}, u32[]{:S(2)}) copy-start(bf16[128,12288]{1,0:T(8,128)(2,1)} %param.27) | copy-start | bytes 9437188
  3.7 4.6 %collective-permute-start = (bf16[64,64]{1,0:T(8,128)(2,1)}, bf16[64,64]{1,0:T(8,128)(2,1)S(1)}, u32[]{:S(2)}, u32[]{:S(2)}) collective-permute-start(bf16[64,64]{1,0:T(8,128)(2,1)} %shard_map.151), channel_id=1, source_target_pairs={{0,1},{1,0},{2,3},{3,2},{4,5},{5,4},{6,7},{7,6},{8,9},{9,8},{10,11... | collective-permute-start | bytes 24584 | tf_op jit(solution)/shard_map/ppermute | solution.py:40
  8.2 12.1 %copy-start.12 = (bf16[1024,64]{0,1:T(8,128)(2,1)S(1)}, bf16[1024,64]{0,1:T(8,128)(2,1)}, u32[]{:S(2)}) copy-start(bf16[1024,64]{0,1:T(8,128)(2,1)} %param.24) | copy-start | bytes 393220
  8.2 12.1 %copy-start.14 = (bf16[128,64]{0,1:T(8,128)(2,1)S(1)}, bf16[128,64]{0,1:T(8,128)(2,1)}, u32[]{:S(2)}) copy-start(bf16[128,64]{0,1:T(8,128)(2,1)} %param.25) | copy-start | bytes 49156
  8.2 12.1 %copy-start.15 = (bf16[128,64]{0,1:T(8,128)(2,1)S(1)}, bf16[128,64]{0,1:T(8,128)(2,1)}, u32[]{:S(2)}) copy-start(bf16[128,64]{0,1:T(8,128)(2,1)} %param.26) | copy-start | bytes 49156
  8.2 12.1 %copy-start.16 = (s32[5]{0:T(128)S(1)}, s32[5]{0:T(128)}, u32[]{:S(2)}) copy-start(s32[5]{0:T(128)} %stack.23.place) | copy-start | bytes 64
  8.3 36.6 %collective-permute-start.4 = (bf16[256,1280]{1,0:T(8,128)(2,1)}, bf16[256,1280]{1,0:T(8,128)(2,1)}, u32[]{:S(2)}, u32[]{:S(2)}) collective-permute-start(bf16[256,1280]{1,0:T(8,128)(2,1)} %shard_map.150.w0), channel_id=1, source_target_pairs={{0,48},{8,56},{16,0},{24,8},{32,16},{40,24},{48,32},{56,40},{64,11... | collective-permute-start | bytes 1966088 | tf_op jit(solution)/shard_map/ppermute | solution.py:26
  13.9 31.7 %collective-permute-start.5 = (bf16[256,1280]{1,0:T(8,128)(2,1)}, bf16[256,1280]{1,0:T(8,128)(2,1)}, u32[]{:S(2)}, u32[]{:S(2)}) collective-permute-start(bf16[256,1280]{1,0:T(8,128)(2,1)} %shard_map.150.w0), channel_id=1, source_target_pairs={{0,16},{8,24},{16,32},{24,40},{32,48},{40,56},{48,0},{56,8},{64,80... | collective-permute-start | bytes 1966088 | tf_op jit(solution)/shard_map/ppermute | solution.py:26
  17.0 31.4 %collective-permute-start.2 = (bf16[512,1280]{1,0:T(8,128)(2,1)}, bf16[512,1280]{1,0:T(8,128)(2,1)}, u32[]{:S(2)}, u32[]{:S(2)}) collective-permute-start(bf16[512,1280]{1,0:T(8,128)(2,1)} %shard_map.149.d.d0), channel_id=1, source_target_pairs={{0,192},{8,200},{16,208},{24,216},{32,224},{40,232},{48,240},{56,2... | collective-permute-start | bytes 3932168 | tf_op jit(solution)/shard_map/ppermute | solution.py:22
  18.0 30.5 %collective-permute-start.3 = (bf16[512,1280]{1,0:T(8,128)(2,1)}, bf16[512,1280]{1,0:T(8,128)(2,1)}, u32[]{:S(2)}, u32[]{:S(2)}) collective-permute-start(bf16[512,1280]{1,0:T(8,128)(2,1)} %shard_map.149.d.d0), channel_id=1, source_target_pairs={{0,64},{8,72},{16,80},{24,88},{32,96},{40,104},{48,112},{56,120},{... | collective-permute-start | bytes 3932168 | tf_op jit(solution)/shard_map/ppermute | solution.py:22
  21.7 6.8 %copy-start.20 = (s32[2]{0:T(128)S(1)}, s32[2]{0:T(128)}, u32[]{:S(2)}) copy-start(s32[2]{0:T(128)} %param.22) | copy-start | bytes 28
  21.7 8.1 %copy-start.17 = (bf16[64,64]{1,0:T(8,128)(2,1)S(1)}, bf16[64,64]{1,0:T(8,128)(2,1)}, u32[]{:S(2)}) copy-start(bf16[64,64]{1,0:T(8,128)(2,1)} %shard_map.151) | copy-start | bytes 24580
  23.6 9.9 %all-to-all-start = ((bf16[4,128,192]{1,2,0:T(8,128)(2,1)}), bf16[4,128,192]{1,2,0:T(8,128)(2,1)}, u32[]{:S(2)}, u32[]{:S(2)}) async-start(bf16[4,128,192]{1,2,0:T(8,128)(2,1)} %copy.16), calls=%async_computation | async-start | bytes 393216 | tf_op jit(solution)/shard_map/all_to_all | solution.py:326
  35.7 9.1 %all-to-all-start.1 = ((bf16[4,96,128]{2,1,0:T(8,128)(2,1)}), bf16[4,96,128]{2,1,0:T(8,128)(2,1)S(1)}, u32[]{:S(2)}, u32[]{:S(2)}) async-start(bf16[4,96,128]{2,1,0:T(8,128)(2,1)} %shard_map.153), calls=%async_computation.1 | async-start | bytes 196608 | tf_op jit(solution)/shard_map/all_to_all | solution.py:329
  40.5 5.7 %collective-permute-start.1 = (bf16[256,1280]{1,0:T(8,128)(2,1)}, bf16[256,1280]{1,0:T(8,128)(2,1)}, u32[]{:S(2)}, u32[]{:S(2)}) collective-permute-start(bf16[256,1280]{1,0:T(8,128)(2,1)} %shard_map.150.w0), channel_id=1, source_target_pairs={{0,8},{8,0},{16,24},{24,16},{32,40},{40,32},{48,56},{56,48},{64,72... | collective-permute-start | bytes 1966088 | tf_op jit(solution)/shard_map/ppermute | solution.py:32
  44.8 16.6 %copy-start.3 = (bf16[256,1280]{1,0:T(8,128)(2,1)S(1)}, bf16[256,1280]{1,0:T(8,128)(2,1)}, u32[]{:S(2)}) copy-start(bf16[256,1280]{1,0:T(8,128)(2,1)} %shard_map.150.w0) | copy-start | bytes 1966084
  45.7 2.8 %collective-permute-start.6 = (bf16[256,1280]{1,0:T(8,128)(2,1)}, bf16[256,1280]{1,0:T(8,128)(2,1)}, u32[]{:S(2)}, u32[]{:S(2)}) collective-permute-start(bf16[256,1280]{1,0:T(8,128)(2,1)} %collective-permute-done.4.w1), channel_id=1, source_target_pairs={{0,8},{8,0},{16,24},{24,16},{32,40},{40,32},{48,56},{56,48},{64,72... | collective-permute-start | bytes 1966088 | tf_op jit(solution)/shard_map/ppermute | solution.py:32
  45.7 3.4 %collective-permute-start.7 = (bf16[256,1280]{1,0:T(8,128)(2,1)}, bf16[256,1280]{1,0:T(8,128)(2,1)}, u32[]{:S(2)}, u32[]{:S(2)}) collective-permute-start(bf16[256,1280]{1,0:T(8,128)(2,1)} %collective-permute-done.5.w3), channel_id=1, source_target_pairs={{0,8},{8,0},{16,24},{24,16},{32,40},{40,32},{48,56},{56,48},{64,72... | collective-permute-start | bytes 1966088 | tf_op jit(solution)/shard_map/ppermute | solution.py:32
  49.0 36.3 %collective-permute-start.8 = (bf16[512,1280]{1,0:T(8,128)(2,1)}, bf16[512,1280]{1,0:T(8,128)(2,1)}, u32[]{:S(2)}, u32[]{:S(2)}) collective-permute-start(bf16[512,1280]{1,0:T(8,128)(2,1)} %shard_map.149.d.d0), channel_id=1, source_target_pairs={{0,128},{8,136},{16,144},{24,152},{32,160},{40,168},{48,176},{56,1... | collective-permute-start | bytes 3932168 | tf_op jit(solution)/shard_map/ppermute | solution.py:22
  50.5 34.9 %collective-permute-start.9 = (bf16[256,1280]{1,0:T(8,128)(2,1)}, bf16[256,1280]{1,0:T(8,128)(2,1)}, u32[]{:S(2)}, u32[]{:S(2)}) collective-permute-start(bf16[256,1280]{1,0:T(8,128)(2,1)} %shard_map.150.w0), channel_id=1, source_target_pairs={{0,32},{8,40},{16,48},{24,56},{32,0},{40,8},{48,16},{56,24},{64,96... | collective-permute-start | bytes 1966088 | tf_op jit(solution)/shard_map/ppermute | solution.py:26
  58.4 14.0 %collective-permute-start.10 = (bf16[128,2304]{1,0:T(8,128)(2,1)}, bf16[128,2304]{1,0:T(8,128)(2,1)S(1)}, u32[]{:S(2)}, u32[]{:S(2)}) collective-permute-start(bf16[128,2304]{1,0:T(8,128)(2,1)} %get-tuple-element.71), channel_id=1, source_target_pairs={{0,2},{1,3},{2,4},{3,5},{4,6},{5,7},{6,0},{7,1},{8,10},{9,11},{10,... | collective-permute-start | bytes 1769480 | tf_op jit(solution)/shard_map/ppermute | solution.py:36
  59.9 12.5 %collective-permute-start.11 = (bf16[128,2304]{1,0:T(8,128)(2,1)}, bf16[128,2304]{1,0:T(8,128)(2,1)S(1)}, u32[]{:S(2)}, u32[]{:S(2)}) collective-permute-start(bf16[128,2304]{1,0:T(8,128)(2,1)} %get-tuple-element.72), channel_id=1, source_target_pairs={{0,6},{1,7},{2,0},{3,1},{4,2},{5,3},{6,4},{7,5},{8,14},{9,15},{10,... | collective-permute-start | bytes 1769480 | tf_op jit(solution)/shard_map/ppermute | solution.py:36
  60.4 25.0 %collective-permute-start.22 = (f32[2,96,128]{2,1,0:T(8,128)S(1)}, f32[2,96,128]{2,1,0:T(8,128)S(1)}, u32[]{:S(2)}, u32[]{:S(2)}) collective-permute-start(f32[2,96,128]{2,1,0:T(8,128)S(1)} %convert_reduce_fusion), channel_id=1, source_target_pairs={{0,1},{1,0},{2,3},{3,2},{4,5},{5,4},{6,7},{7,6},{8,9},{9,8},{10,11... | collective-permute-start | bytes 294920 | tf_op jit(solution)/shard_map/ppermute | solution.py:40
  74.1 39.8 %collective-permute-start.15 = (bf16[2,128,2304]{2,1,0:T(8,128)(2,1)}, bf16[2,128,2304]{2,1,0:T(8,128)(2,1)}, u32[]{:S(2)}, u32[]{:S(2)}) collective-permute-start(bf16[2,128,2304]{2,1,0:T(8,128)(2,1)} %get-tuple-element.75), channel_id=1, source_target_pairs={{0,2},{1,3},{2,4},{3,5},{4,6},{5,7},{6,0},{7,1},{8,10},{9,11},{10,... | collective-permute-start | bytes 3538952 | tf_op jit(solution)/shard_map/ppermute | solution.py:36
  76.1 37.8 %collective-permute-start.16 = (bf16[2,128,2304]{2,1,0:T(8,128)(2,1)}, bf16[2,128,2304]{2,1,0:T(8,128)(2,1)}, u32[]{:S(2)}, u32[]{:S(2)}) collective-permute-start(bf16[2,128,2304]{2,1,0:T(8,128)(2,1)} %get-tuple-element.76), channel_id=1, source_target_pairs={{0,6},{1,7},{2,0},{3,1},{4,2},{5,3},{6,4},{7,5},{8,14},{9,15},{10,... | collective-permute-start | bytes 3538952 | tf_op jit(solution)/shard_map/ppermute | solution.py:36
  85.4 5.3 %collective-permute-start.12 = (bf16[256,1280]{1,0:T(8,128)(2,1)}, bf16[256,1280]{1,0:T(8,128)(2,1)}, u32[]{:S(2)}, u32[]{:S(2)}) collective-permute-start(bf16[256,1280]{1,0:T(8,128)(2,1)} %collective-permute-done.9.w2), channel_id=1, source_target_pairs={{0,8},{8,0},{16,24},{24,16},{32,40},{40,32},{48,56},{56,48},{64,72... | collective-permute-start | bytes 1966088 | tf_op jit(solution)/shard_map/ppermute | solution.py:32
  86.2 19.9 %all-to-all-start.2 = ((bf16[8,2,96,128]{3,2,1,0:T(8,128)(2,1)}), bf16[8,2,96,128]{3,2,1,0:T(8,128)(2,1)S(1)}, u32[]{:S(2)}, u32[]{:S(2)}) async-start(bf16[8,2,96,128]{3,2,1,0:T(8,128)(2,1)} %broadcast_in_dim.4), calls=%async_computation.2 | async-start | bytes 786432 | tf_op jit(solution)/shard_map/all_to_all | solution.py:281
  101.4 17.0 %collective-permute-start.13 = (bf16[128,1792]{1,0:T(8,128)(2,1)}, bf16[128,1792]{1,0:T(8,128)(2,1)}, u32[]{:S(2)}, u32[]{:S(2)}) collective-permute-start(bf16[128,1792]{1,0:T(8,128)(2,1)} %get-tuple-element.80), channel_id=1, source_target_pairs={{0,2},{1,3},{2,4},{3,5},{4,6},{5,7},{6,0},{7,1},{8,10},{9,11},{10,... | collective-permute-start | bytes 1376264 | tf_op jit(solution)/shard_map/ppermute | solution.py:36
  103.0 15.5 %collective-permute-start.14 = (bf16[128,1792]{1,0:T(8,128)(2,1)}, bf16[128,1792]{1,0:T(8,128)(2,1)}, u32[]{:S(2)}, u32[]{:S(2)}) collective-permute-start(bf16[128,1792]{1,0:T(8,128)(2,1)} %get-tuple-element.81), channel_id=1, source_target_pairs={{0,6},{1,7},{2,0},{3,1},{4,2},{5,3},{6,4},{7,5},{8,14},{9,15},{10,... | collective-permute-start | bytes 1376264 | tf_op jit(solution)/shard_map/ppermute | solution.py:36
  107.6 37.7 %all-to-all-start.3 = ((bf16[4,16,96,128]{3,2,1,0:T(8,128)(2,1)}), bf16[4,16,96,128]{3,2,1,0:T(8,128)(2,1)}, u32[]{:S(2)}, u32[]{:S(2)}) async-start(bf16[4,16,96,128]{3,2,1,0:T(8,128)(2,1)} %broadcast_in_dim.5), calls=%async_computation.3 | async-start | bytes 3145728 | tf_op jit(solution)/shard_map/all_to_all | solution.py:281
  115.2 3.3 %copy-start.8 = (bf16[2,128,1792]{2,1,0:T(8,128)(2,1)S(1)}, bf16[2,128,1792]{2,1,0:T(8,128)(2,1)}, u32[]{:S(2)}) copy-start(bf16[2,128,1792]{2,1,0:T(8,128)(2,1)} %get-tuple-element.87.three) | copy-start | bytes 2752516
  117.4 12.8 %collective-permute-start.21 = (bf16[2,64,2304]{2,1,0:T(8,128)(2,1)S(1)}, bf16[2,64,2304]{2,1,0:T(8,128)(2,1)S(1)}, u32[]{:S(2)}, u32[]{:S(2)}) collective-permute-start(bf16[2,64,2304]{2,1,0:T(8,128)(2,1)S(1)} %get-tuple-element.83), channel_id=1, source_target_pairs={{0,1},{1,0},{2,3},{3,2},{4,5},{5,4},{6,7},{7,6},{8,9},{9,8},{10,11... | collective-permute-start | bytes 1769480 | tf_op jit(solution)/shard_map/ppermute | solution.py:40
  118.5 17.9 %copy-start.4 = (bf16[2,128,1792]{2,1,0:T(8,128)(2,1)S(1)}, bf16[2,128,1792]{2,1,0:T(8,128)(2,1)}, u32[]{:S(2)}) copy-start(bf16[2,128,1792]{2,1,0:T(8,128)(2,1)} %get-tuple-element.79.own) | copy-start | bytes 2752516
  119.9 14.9 %collective-permute-start.19 = (bf16[2,128,1024]{2,1,0:T(8,128)(2,1)S(1)}, bf16[2,128,1024]{2,1,0:T(8,128)(2,1)S(1)}, u32[]{:S(2)}, u32[]{:S(2)}) collective-permute-start(bf16[2,128,1024]{2,1,0:T(8,128)(2,1)S(1)} %get-tuple-element.90), channel_id=1, source_target_pairs={{0,2},{1,3},{2,4},{3,5},{4,6},{5,7},{6,0},{7,1},{8,10},{9,11},{10,... | collective-permute-start | bytes 1572872 | tf_op jit(solution)/shard_map/ppermute | solution.py:36
  121.5 14.9 %collective-permute-start.20 = (bf16[2,128,1024]{2,1,0:T(8,128)(2,1)S(1)}, bf16[2,128,1024]{2,1,0:T(8,128)(2,1)S(1)}, u32[]{:S(2)}, u32[]{:S(2)}) collective-permute-start(bf16[2,128,1024]{2,1,0:T(8,128)(2,1)S(1)} %get-tuple-element.91), channel_id=1, source_target_pairs={{0,6},{1,7},{2,0},{3,1},{4,2},{5,3},{6,4},{7,5},{8,14},{9,15},{10,... | collective-permute-start | bytes 1572872 | tf_op jit(solution)/shard_map/ppermute | solution.py:36
  122.0 18.1 %collective-permute-start.17 = (bf16[2,128,768]{2,1,0:T(8,128)(2,1)S(1)}, bf16[2,128,768]{2,1,0:T(8,128)(2,1)S(1)}, u32[]{:S(2)}, u32[]{:S(2)}) collective-permute-start(bf16[2,128,768]{2,1,0:T(8,128)(2,1)S(1)} %get-tuple-element.88), channel_id=1, source_target_pairs={{0,2},{1,3},{2,4},{3,5},{4,6},{5,7},{6,0},{7,1},{8,10},{9,11},{10,... | collective-permute-start | bytes 1179656 | tf_op jit(solution)/shard_map/ppermute | solution.py:36
  123.5 17.1 %collective-permute-start.18 = (bf16[2,128,768]{2,1,0:T(8,128)(2,1)S(1)}, bf16[2,128,768]{2,1,0:T(8,128)(2,1)S(1)}, u32[]{:S(2)}, u32[]{:S(2)}) collective-permute-start(bf16[2,128,768]{2,1,0:T(8,128)(2,1)S(1)} %get-tuple-element.89), channel_id=1, source_target_pairs={{0,6},{1,7},{2,0},{3,1},{4,2},{5,3},{6,4},{7,5},{8,14},{9,15},{10,... | collective-permute-start | bytes 1179656 | tf_op jit(solution)/shard_map/ppermute | solution.py:36
  130.9 10.4 %copy-start.11 = (bf16[2,64,768]{2,1,0:T(8,128)(2,1)}, bf16[2,64,768]{2,1,0:T(8,128)(2,1)S(1)}, u32[]{:S(2)}) copy-start(bf16[2,64,768]{2,1,0:T(8,128)(2,1)S(1)} %get-tuple-element.105.e0) | copy-start | bytes 589828
  136.6 8.6 %collective-permute-start.23 = (bf16[2,64,1024]{2,1,0:T(8,128)(2,1)S(1)}, bf16[2,64,1024]{2,1,0:T(8,128)(2,1)S(1)}, u32[]{:S(2)}, u32[]{:S(2)}) collective-permute-start(bf16[2,64,1024]{2,1,0:T(8,128)(2,1)S(1)} %get-tuple-element.96), channel_id=1, source_target_pairs={{0,1},{1,0},{2,3},{3,2},{4,5},{5,4},{6,7},{7,6},{8,9},{9,8},{10,11... | collective-permute-start | bytes 786440 | tf_op jit(solution)/shard_map/ppermute | solution.py:40
  137.6 16.1 %collective-permute-start.24 = (bf16[2,64,768]{2,1,0:T(8,128)(2,1)}, bf16[2,64,768]{2,1,0:T(8,128)(2,1)}, u32[]{:S(2)}, u32[]{:S(2)}) collective-permute-start(bf16[2,64,768]{2,1,0:T(8,128)(2,1)} %get-tuple-element.93), channel_id=1, source_target_pairs={{0,64},{8,72},{16,80},{24,88},{32,96},{40,104},{48,112},{56,120},{... | collective-permute-start | bytes 589832 | tf_op jit(solution)/shard_map/ppermute | solution.py:22
  137.6 16.1 %collective-permute-start.25 = (bf16[2,64,768]{2,1,0:T(8,128)(2,1)}, bf16[2,64,768]{2,1,0:T(8,128)(2,1)}, u32[]{:S(2)}, u32[]{:S(2)}) collective-permute-start(bf16[2,64,768]{2,1,0:T(8,128)(2,1)} %get-tuple-element.106), channel_id=1, source_target_pairs={{0,192},{8,200},{16,208},{24,216},{32,224},{40,232},{48,240},{56,2... | collective-permute-start | bytes 589832 | tf_op jit(solution)/shard_map/ppermute | solution.py:22
  141.3 3.9 %copy-start.9 = (bf16[2,64,768]{2,1,0:T(8,128)(2,1)}, bf16[2,64,768]{2,1,0:T(8,128)(2,1)S(1)}, u32[]{:S(2)}) copy-start(bf16[2,64,768]{2,1,0:T(8,128)(2,1)S(1)} %get-tuple-element.107.keep) | copy-start | bytes 589828
  141.3 7.3 %collective-permute-start.26 = (bf16[2,64,768]{2,1,0:T(8,128)(2,1)}, bf16[2,64,768]{2,1,0:T(8,128)(2,1)}, u32[]{:S(2)}, u32[]{:S(2)}) collective-permute-start(bf16[2,64,768]{2,1,0:T(8,128)(2,1)} %get-tuple-element.108), channel_id=1, source_target_pairs={{0,1},{1,0},{2,3},{3,2},{4,5},{5,4},{6,7},{7,6},{8,9},{9,8},{10,11... | collective-permute-start | bytes 589832 | tf_op jit(solution)/shard_map/ppermute | solution.py:40
  145.2 14.0 %collective-permute-start.29 = (bf16[2,64,1024]{2,1,0:T(8,128)(2,1)S(1)}, bf16[2,64,1024]{2,1,0:T(8,128)(2,1)}, u32[]{:S(2)}, u32[]{:S(2)}) collective-permute-start(bf16[2,64,1024]{2,1,0:T(8,128)(2,1)S(1)} %shard_map.163), channel_id=1, source_target_pairs={{0,128},{8,136},{16,144},{24,152},{32,160},{40,168},{48,176},{56,1... | collective-permute-start | bytes 786440 | tf_op jit(solution)/shard_map/ppermute | solution.py:22
  145.3 3.3 %copy-start.10 = (bf16[2,64,768]{2,1,0:T(8,128)(2,1)S(1)}, bf16[2,64,768]{2,1,0:T(8,128)(2,1)}, u32[]{:S(2)}) copy-start(bf16[2,64,768]{2,1,0:T(8,128)(2,1)} %copy-done.9) | copy-start | bytes 589828
  150.2 5.4 %collective-permute-start.27 = (bf16[2,64,256]{2,1,0:T(8,128)(2,1)S(1)}, bf16[2,64,256]{2,1,0:T(8,128)(2,1)S(1)}, u32[]{:S(2)}, u32[]{:S(2)}) collective-permute-start(bf16[2,64,256]{2,1,0:T(8,128)(2,1)S(1)} %get-tuple-element.110), channel_id=1, source_target_pairs={{0,64},{8,72},{16,80},{24,88},{32,96},{40,104},{48,112},{56,120},{... | collective-permute-start | bytes 196616 | tf_op jit(solution)/shard_map/ppermute | solution.py:22
  153.7 5.5 %collective-permute-start.28 = (bf16[2,64,256]{2,1,0:T(8,128)(2,1)S(1)}, bf16[2,64,256]{2,1,0:T(8,128)(2,1)S(1)}, u32[]{:S(2)}, u32[]{:S(2)}) collective-permute-start(bf16[2,64,256]{2,1,0:T(8,128)(2,1)S(1)} %get-tuple-element.111), channel_id=1, source_target_pairs={{0,192},{8,200},{16,208},{24,216},{32,224},{40,232},{48,240},{56,2... | collective-permute-start | bytes 196616 | tf_op jit(solution)/shard_map/ppermute | solution.py:22
  155.6 3.6 %copy-start.18 = (bf16[2,64,256]{2,1,0:T(8,128)(2,1)}, bf16[2,64,256]{2,1,0:T(8,128)(2,1)S(1)}, u32[]{:S(2)}) copy-start(bf16[2,64,256]{2,1,0:T(8,128)(2,1)S(1)} %collective-permute-done.27.f1) | copy-start | bytes 196612
  (7 other events, 9.5 us)
